TPU v7x, 128 devices: a whole 4x4x4 slice. The times are simulated.
128 devices in a mesh: seq: 8 (over x, core), exp: 16 (over y, z).
Axes of the slice: x: 4, y: 4, z: 4, core: 2. Of those that a mesh axis runs over, the one named last changes fastest.
Arguments:
- hidden: bfloat16 [16384, 2048], P(('seq', 'exp')), may hold values from -6 to 6
- cotangent: bfloat16 [16384, 2048], P(('seq', 'exp')), may hold values from -6 to 6
- norm_gain: float32 [2048], replicated, may hold values from 0.5 to 1.5
- router: bfloat16 [2048, 128], replicated, may hold values from -0.125 to 0.125
- w_gate: bfloat16 [128, 2048, 768], P(('seq', 'exp')), may hold values from -0.125 to 0.125
- w_up: bfloat16 [128, 2048, 768], P(('seq', 'exp')), may hold values from -0.125 to 0.125
- w_down: bfloat16 [128, 768, 2048], P(('seq', 'exp')), may hold values from -0.21875 to 0.21875
- expert_ids: int32 [16384, 8], P(('seq', 'exp')), may hold values from 0 to 127, all different within a row; in each aligned block of 128 rows (0 to 127, 128 to 255, ...) at most 10 rows name the same one
Outputs:
- d_hidden: bfloat16 [16384, 2048], P(('seq', 'exp'))
- d_gain: float32 [2048], replicated
- d_router: float32 [2048, 128], replicated
- d_wgate: bfloat16 [128, 2048, 768], P(('seq', 'exp'))
- d_wup: bfloat16 [128, 2048, 768], P(('seq', 'exp'))
- d_wdown: bfloat16 [128, 768, 2048], P(('seq', 'exp'))
Inputs may be any that keep to these rules, and one draw needn't show every extreme that they name: `expert_ids`: each row names 8 different experts; among the 128 rows of one device no expert is named by more than 10 rows, a bound that some block reaches.
All inputs are finite; a program needn't handle non-finite values.
Results may differ from a plain program's by a relative error of at most 0.0083.
Values may be sent and summed in bfloat16 or wider, within the bound.
No kernel may reach another device: no remote copies, remote signals or barrier semaphores. Data moves between devices by JAX's collectives and lax.ppermute only.
A program may use at most 192 MiB of HBM per device.

v0:
```python
import jax
import jax.numpy as jnp
from jax import lax
from jax.sharding import PartitionSpec as P

norm_eps = 1e-06


def expert_backward(x_rows, cot_rows, gate_rows, weight_gate, weight_up, weight_down):
    pre_gate = jnp.dot(x_rows, weight_gate, preferred_element_type=jnp.float32)
    pre_up = jnp.dot(x_rows, weight_up, preferred_element_type=jnp.float32)
    sigm = jax.nn.sigmoid(pre_gate)
    act = (pre_gate * sigm * pre_up).astype(jnp.bfloat16)
    output = jnp.dot(act, weight_down, preferred_element_type=jnp.float32)
    gate_grad = jnp.sum(cot_rows.astype(jnp.float32) * output, axis=1).astype(jnp.bfloat16)
    gated = (gate_rows.astype(jnp.float32)[:, None] * cot_rows.astype(jnp.float32)).astype(
        jnp.bfloat16
    )
    d_act = jnp.dot(gated, weight_down.T, preferred_element_type=jnp.float32)
    grad_down = jnp.dot(act.T, gated, preferred_element_type=jnp.float32).astype(jnp.bfloat16)
    grad_pre_gate = (d_act * pre_up * sigm * (1.0 + pre_gate * (1.0 - sigm))).astype(jnp.bfloat16)
    grad_pre_up = (d_act * pre_gate * sigm).astype(jnp.bfloat16)
    grad_gate = jnp.dot(x_rows.T, grad_pre_gate, preferred_element_type=jnp.float32).astype(
        jnp.bfloat16
    )
    grad_up = jnp.dot(x_rows.T, grad_pre_up, preferred_element_type=jnp.float32).astype(
        jnp.bfloat16
    )
    grad_x = (
        jnp.dot(grad_pre_gate, weight_gate.T, preferred_element_type=jnp.float32)
        + jnp.dot(grad_pre_up, weight_up.T, preferred_element_type=jnp.float32)
    ).astype(jnp.bfloat16)
    return (grad_x, gate_grad, grad_gate, grad_up, grad_down)


def on_device(hidden, cotangent, norm_gain, router, w_gate, w_up, w_down, expert_ids):
    token_count, model_width = hidden.shape
    top_count = expert_ids.shape[1]
    expert_count = router.shape[1]
    capacity = max(2, 5 * token_count * top_count // (4 * expert_count))
    slot_rows = token_count * top_count
    assign_count = token_count * top_count
    hidden_f = hidden.astype(jnp.float32)
    scale_r = lax.rsqrt(jnp.mean(hidden_f * hidden_f, axis=-1, keepdims=True) + norm_eps)
    normed = (hidden_f * scale_r * norm_gain).astype(jnp.bfloat16)
    logits = jnp.dot(normed, router, preferred_element_type=jnp.float32)
    picked = jnp.take_along_axis(logits, expert_ids, axis=1)
    weights = jnp.exp(picked)
    gates = weights / jnp.sum(weights, axis=1, keepdims=True)
    flat_ids = expert_ids.reshape(-1)
    one_hot = (flat_ids[:, None] == jnp.arange(expert_count, dtype=jnp.int32)[None, :]).astype(
        jnp.int32
    )
    local_slot = jnp.sum((jnp.cumsum(one_hot, axis=0) - one_hot) * one_hot, axis=1)
    send_index = flat_ids * capacity + local_slot
    table = jnp.full((expert_count * capacity,), assign_count, jnp.int32)
    table = table.at[send_index].set(jnp.arange(assign_count, dtype=jnp.int32))
    normed_pad = jnp.concatenate([normed, jnp.zeros((1, model_width), jnp.bfloat16)], axis=0)
    cot_pad = jnp.concatenate([cotangent, jnp.zeros((1, model_width), jnp.bfloat16)], axis=0)
    gate_pad = jnp.concatenate(
        [gates.reshape(-1).astype(jnp.bfloat16), jnp.zeros((1,), jnp.bfloat16)]
    )
    token_rows = table // top_count
    send_x = normed_pad[token_rows].reshape(expert_count, capacity, model_width)
    send_cot = cot_pad[token_rows].reshape(expert_count, capacity, model_width)
    send_gate = gate_pad[table].reshape(expert_count, capacity)
    send_count = jnp.sum(one_hot, axis=0).astype(jnp.bfloat16).reshape(expert_count, 1)
    recv_x, recv_cot, recv_gate, recv_count = (
        lax.all_to_all(send_x, ("seq", "exp"), split_axis=0, concat_axis=0, tiled=True),
        lax.all_to_all(send_cot, ("seq", "exp"), split_axis=0, concat_axis=0, tiled=True),
        lax.all_to_all(send_gate, ("seq", "exp"), split_axis=0, concat_axis=0, tiled=True),
        lax.all_to_all(send_count, ("seq", "exp"), split_axis=0, concat_axis=0, tiled=True),
    )
    counts = recv_count[:, 0].astype(jnp.int32)
    offsets = jnp.cumsum(counts) - counts
    slot_axis = jnp.arange(capacity, dtype=jnp.int32)[None, :]
    global_slot = offsets[:, None] + slot_axis
    live = (slot_axis < counts[:, None]) & (global_slot < slot_rows)
    place = jnp.where(live, global_slot, slot_rows).reshape(-1)
    x_rows = (
        jnp.zeros((slot_rows + 1, model_width), jnp.bfloat16)
        .at[place]
        .set(recv_x.reshape(-1, model_width))[:slot_rows]
    )
    cot_rows = (
        jnp.zeros((slot_rows + 1, model_width), jnp.bfloat16)
        .at[place]
        .set(recv_cot.reshape(-1, model_width))[:slot_rows]
    )
    gate_rows = (
        jnp.zeros((slot_rows + 1,), jnp.bfloat16).at[place].set(recv_gate.reshape(-1))[:slot_rows]
    )
    grad_x, gate_grad, grad_gate, grad_up, grad_down = expert_backward(
        x_rows, cot_rows, gate_rows, w_gate[0], w_up[0], w_down[0]
    )
    grad_x_pad = jnp.concatenate([grad_x, jnp.zeros((1, model_width), jnp.bfloat16)], axis=0)
    gate_grad_pad = jnp.concatenate([gate_grad, jnp.zeros((1,), jnp.bfloat16)])
    back_x = grad_x_pad[place].reshape(expert_count, capacity, model_width)
    back_gate = gate_grad_pad[place].reshape(expert_count, capacity)
    home_x, home_gate = (
        lax.all_to_all(back_x, ("seq", "exp"), split_axis=0, concat_axis=0, tiled=True),
        lax.all_to_all(back_gate, ("seq", "exp"), split_axis=0, concat_axis=0, tiled=True),
    )
    own_rows = home_x.reshape(-1, model_width)[send_index].reshape(
        token_count, top_count, model_width
    )
    grad_sum = jnp.sum(own_rows.astype(jnp.float32), axis=1)
    dgate = home_gate.reshape(-1)[send_index].reshape(token_count, top_count).astype(jnp.float32)
    dsel = gates * (dgate - jnp.sum(gates * dgate, axis=1, keepdims=True))
    match = expert_ids[:, :, None] == jnp.arange(expert_count, dtype=jnp.int32)[None, None, :]
    dlogits = jnp.sum(jnp.where(match, dsel[:, :, None], 0.0), axis=1).astype(jnp.bfloat16)
    router_part = jnp.dot(normed.T, dlogits, preferred_element_type=jnp.float32)
    dnormed = grad_sum + jnp.dot(dlogits, router.T, preferred_element_type=jnp.float32)
    gain_part = jnp.sum(dnormed * hidden_f * scale_r, axis=0)
    d_router, d_gain = lax.psum((router_part, gain_part), ("seq", "exp"))
    gained = norm_gain * dnormed
    d_hidden = (
        cotangent.astype(jnp.float32)
        + scale_r * gained
        - hidden_f * scale_r**3 * jnp.mean(gained * hidden_f, axis=-1, keepdims=True)
    ).astype(jnp.bfloat16)
    return (d_hidden, d_gain, d_router, grad_gate[None], grad_up[None], grad_down[None])


def solution(mesh):
    in_specs = (
        P(("seq", "exp"), None),
        P(("seq", "exp"), None),
        P(),
        P(),
        P(("seq", "exp"), None, None),
        P(("seq", "exp"), None, None),
        P(("seq", "exp"), None, None),
        P(("seq", "exp"), None),
    )
    out_specs = (
        P(("seq", "exp"), None),
        P(),
        P(),
        P(("seq", "exp"), None, None),
        P(("seq", "exp"), None, None),
        P(("seq", "exp"), None, None),
    )
    return jax.shard_map(
        on_device, mesh=mesh, in_specs=in_specs, out_specs=out_specs, check_vma=False
    )
```

profile of v0, /device:TPU:1, one launch (start us, length us, event | category | flops | bytes accessed | tf_op | source)
XLA Modules:
  0.0 677.2 jit_solution(1102184635798583892)
XLA Ops:
  11.8 11.5 %all-to-all-start = ((bf16[128,1,1]{2,1,0:T(2,128)(2,1)}), bf16[128,1,1]{2,1,0:T(2,128)(2,1)S(1)}, u32[]{:S(2)}, u32[]{:S(2)}) async-start(bf16[128,1,1]{2,1,0:T(2,128)(2,1)} %copy.75), calls=%async_computation | async-start | bytes 131072 | tf_op jit(solution)/shard_map/all_to_all | solution.py:72
  30.5 12.0 %gather_fusion.1 = bf16[1280,2048]{1,0:T(8,128)(2,1)} fusion(bf16[129,2048]{1,0:T(8,128)(2,1)} %concatenate.16, s32[2048]{0:T(1024)S(1)} %get-tuple-element.23), kind=kCustom, calls=%fused_computation.1 | custom fusion | bytes 10490880 | tf_op jit(solution)/shard_map/gather | solution.py:65
  42.4 9.6 %reshape.271 = bf16[128,10,2048]{2,1,0:T(8,128)(2,1)} reshape(bf16[1280,2048]{1,0:T(8,128)(2,1)} %gather_fusion.1) | data formatting | bytes 10485760 | tf_op jit(solution)/shard_map/reshape | solution.py:65
  52.0 10.2 %all-to-all-start.2 = ((bf16[128,10,2048]{2,1,0:T(8,128)(2,1)}), bf16[128,10,2048]{2,1,0:T(8,128)(2,1)}, u32[]{:S(2)}, u32[]{:S(2)}) async-start(bf16[128,10,2048]{2,1,0:T(8,128)(2,1)} %reshape.271), calls=%async_computation.2 | async-start | bytes 16777216 | tf_op jit(solution)/shard_map/all_to_all | solution.py:70
  67.0 12.0 %gather_fusion.2 = bf16[1280,2048]{1,0:T(8,128)(2,1)} fusion(bf16[129,2048]{1,0:T(8,128)(2,1)} %concatenate.17, s32[2048]{0:T(1024)S(1)} %get-tuple-element.23), kind=kCustom, calls=%fused_computation.2 | custom fusion | bytes 10490880 | tf_op jit(solution)/shard_map/gather | solution.py:64
  79.0 9.5 %reshape.273 = bf16[128,10,2048]{2,1,0:T(8,128)(2,1)} reshape(bf16[1280,2048]{1,0:T(8,128)(2,1)} %gather_fusion.2) | data formatting | bytes 10485760 | tf_op jit(solution)/shard_map/reshape | solution.py:64
  88.5 78.9 %all-to-all-done.2 = bf16[128,10,2048]{2,1,0:T(8,128)(2,1)} async-done(((bf16[128,10,2048]{2,1,0:T(8,128)(2,1)}), bf16[128,10,2048]{2,1,0:T(8,128)(2,1)}, u32[]{:S(2)}, u32[]{:S(2)}) %all-to-all-start.2) | async-done | bytes 5242912 | tf_op jit(solution)/shard_map/all_to_all | solution.py:70
  167.4 12.3 %all-to-all-start.3 = ((bf16[128,10,2048]{2,1,0:T(8,128)(2,1)}), bf16[128,10,2048]{2,1,0:T(8,128)(2,1)}, u32[]{:S(2)}, u32[]{:S(2)}) async-start(bf16[128,10,2048]{2,1,0:T(8,128)(2,1)} %reshape.273), calls=%async_computation.3 | async-start | bytes 16777216 | tf_op jit(solution)/shard_map/all_to_all | solution.py:69
  181.5 6.8 %gather_fusion.7 = f32[1024]{0:T(1024)S(1)} fusion(f32[128,128]{1,0:T(8,128)S(1)} %fusion.50, s32[1024]{0:T(1024)S(1)} %reshape.338), kind=kCustom, calls=%fused_computation.7 | custom fusion | bytes 16384 | tf_op jit(solution)/shard_map/jit(take_along_axis)/gather | solution.py:47
  191.7 9.9 %reshape.364 = bf16[1280,2048]{1,0:T(8,128)(2,1)} reshape(bf16[128,10,2048]{2,1,0:T(8,128)(2,1)} %all-to-all-done.2) | data formatting | bytes 10485760 | tf_op jit(solution)/shard_map/reshape | solution.py:88
  201.5 13.8 %scatter_custom_fusion.2 = bf16[1025,2048]{1,0:T(8,128)(2,1)} fusion(s32[1280]{0:T(1024)S(1)} %fusion.44, bf16[1280,2048]{1,0:T(8,128)(2,1)} %reshape.364, bf16[]{:T(256)} %constant.24.clone.1), kind=kCustom, calls=%fused_computation.45 | custom fusion | bytes 4198912 | tf_op jit(solution)/shard_map/scatter | solution.py:88
  215.3 70.1 %all-to-all-done.3 = bf16[128,10,2048]{2,1,0:T(8,128)(2,1)} async-done(((bf16[128,10,2048]{2,1,0:T(8,128)(2,1)}), bf16[128,10,2048]{2,1,0:T(8,128)(2,1)}, u32[]{:S(2)}, u32[]{:S(2)}) %all-to-all-start.3) | async-done | bytes 5242912 | tf_op jit(solution)/shard_map/all_to_all | solution.py:69
  285.4 9.9 %reshape.372 = bf16[1280,2048]{1,0:T(8,128)(2,1)} reshape(bf16[128,10,2048]{2,1,0:T(8,128)(2,1)} %all-to-all-done.3) | data formatting | bytes 10485760 | tf_op jit(solution)/shard_map/reshape | solution.py:83
  295.3 13.4 %scatter_custom_fusion.3 = bf16[1025,2048]{1,0:T(8,128)(2,1)} fusion(s32[1280]{0:T(1024)S(1)} %fusion.44, bf16[1280,2048]{1,0:T(8,128)(2,1)} %reshape.372, bf16[]{:T(256)} %constant.24.clone.1), kind=kCustom, calls=%fused_computation.43 | custom fusion | bytes 4198912 | tf_op jit(solution)/shard_map/scatter | solution.py:83
  308.7 6.3 fusion.4
  324.2 8.0 %gather_fusion.5 = bf16[1280]{0:T(1024)(128)(2,1)S(1)} fusion(bf16[1025]{0:T(1024)(128)(2,1)S(1)} %pad_maximum_fusion, s32[2048]{0:T(1024)S(1)} %pad_clamp_fusion), kind=kCustom, calls=%fused_computation.5 | custom fusion | bytes 10240 | tf_op jit(solution)/shard_map/gather | solution.py:99
  332.9 8.8 %all-to-all-start.5 = ((bf16[128,1,10]{2,1,0:T(2,128)(2,1)}), bf16[128,1,10]{2,1,0:T(2,128)(2,1)S(1)}, u32[]{:S(2)}, u32[]{:S(2)}) async-start(bf16[128,1,10]{2,1,0:T(2,128)(2,1)} %all_to_all.34), calls=%async_computation.5 | async-start | bytes 131072 | tf_op jit(solution)/shard_map/all_to_all | solution.py:102
  341.8 9.5 %all-to-all-done.5 = bf16[128,1,10]{2,1,0:T(2,128)(2,1)S(1)} async-done(((bf16[128,1,10]{2,1,0:T(2,128)(2,1)}), bf16[128,1,10]{2,1,0:T(2,128)(2,1)S(1)}, u32[]{:S(2)}, u32[]{:S(2)}) %all-to-all-start.5) | async-done | bytes 2592 | tf_op jit(solution)/shard_map/all_to_all | solution.py:102
  351.6 6.8 %gather_fusion.6 = bf16[1024]{0:T(1024)(128)(2,1)S(1)} fusion(bf16[1280]{0:T(1024)(128)(2,1)S(1)} %reshape.277, s32[1024]{0:T(1024)S(1)} %broadcast_clamp_fusion), kind=kCustom, calls=%fused_computation.6 | custom fusion | bytes 8192 | tf_op jit(solution)/shard_map/gather | solution.py:108
  358.8 8.0 %gather_fusion = bf16[1280]{0:T(1024)(128)(2,1)S(1)} fusion(bf16[1025]{0:T(1024)(128)(2,1)S(1)} %pad_maximum_fusion.1, s32[2048]{0:T(1024)S(1)} %get-tuple-element.24), kind=kCustom, calls=%fused_computation | custom fusion | bytes 10240 | tf_op jit(solution)/shard_map/gather | solution.py:66
  367.0 13.9 %all_to_all.41 = bf16[128,1,10]{2,1,0:T(2,128)(2,1)S(1)} all-to-all(bf16[128,1,10]{2,1,0:T(2,128)(2,1)S(1)} %all_to_all.33), channel_id=1, replica_groups=mesh['seq'=8,'exp'=16] {'seq','exp'}, dimensions={0} | all-to-all | bytes 5120 | tf_op jit(solution)/shard_map/all_to_all | solution.py:71
  381.2 12.9 %scatter_custom_fusion.1 = bf16[1025]{0:T(1024)(128)(2,1)S(1)} fusion(s32[1280]{0:T(1024)S(1)} %fusion.44, bf16[1280]{0:T(1024)(128)(2,1)S(1)} %reshape.356, bf16[]{:T(256)} %constant.24.clone.1), kind=kCustom, calls=%fused_computation.108 | custom fusion | bytes 2052 | tf_op jit(solution)/shard_map/scatter | solution.py:91
  394.1 9.2 %multiply_convert_fusion.1 = (bf16[1024,768]{1,0:T(8,128)(2,1)S(1)}, bf16[1024,768]{1,0:T(8,128)(2,1)S(1)}) fusion(f32[1024,768]{1,0:T(8,128)} %copy-done.20, f32[1024,768]{1,0:T(8,128)} %get-tuple-element.21, bf16[1,768,2048]{2,1,0:T(8,128)(2,1)} %param.14, f32[1024]{0:T(1024)S(1)} %slice_convert_fusion, bf16[1025,2048]{1,0:T(8,128)(2,1)} %scatter_custom_fusion.2), kind=kOutput, calls=%fused_computation.32 | convolution fusion | flops 3237740544 | bytes 16781312 | tf_op jit(solution)/shard_map/dot_general | solution.py:19
  413.0 13.6 %gather_fusion.3 = bf16[1280,2048]{1,0:T(8,128)(2,1)} fusion(bf16[1025,2048]{1,0:T(8,128)(2,1)} %concatenate.18, s32[2048]{0:T(1024)S(1)} %pad_clamp_fusion), kind=kCustom, calls=%fused_computation.3 | custom fusion | bytes 10490880 | tf_op jit(solution)/shard_map/gather | solution.py:98
  426.6 9.5 %reshape.275 = bf16[128,10,2048]{2,1,0:T(8,128)(2,1)} reshape(bf16[1280,2048]{1,0:T(8,128)(2,1)} %gather_fusion.3) | data formatting | bytes 10485760 | tf_op jit(solution)/shard_map/reshape | solution.py:98
  436.1 5.8 all-to-all-start.4
  444.9 8.0 %fusion.13 = bf16[1,2048,768]{2,1,0:T(8,128)(2,1)} fusion(bf16[1024,768]{1,0:T(8,128)(2,1)} %copy-done.21, bf16[1025,2048]{1,0:T(8,128)(2,1)} %scatter_custom_fusion.3), kind=kOutput, calls=%fused_computation.36 | convolution fusion | flops 3222798336 | bytes 8912896 | tf_op jit(solution)/shard_map/dot_general | solution.py:26
  463.3 86.5 %all-to-all-done.4 = bf16[128,10,2048]{2,1,0:T(8,128)(2,1)} async-done(((bf16[128,10,2048]{2,1,0:T(8,128)(2,1)}), bf16[128,10,2048]{2,1,0:T(8,128)(2,1)}, u32[]{:S(2)}, u32[]{:S(2)}) %all-to-all-start.4) | async-done | bytes 5242912 | tf_op jit(solution)/shard_map/all_to_all | solution.py:101
  549.8 9.8 %reshape.276 = bf16[1280,2048]{1,0:T(8,128)(2,1)} reshape(bf16[128,10,2048]{2,1,0:T(8,128)(2,1)} %all-to-all-done.4) | data formatting | bytes 10485760 | tf_op jit(solution)/shard_map/reshape | solution.py:104
  559.6 12.0 %gather_fusion.4 = bf16[1024,2048]{1,0:T(8,128)(2,1)} fusion(bf16[1280,2048]{1,0:T(8,128)(2,1)} %reshape.276, s32[1024]{0:T(1024)S(1)} %broadcast_clamp_fusion), kind=kCustom, calls=%fused_computation.4 | custom fusion | bytes 8392704 | tf_op jit(solution)/shard_map/gather | solution.py:104
  578.3 66.0 %psum.14 = f32[2048]{0:T(1024)} all-reduce(f32[2048]{0:T(1024)S(1)} %get-tuple-element.6), channel_id=1, replica_groups=mesh['seq'=8,'exp'=16] {'seq','exp'}, use_global_device_ids=true, to_apply=%region_17.18 | all-reduce | flops 2048 | bytes 16384 | tf_op jit(solution)/shard_map/psum | solution.py:115
  647.1 20.5 %all-reduce.5.cloned.1.call-done = f32[2048,128]{1,0:T(8,128)} async-done(((f32[2048,128]{1,0:T(8,128)}), f32[2048,128]{1,0:T(8,128)}) %all-reduce.5.cloned.1.call-update) | async-done | bytes 1048592 | tf_op jit(solution)/shard_map/psum | solution.py:115
  (137 shorter events, 67.2 us)
Async XLA Ops:
  7.2 307.8 %copy-start = (bf16[1,2048,768]{2,1,0:T(8,128)(2,1)S(1)}, bf16[1,2048,768]{2,1,0:T(8,128)(2,1)}, u32[]{:S(2)}) copy-start(bf16[1,2048,768]{2,1,0:T(8,128)(2,1)} %param.13) | copy-start | bytes 9437188
  8.1 34.3 %copy-start.6 = (s32[128,8]{1,0:T(8,128)}, s32[128,8]{1,0:T(8,128)S(1)}, u32[]{:S(2)}) copy-start(s32[128,8]{1,0:T(8,128)S(1)} %copy.74) | copy-start | bytes 12292
  11.8 40.2 %all-to-all-start = ((bf16[128,1,1]{2,1,0:T(2,128)(2,1)}), bf16[128,1,1]{2,1,0:T(2,128)(2,1)S(1)}, u32[]{:S(2)}, u32[]{:S(2)}) async-start(bf16[128,1,1]{2,1,0:T(2,128)(2,1)} %copy.75), calls=%async_computation | async-start | bytes 131072 | tf_op jit(solution)/shard_map/all_to_all | solution.py:72
  52.0 12.1 %copy-start.9 = (f32[2048]{0:T(1024)S(1)}, f32[2048]{0:T(1024)}, u32[]{:S(2)}) copy-start(f32[2048]{0:T(1024)} %param.10) | copy-start | bytes 24580
  52.0 115.4 %all-to-all-start.2 = ((bf16[128,10,2048]{2,1,0:T(8,128)(2,1)}), bf16[128,10,2048]{2,1,0:T(8,128)(2,1)}, u32[]{:S(2)}, u32[]{:S(2)}) async-start(bf16[128,10,2048]{2,1,0:T(8,128)(2,1)} %reshape.271), calls=%async_computation.2 | async-start | bytes 16777216 | tf_op jit(solution)/shard_map/all_to_all | solution.py:70
  64.1 14.9 %copy-start.11 = (f32[128]{0:T(128)}, f32[128]{0:T(128)S(1)}, u32[]{:S(2)}) copy-start(f32[128]{0:T(128)S(1)} %get-tuple-element.19) | copy-start | bytes 1540
  88.5 91.3 %copy-start.8 = (s32[128,8]{0,1:T(8,128)S(1)}, s32[128,8]{0,1:T(8,128)}, u32[]{:S(2)}) copy-start(s32[128,8]{0,1:T(8,128)} %param.15) | copy-start | bytes 12292
  167.4 118.0 %all-to-all-start.3 = ((bf16[128,10,2048]{2,1,0:T(8,128)(2,1)}), bf16[128,10,2048]{2,1,0:T(8,128)(2,1)}, u32[]{:S(2)}, u32[]{:S(2)}) async-start(bf16[128,10,2048]{2,1,0:T(8,128)(2,1)} %reshape.273), calls=%async_computation.3 | async-start | bytes 16777216 | tf_op jit(solution)/shard_map/all_to_all | solution.py:69
  308.7 6.3 copy-start.3
  308.7 11.6 %slice-start = ((s8[4227072]{0:T(1024)(128)(4,1)}), s8[4194304]{0:T(1024)(128)(4,1)S(1)}, s32[]{:S(2)}) async-start(s8[4227072]{0:T(1024)(128)(4,1)} %bitcast.59), calls=%async_computation.7 | async-start | bytes 8388608
  315.0 5.3 copy-start.20
  315.0 5.3 slice-start.1
  315.0 5.3 copy-start.14
  320.3 3.8 copy-start.16
  332.9 18.3 %all-to-all-start.5 = ((bf16[128,1,10]{2,1,0:T(2,128)(2,1)}), bf16[128,1,10]{2,1,0:T(2,128)(2,1)S(1)}, u32[]{:S(2)}, u32[]{:S(2)}) async-start(bf16[128,1,10]{2,1,0:T(2,128)(2,1)} %all_to_all.34), calls=%async_computation.5 | async-start | bytes 131072 | tf_op jit(solution)/shard_map/all_to_all | solution.py:102
  394.1 9.3 %copy-start.15 = (bf16[1,2048,768]{2,1,0:T(8,128)(2,1)S(1)}, bf16[1,2048,768]{2,1,0:T(8,128)(2,1)}, u32[]{:S(2)}) copy-start(bf16[1,2048,768]{2,1,0:T(8,128)(2,1)} %param.12) | copy-start | bytes 9437188
  403.3 3.5 copy-start.18
  403.3 3.5 copy-start.21
  436.1 5.9 copy-start.7
  436.1 16.7 %slice-start.4 = ((s8[4227072]{0:T(1024)(128)(4,1)}), s8[32768]{0:T(1024)(128)(4,1)S(1)}, s32[]{:S(2)}) async-start(s8[4227072]{0:T(1024)(128)(4,1)} %bitcast.63), calls=%async_computation.11 | async-start | bytes 65536
  436.1 113.6 %all-to-all-start.4 = ((bf16[128,10,2048]{2,1,0:T(8,128)(2,1)}), bf16[128,10,2048]{2,1,0:T(8,128)(2,1)}, u32[]{:S(2)}, u32[]{:S(2)}) async-start(bf16[128,10,2048]{2,1,0:T(8,128)(2,1)} %reshape.275), calls=%async_computation.4 | async-start | bytes 16777216 | tf_op jit(solution)/shard_map/all_to_all | solution.py:101
  441.9 225.7 %all-reduce.5.cloned.1.call-start = ((), (), s32[]{:S(2)}) async-start(), calls=%async_computation.6 | async-start | bytes 2097152 | tf_op jit(solution)/shard_map/psum | solution.py:115
  444.8 8.1 %slice-start.5 = ((s8[4227072]{0:T(1024)(128)(4,1)}), s8[4194304]{0:T(1024)(128)(4,1)S(1)}, s32[]{:S(2)}) async-start(s8[4227072]{0:T(1024)(128)(4,1)} %bitcast.63), calls=%async_computation.12 | async-start | bytes 8388608
  444.8 8.0 %copy-start.19 = (bf16[1024,768]{1,0:T(8,128)(2,1)S(1)}, bf16[1024,768]{1,0:T(8,128)(2,1)}, u32[]{:S(2)}) copy-start(bf16[1024,768]{1,0:T(8,128)(2,1)} %copy-done.18) | copy-start | bytes 4718596
  444.8 13.3 %slice-start.2 = ((s8[4227072]{0:T(1024)(128)(4,1)}), s8[4194304]{0:T(1024)(128)(4,1)S(1)}, s32[]{:S(2)}) async-start(s8[4227072]{0:T(1024)(128)(4,1)} %bitcast.61), calls=%async_computation.9 | async-start | bytes 8388608
  452.9 5.2 slice-start.3
  452.9 5.2 copy-start.17
  571.7 5.2 copy-start.2
  571.7 5.2 copy-start.5
  571.7 5.2 copy-start.10
  571.7 5.2 copy-start.12
  571.7 72.7 %copy-start.13 = (f32[128]{0:T(128)S(1)}, f32[128]{0:T(128)}, u32[]{:S(2)}) copy-start(f32[128]{0:T(128)} %get-tuple-element.18) | copy-start | bytes 1540
  (2 other events, 1.6 us)
Sparse Core Ops, SparseCore 0:
  447.5 220.0 all-reduce.4
where the time goes:
time: 686 us; the launch traced here: 677 us
  waiting for transfers between devices  266 us (39%)
  local copies, waits for them, and re-layouts  196 us (29%)
  blocking collectives  79.9 us (12%)
  matrix products  55.3 us (8%)
  starting transfers between devices  48.6 us (7%)
  other arithmetic  17.1 us (2%)
  between operations  15.1 us (2%)
    all_to_all x1, waiting for transfers between devices, on_device(): lax.all_to_all(back_x, ('seq', 'exp'), split_axis=0, concat_axis=0, tiled...  86.5 us
    all_to_all x1, waiting for transfers between devices, on_device(): lax.all_to_all(send_cot, ('seq', 'exp'), split_axis=0, concat_axis=0, til...  78.9 us
    all_to_all x1, waiting for transfers between devices, on_device(): lax.all_to_all(send_x, ('seq', 'exp'), split_axis=0, concat_axis=0, tiled...  70.1 us
    psum x1, blocking collectives, on_device(): d_router, d_gain = lax.psum((router_part, gain_part), ('seq', 'exp'))  66 us
    psum x1, waiting for transfers between devices, on_device(): d_router, d_gain = lax.psum((router_part, gain_part), ('seq', 'exp'))  20.5 us
    all_to_all x1, blocking collectives, on_device(): lax.all_to_all(send_gate, ('seq', 'exp'), split_axis=0, concat_axis=0, ti...  13.9 us
    scatter x1, local copies, waits for them, and re-layouts, on_device(): cot_rows = jnp.zeros((slot_rows + 1, model_width), jnp.bfloat16).at[place...  13.8 us
  transfers between devices with their start and end apart: 6, of which 5 were waited for; matrix products, arithmetic and copies ran while one was open for 21% of the time, Pallas kernels for 0%

commit v1 on v0

v1 whole, which is shorter than its diff:
```python
import functools

import jax
import jax.numpy as jnp
from jax import lax
from jax.experimental import pallas as pl
from jax.experimental.pallas import tpu as pltpu
from jax.sharding import PartitionSpec as P

norm_eps = 1e-06
HI = 8
SUB = 8
MSG = 128
AXES = ("seq", "exp")
bf16, f32 = jnp.bfloat16, jnp.float32
VMEM_LIMIT = 56 * 1024 * 1024


def params(**kw):
    return pltpu.CompilerParams(vmem_limit_bytes=VMEM_LIMIT, **kw)


def whole(shape):
    return pl.BlockSpec(shape, lambda *_: (0,) * len(shape))


def iota(shape, dim):
    return lax.broadcasted_iota(jnp.int32, shape, dim)


def mm(a, b):
    return jnp.dot(a, b, preferred_element_type=f32)


def mm_nt(a, b):
    return lax.dot_general(a, b, (((1,), (1,)), ((), ())), preferred_element_type=f32)


def mm_tn(a, b):
    return lax.dot_general(a, b, (((0,), (0,)), ((), ())), preferred_element_type=f32)


def exchange(x):
    return lax.all_to_all(x, AXES, split_axis=0, concat_axis=0, tiled=True)


def front_kernel(hid_ref, cot_ref, gain_ref, ids_ref, s1_ref, normed_ref, slot_ref, slot_t_ref, nc, p8):
    step = pl.program_id(0)
    tokens, width = hid_ref.shape
    experts = slot_ref.shape[1]
    tile = nc.shape[2]

    @pl.when(step == 0)
    def _():
        h = hid_ref[...].astype(f32)
        scale = lax.rsqrt(jnp.mean(h * h, axis=1, keepdims=True) + norm_eps)
        normed = (h * scale * gain_ref[...]).astype(bf16)
        normed_ref[...] = normed
        for j in range(width // tile):
            nc[j] = normed[:, j * tile : (j + 1) * tile]
            nc[width // tile + j] = cot_ref[:, j * tile : (j + 1) * tile]
        ids = ids_ref[...]
        lane = iota((tokens, experts), 1)
        member = jnp.zeros((tokens, experts), f32)
        for k in range(ids.shape[1]):
            member += jnp.where(ids[:, k : k + 1] == lane, 1.0, 0.0)
        lower = jnp.where(iota((tokens, tokens), 1) < iota((tokens, tokens), 0), 1.0, 0.0)
        position = mm(lower.astype(bf16), member.astype(bf16))
        slot = jnp.where(member > 0.0, position, 99.0)
        slot_ref[...] = slot
        slot_t = slot.T
        slot_t_ref[...] = slot_t
        which = iota((experts, HI, tokens), 1).astype(f32)
        chosen = jnp.where(slot_t[:, None, :] == which, 1.0, 0.0)
        p8[...] = chosen.reshape(experts * HI, tokens).astype(bf16)

    s1_ref[...] = mm(p8[...], nc[step]).astype(bf16)


def front(hidden, cotangent, gain, ids, experts):
    tokens, width = hidden.shape
    tile = min(512, width)
    steps = 2 * width // tile
    return pl.pallas_call(
        front_kernel,
        grid=(steps,),
        in_specs=[whole((tokens, width)), whole((tokens, width)), whole((1, width)), whole(ids.shape)],
        out_specs=[
            pl.BlockSpec((experts * HI, tile), lambda i: (0, i)),
            whole((tokens, width)),
            whole((tokens, experts)),
            whole((experts, tokens)),
        ],
        out_shape=[
            jax.ShapeDtypeStruct((experts * HI, 2 * width), bf16),
            jax.ShapeDtypeStruct((tokens, width), bf16),
            jax.ShapeDtypeStruct((tokens, experts), f32),
            jax.ShapeDtypeStruct((experts, tokens), f32),
        ],
        scratch_shapes=[pltpu.VMEM((steps, tokens, tile), bf16), pltpu.VMEM((experts * HI, tokens), bf16)],
        compiler_params=params(),
        cost_estimate=pl.CostEstimate(flops=4 * experts * HI * tokens * width, bytes_accessed=10_000_000, transcendentals=tokens),
    )(hidden, cotangent, gain, ids)


def second_kernel(normed_ref, cot_ref, slot_ref, slot_t_ref, router_ref, gates_ref, s2_ref):
    tokens, width = normed_ref.shape
    experts = slot_ref.shape[1]
    half = width // 2
    logits = mm(normed_ref[...], router_ref[...])
    weights = jnp.where(slot_ref[...] < 50.0, jnp.exp(logits), 0.0)
    gates = weights / jnp.sum(weights, axis=1, keepdims=True)
    gates_ref[...] = gates
    slot_t = slot_t_ref[...]
    gates_t = gates.T
    lane = iota((experts, MSG), 1)
    message = jnp.where(lane == 10, jnp.sum(jnp.where(slot_t < 50.0, 1.0, 0.0), axis=1, keepdims=True), 0.0)
    for s in range(10):
        message = message + jnp.where(
            lane == s, jnp.sum(jnp.where(slot_t == s, gates_t, 0.0), axis=1, keepdims=True), 0.0
        )
    sub = iota((experts, SUB, MSG), 1)
    spread = jnp.where(sub == 0, message[:, None, :], 0.0).reshape(experts * SUB, MSG)
    s2_ref[:, half:] = spread.astype(bf16)
    row = iota((experts, SUB, tokens), 1)
    chosen = jnp.where(slot_t[:, None, :] == (HI + row // 4).astype(f32), 1.0, 0.0)
    total = None
    for j in range(4):
        pick = jnp.where(row % 4 == j, chosen, 0.0).reshape(experts * SUB, tokens).astype(bf16)
        source = normed_ref if j < 2 else cot_ref
        term = mm(pick, source[:, (j % 2) * half : (j % 2 + 1) * half])
        total = term if total is None else total + term
    s2_ref[:, :half] = total.astype(bf16)


def second(normed, cotangent, slot, slot_t, router):
    tokens, width = normed.shape
    experts = slot.shape[1]
    return pl.pallas_call(
        second_kernel,
        out_shape=[
            jax.ShapeDtypeStruct((tokens, experts), f32),
            jax.ShapeDtypeStruct((experts * SUB, width // 2 + MSG), bf16),
        ],
        compiler_params=params(),
        cost_estimate=pl.CostEstimate(flops=4 * experts * SUB * tokens * width, bytes_accessed=4_000_000, transcendentals=tokens * experts),
    )(normed, cotangent, slot, slot_t, router)


def expert_rows(x, c, wg_ref, wu_ref, wd_ref):
    a = mm(x, wg_ref[...])
    b = mm(x, wu_ref[...])
    u = mm_nt(c, wd_ref[...])
    s = jax.nn.sigmoid(a)
    act = (a * s * b).astype(bf16)
    q = jnp.sum(act.astype(f32) * u, axis=1, keepdims=True)
    da = (u * b * s * (1.0 + a * (1.0 - s))).astype(bf16)
    db = (u * a * s).astype(bf16)
    return act, q, da, db


def rows_kernel(x_ref, c_ref, wg_ref, wu_ref, wd_ref, act_ref, da_ref, db_ref, q_ref, dx_ref):
    act, q, da, db = expert_rows(x_ref[...], c_ref[...], wg_ref, wu_ref, wd_ref)
    act_ref[...] = act
    da_ref[...] = da
    db_ref[...] = db
    sources = q_ref.shape[0]
    lane, which = iota((sources, HI, MSG), 2), iota((sources, HI, MSG), 1)
    q_ref[...] = jnp.sum(jnp.where(lane == which, q.reshape(sources, HI, 1), 0.0), axis=1)
    dx_ref[...] = (mm_nt(da, wg_ref[...]) + mm_nt(db, wu_ref[...])).astype(bf16)


def rows(r1, wg, wu, wd):
    total, both = r1.shape
    width, hid = wg.shape
    block = min(256, total)
    one = pl.BlockSpec((block, hid), lambda i: (i, 0))
    return pl.pallas_call(
        rows_kernel,
        grid=(total // block,),
        in_specs=[
            pl.BlockSpec((block, width), lambda i: (i, 0)),
            pl.BlockSpec((block, width), lambda i: (i, 1)),
            whole(wg.shape),
            whole(wu.shape),
            whole(wd.shape),
        ],
        out_specs=[one, one, one, pl.BlockSpec((block // HI, MSG), lambda i: (i, 0)), pl.BlockSpec((block, width), lambda i: (i, 0))],
        out_shape=[jax.ShapeDtypeStruct((total, hid), bf16)] * 3
        + [
            jax.ShapeDtypeStruct((total // HI, MSG), f32),
            jax.ShapeDtypeStruct((total, width + width // 2), bf16),
        ],
        compiler_params=params(),
        cost_estimate=pl.CostEstimate(flops=10 * total * width * hid, bytes_accessed=30_000_000, transcendentals=total * hid),
    )(r1, r1, wg, wu, wd)


def tail_kernel(limit, r2_ref, q8_ref, wg_ref, wu_ref, wd_ref, xc_ref, act_ref, da_ref, db_ref, msg_ref, scale_ref):
    sources = q8_ref.shape[0]
    width, hid = wg_ref.shape
    half = width // 2
    chunk = min(32, sources)
    out_rows, in_rows = 2 * chunk, SUB * chunk
    index, column = iota((4 * out_rows, in_rows), 0), iota((4 * out_rows, in_rows), 1)
    pick = jnp.where(column == 4 * (index % out_rows) + index // out_rows, 1.0, 0.0).astype(bf16)
    for j in range(sources // chunk):
        part = mm(pick, r2_ref[j * in_rows : (j + 1) * in_rows, :half]).astype(bf16)
        for quarter in range(4):
            xc_ref[j * out_rows : (j + 1) * out_rows, quarter * half : (quarter + 1) * half] = part[
                quarter * out_rows : (quarter + 1) * out_rows
            ]
    act, q, da, db = expert_rows(xc_ref[:, :width], xc_ref[:, width:], wg_ref, wu_ref, wd_ref)
    act_ref[...] = act
    da_ref[...] = da
    db_ref[...] = db
    total = 2 * sources
    parity = iota((total, MSG), 0) % 2
    spread = jnp.where(iota((total, MSG), 1) == HI + parity, q, 0.0).astype(bf16)
    gather = jnp.where(iota((sources, total), 1) // 2 == iota((sources, total), 0), 1.0, 0.0).astype(bf16)
    q_all = q8_ref[...].astype(bf16).astype(f32) + mm(gather, spread)
    meta = jnp.sum(r2_ref[:, half:].astype(f32).reshape(sources, SUB, MSG), axis=1)
    lane = iota((sources, MSG), 1)
    count = jnp.sum(jnp.where(lane == 10, meta, 0.0), axis=1, keepdims=True)
    lower = jnp.where(iota((sources, sources), 1) < iota((sources, sources), 0), 1.0, 0.0).astype(bf16)
    offset = mm(lower, jnp.broadcast_to(count, (sources, MSG)).astype(bf16))
    slot = jnp.where(lane < 10, lane, lane - 10).astype(f32)
    kept = (slot < count) & (offset + slot < limit) & (lane < 20)
    msg_ref[...] = jnp.where(kept, jnp.where(lane < 10, q_all, 1.0), 0.0)
    scale_ref[...] = jnp.where(kept & (lane < 10), meta, 0.0).astype(bf16)


def tail(r2, q8, wg, wu, wd, limit):
    sources = q8.shape[0]
    width, hid = wg.shape
    return pl.pallas_call(
        functools.partial(tail_kernel, float(limit)),
        out_shape=[jax.ShapeDtypeStruct((2 * sources, 2 * width), bf16)]
        + [jax.ShapeDtypeStruct((2 * sources, hid), bf16)] * 3
        + [jax.ShapeDtypeStruct((sources, MSG), f32), jax.ShapeDtypeStruct((sources, MSG), bf16)],
        compiler_params=params(),
        cost_estimate=pl.CostEstimate(flops=12 * sources * width * hid, bytes_accessed=16_000_000, transcendentals=2 * sources * hid),
    )(r2, q8, wg, wu, wd)


def tail_dx_kernel(da_ref, db_ref, wg_ref, wu_ref, dx_ref):
    dx_ref[...] = (mm_nt(da_ref[...], wg_ref[...]) + mm_nt(db_ref[...], wu_ref[...])).astype(bf16)


def tail_dx(da, db, wg, wu):
    return pl.pallas_call(
        tail_dx_kernel,
        out_shape=jax.ShapeDtypeStruct((da.shape[0], wg.shape[0]), bf16),
        compiler_params=params(),
        cost_estimate=pl.CostEstimate(flops=4 * da.shape[0] * wg.size, bytes_accessed=8_000_000, transcendentals=0),
    )(da, db, wg, wu)


def column_of(table):
    sources = table.shape[0]
    lane, which = iota((sources, HI, MSG), 2), iota((sources, HI, MSG), 1)
    spread = jnp.where(lane == which, table[:, None, :], 0.0)
    return jnp.sum(spread.reshape(sources * HI, MSG), axis=1, keepdims=True)


def tail_column_of(table):
    sources = table.shape[0]
    total = 2 * sources
    scatter = jnp.where(iota((total, sources), 0) // 2 == iota((total, sources), 1), 1.0, 0.0).astype(bf16)
    lane = HI + iota((total, MSG), 0) % 2
    return jnp.sum(jnp.where(iota((total, MSG), 1) == lane, mm(scatter, table), 0.0), axis=1, keepdims=True)


def weights_kernel(x_ref, c_ref, x2_ref, c2_ref, act_ref, da_ref, db_ref, act2_ref, da2_ref, db2_ref, scale_ref, wg_ref, wu_ref, dwg_ref, dwu_ref, dwd_ref, part_ref, act_s, da_s, db_s):
    main = act_ref.shape[0]

    @pl.when(pl.program_id(0) == 0)
    def _():
        table = scale_ref[...]
        column, tail_column = column_of(table.astype(f32)), tail_column_of(table)
        for source, source2, target in ((act_ref, act2_ref, act_s), (da_ref, da2_ref, da_s), (db_ref, db2_ref, db_s)):
            target[:main] = (source[...].astype(f32) * column).astype(bf16)
            target[main:] = (source2[...].astype(f32) * tail_column).astype(bf16)

    def both(first, second, scaled):
        return mm_tn(first, scaled[:main]) + mm_tn(second, scaled[main:])

    dwg = both(x_ref[...], x2_ref[...], da_s)
    dwu = both(x_ref[...], x2_ref[...], db_s)
    dwg_ref[...] = dwg.astype(bf16)
    dwu_ref[...] = dwu.astype(bf16)
    dwd_ref[...] = (mm_tn(act_s[:main], c_ref[...]) + mm_tn(act_s[main:], c2_ref[...])).astype(bf16)
    product = dwg * wg_ref[...].astype(f32) + dwu * wu_ref[...].astype(f32)
    folded = product[:, :MSG]
    for j in range(1, product.shape[1] // MSG):
        folded = folded + product[:, j * MSG : (j + 1) * MSG]
    part_ref[...] = jnp.broadcast_to(jnp.sum(folded.T, axis=0, keepdims=True), part_ref.shape)


def weight_grads(r1, xc2, acts, acts2, scale, wg, wu):
    main, tail_rows = r1.shape[0], xc2.shape[0]
    width, hid = wg.shape
    tile = min(256, width)
    steps = width // tile
    return pl.pallas_call(
        weights_kernel,
        grid=(steps,),
        in_specs=[
            pl.BlockSpec((main, tile), lambda i: (0, i)),
            pl.BlockSpec((main, tile), lambda i: (0, i + steps)),
            pl.BlockSpec((tail_rows, tile), lambda i: (0, i)),
            pl.BlockSpec((tail_rows, tile), lambda i: (0, i + steps)),
        ]
        + [whole((main, hid))] * 3
        + [whole((tail_rows, hid))] * 3
        + [whole(scale.shape)]
        + [pl.BlockSpec((tile, hid), lambda i: (i, 0))] * 2,
        out_specs=[
            pl.BlockSpec((tile, hid), lambda i: (i, 0)),
            pl.BlockSpec((tile, hid), lambda i: (i, 0)),
            pl.BlockSpec((hid, tile), lambda i: (0, i)),
            pl.BlockSpec((8, tile), lambda i: (0, i)),
        ],
        out_shape=[
            jax.ShapeDtypeStruct((width, hid), bf16),
            jax.ShapeDtypeStruct((width, hid), bf16),
            jax.ShapeDtypeStruct((hid, width), bf16),
            jax.ShapeDtypeStruct((8, width), f32),
        ],
        scratch_shapes=[pltpu.VMEM((main + tail_rows, hid), bf16)] * 3,
        compiler_params=params(),
        cost_estimate=pl.CostEstimate(flops=6 * (main + tail_rows) * width * hid, bytes_accessed=36_000_000, transcendentals=0),
    )(r1, r1, xc2, xc2, *acts, *acts2, scale, wg, wu)


def home_kernel(q_ref, slot_ref, gates_ref, dl_ref, gk_t_ref, msg_ref):
    experts = q_ref.shape[0]
    q_t = q_ref[...].T
    slot, gates = slot_ref[...], gates_ref[...]
    dgate = jnp.zeros_like(gates)
    kept = jnp.zeros_like(gates)
    for s in range(10):
        here = slot == s
        dgate = dgate + jnp.where(here, q_t[s : s + 1, :], 0.0)
        kept = kept + jnp.where(here, q_t[10 + s : 11 + s, :], 0.0)
    dsel = gates * (dgate - jnp.sum(gates * dgate, axis=1, keepdims=True))
    dl = dsel.astype(bf16)
    dl_ref[...] = dl
    gk_t_ref[...] = (gates.astype(bf16).astype(f32) * kept).T
    dl = dl.astype(f32)
    lane = iota((MSG, experts), 0)
    out = jnp.zeros((MSG, experts), f32)
    for s in range(10):
        out = out + jnp.where(lane == s, jnp.sum(jnp.where(slot == s, dl, 0.0), axis=0, keepdims=True), 0.0)
    msg_ref[...] = out.T


def home(q, slot, gates):
    tokens, experts = slot.shape
    return pl.pallas_call(
        home_kernel,
        out_shape=[
            jax.ShapeDtypeStruct((tokens, experts), bf16),
            jax.ShapeDtypeStruct((experts, tokens), f32),
            jax.ShapeDtypeStruct((experts, MSG), f32),
        ],
        compiler_params=params(),
        cost_estimate=pl.CostEstimate(flops=40 * tokens * experts, bytes_accessed=400_000, transcendentals=0),
    )(q, slot, gates)


def narrow_kernel(ds_ref, x_ref, x2_ref, dx2_ref, part_ref, _, out_ref):
    sources = ds_ref.shape[0]
    width = x_ref.shape[1]
    half = width // 2
    table = ds_ref[...]
    column = jnp.broadcast_to(column_of(table), (sources * HI, MSG)).astype(bf16)
    tail_column = jnp.broadcast_to(tail_column_of(table.astype(bf16)), (2 * sources, MSG)).astype(bf16)
    dr = (mm_tn(column, x_ref[...]) + mm_tn(tail_column, x2_ref[...]))[0:1]
    part = part_ref[0:1, :]
    chunk = min(32, sources)
    n_rows = SUB * chunk
    row, col = iota((n_rows, 4 * chunk), 0), iota((n_rows, 4 * chunk), 1)
    sub = row % SUB
    source_row = 2 * (row // SUB) + sub // 2 + (sub % 2) * 2 * chunk
    pick = jnp.where((sub < 4) & (col == source_row), 1.0, 0.0).astype(bf16)
    sub = iota((n_rows, half), 0) % SUB
    fixed = jnp.where(sub == 4, dr[:, :half], 0.0)
    fixed = jnp.where(sub == 5, dr[:, half:], fixed)
    fixed = jnp.where(sub == 6, part[:, :half], fixed)
    fixed = jnp.where(sub == 7, part[:, half:], fixed)
    for j in range(sources // chunk):
        dx2 = dx2_ref[j * 2 * chunk : (j + 1) * 2 * chunk, :]
        halves = jnp.concatenate([dx2[:, :half], dx2[:, half:]], axis=0)
        out_ref[j * n_rows : (j + 1) * n_rows, :] = (mm(pick, halves) + fixed).astype(bf16)


def narrow(ds, r1, xc2, dx2, part, back):
    sources = ds.shape[0]
    width = dx2.shape[1]
    half = width // 2
    return pl.pallas_call(
        narrow_kernel,
        grid=(1,),
        in_specs=[
            whole(ds.shape),
            pl.BlockSpec((sources * HI, width), lambda i: (0, 0)),
            pl.BlockSpec((2 * sources, width), lambda i: (0, 0)),
            whole(dx2.shape),
            whole(part.shape),
            pl.BlockSpec(memory_space=pl.ANY),
        ],
        out_specs=pl.BlockSpec((sources * SUB, half), lambda i: (0, 2)),
        out_shape=jax.ShapeDtypeStruct(back.shape, bf16),
        input_output_aliases={5: 0},
        compiler_params=params(),
        cost_estimate=pl.CostEstimate(flops=3 * sources * HI * MSG * width, bytes_accessed=9_000_000, transcendentals=0),
    )(ds, r1, xc2, dx2, part, back)


def final_kernel(dx_ref, ext_ref, slot_t_ref, gk_t_ref, dl_ref, router_t_ref, gain_ref, hid_ref, cot_ref, dh_ref, dgain_ref, drouter_ref, total, columns, gains):
    step, last = pl.program_id(0), pl.num_programs(0) - 1
    chunk, tokens = slot_t_ref.shape
    n_rows = chunk * SUB
    width = hid_ref.shape[1]
    half = width // 2
    slot, gk = slot_t_ref[...][:, None, :], gk_t_ref[...][:, None, :]
    which = iota((chunk, SUB, tokens), 1)

    def weights(mask):
        return jnp.where(mask, gk, 0.0).reshape(n_rows, tokens).astype(bf16)

    ext = ext_ref[...]
    main = mm_tn(weights(slot == which.astype(f32)), dx_ref[...])
    in_tail = (which < 4) & (slot == (HI + which // 2).astype(f32))
    low = mm_tn(weights(in_tail & (which % 2 == 0)), ext)
    high = mm_tn(weights(in_tail & (which % 2 == 1)), ext)
    row, col = iota((chunk, n_rows), 0), iota((chunk, n_rows), 1)

    def every(sub):
        return mm(jnp.where(col == row * SUB + sub, 1.0, 0.0).astype(bf16), ext)

    begin = pl.multiple_of(step * chunk, chunk)
    for side, offset in ((0, 0), (1, half)):
        router_rows = every(4 + side)
        columns[pl.ds(begin, chunk), offset : offset + half] = router_rows
        gain_rows = every(6 + side) + router_rows * router_t_ref[:, offset : offset + half].astype(f32)
        gain_sum = jnp.sum(gain_rows, axis=0, keepdims=True)
        tail_part = high if side else low

        @pl.when(step == 0)
        def _():
            gains[:, offset : offset + half] = gain_sum
            total[:, offset : offset + half] = main[:, offset : offset + half] + tail_part

        @pl.when(step > 0)
        def _():
            gains[:, offset : offset + half] += gain_sum
            total[:, offset : offset + half] += main[:, offset : offset + half] + tail_part

    total[...] += mm(dl_ref[...], router_t_ref[...])

    @pl.when(step == last)
    def _():
        gain = gain_ref[...]
        h = hid_ref[...].astype(f32)
        scale = lax.rsqrt(jnp.mean(h * h, axis=1, keepdims=True) + norm_eps)
        gained = gain * total[...]
        mean = jnp.mean(gained * h, axis=1, keepdims=True)
        dh_ref[...] = (cot_ref[...].astype(f32) + scale * gained - h * (scale * scale * scale) * mean).astype(bf16)
        dgain_ref[...] = gains[...] / gain
        drouter_ref[...] = columns[...].T


def final(rd, slot_t, gk_t, dl, router_t, gain, hidden, cotangent):
    experts, tokens = slot_t.shape
    width = hidden.shape[1]
    half = width // 2
    chunk = min(32, experts)
    steps = experts // chunk
    return pl.pallas_call(
        final_kernel,
        grid=(steps,),
        in_specs=[
            pl.BlockSpec((chunk * SUB, width), lambda i: (i, 0)),
            pl.BlockSpec((chunk * SUB, half), lambda i: (i, 2)),
            pl.BlockSpec((chunk, tokens), lambda i: (i, 0)),
            pl.BlockSpec((chunk, tokens), lambda i: (i, 0)),
            pl.BlockSpec((None, tokens, chunk), lambda i: (i, 0, 0)),
            pl.BlockSpec((chunk, width), lambda i: (i, 0)),
            whole((1, width)),
            whole((tokens, width)),
            whole((tokens, width)),
        ],
        out_specs=[whole((tokens, width)), whole((1, width)), whole((width, experts))],
        out_shape=[
            jax.ShapeDtypeStruct((tokens, width), bf16),
            jax.ShapeDtypeStruct((1, width), f32),
            jax.ShapeDtypeStruct((width, experts), f32),
        ],
        scratch_shapes=[pltpu.VMEM((tokens, width), f32), pltpu.VMEM((experts, width), f32), pltpu.VMEM((1, width), f32)],
        compiler_params=params(),
        cost_estimate=pl.CostEstimate(flops=4 * experts * SUB * tokens * width, bytes_accessed=9_000_000, transcendentals=tokens),
    )(rd, rd, slot_t, gk_t, dl, router_t, gain, hidden, cotangent)


def on_device(hidden, cotangent, norm_gain, router, w_gate, w_up, w_down, expert_ids):
    tokens, width = hidden.shape
    top = expert_ids.shape[1]
    experts = router.shape[1]
    half = width // 2
    limit = tokens * top
    gain = norm_gain.reshape(1, width)
    wg, wu, wd = w_gate[0], w_up[0], w_down[0]

    s1, normed, slot, slot_t = front(hidden, cotangent, gain, expert_ids, experts)
    r1 = exchange(s1.reshape(experts, HI, 2 * width)).reshape(experts * HI, 2 * width)
    gates, s2 = second(normed, cotangent, slot, slot_t, router)
    r2 = exchange(s2.reshape(experts, SUB, half + MSG)).reshape(experts * SUB, half + MSG)
    act, da, db, q8, back = rows(r1, wg, wu, wd)
    xc2, act2, da2, db2, q_msg, scale = tail(r2, q8, wg, wu, wd, limit)
    q_home = exchange(q_msg.reshape(experts, 1, MSG)).reshape(experts, MSG)
    dx2 = tail_dx(da2, db2, wg, wu)
    d_wgate, d_wup, d_wdown, part = weight_grads(r1, xc2, (act, da, db), (act2, da2, db2), scale, wg, wu)
    dl, gk_t, ds_msg = home(q_home, slot, gates)
    ds = exchange(ds_msg.reshape(experts, 1, MSG)).reshape(experts, MSG)
    back = narrow(ds, r1, xc2, dx2, part, back)
    rd = exchange(back.reshape(experts, HI, width + half)).reshape(experts * HI, width + half)
    chunk = min(32, experts)
    dl = dl.reshape(tokens, experts // chunk, chunk).transpose(1, 0, 2)
    d_hidden, d_gain, d_router = final(rd, slot_t, gk_t, dl, router.T, gain, hidden, cotangent)
    return (d_hidden, d_gain.reshape(width), d_router, d_wgate[None], d_wup[None], d_wdown[None])


def solution(mesh):
    rows_spec, stack_spec = P(AXES, None), P(AXES, None, None)
    in_specs = (rows_spec, rows_spec, P(), P(), stack_spec, stack_spec, stack_spec, rows_spec)
    out_specs = (rows_spec, P(), P(), stack_spec, stack_spec, stack_spec)
    return jax.shard_map(on_device, mesh=mesh, in_specs=in_specs, out_specs=out_specs, check_vma=False)
```

time: 686 us -> 333 us (0.49)
  local copies, waits for them, and re-layouts: 196 us -> 5.97 us
  Pallas kernels: 0 us -> 91.6 us
  waiting for transfers between devices: 266 us -> 186 us
  blocking collectives: 79.9 us -> 0 us
  matrix products: 55.3 us -> 0 us
  other arithmetic: 17.1 us -> 0 us
  between operations: 15.1 us -> 0.72 us
    pallas_call x0 -> x9, Pallas kernels: none -> 91.6 us  [the longest x1 26 us: rows(): pl.pallas_call(rows_kernel, grid=(total // block,), in_specs=[pl.BlockSpe...]
    gather x12 -> x0, local copies, waits for them, and re-layouts: 79.5 us -> none  [the longest x1 13.6 us: on_device(): back_x = grad_x_pad[place].reshape(expert_count, capacity, model_width)]
    psum x1 -> x0, blocking collectives: 66 us -> none  [on_device(): d_router, d_gain = lax.psum((router_part, gain_part), ('seq', 'exp'))]
    all_to_all x5, waiting for transfers between devices: 245 us -> 186 us  [exchange(): return lax.all_to_all(x, AXES, split_axis=0, concat_axis=0, tiled=True)]
    reshape x8 -> x1, local copies, waits for them, and re-layouts: 58.5 us -> 0.78 us  [on_device(): dl = dl.reshape(tokens, experts // chunk, chunk).transpose(1, 0, 2)]
    dot_general x12 -> x0, matrix products: 55.3 us -> none  [the longest x1 9.21 us: expert_backward(): d_act = jnp.dot(gated, weight_down.T, preferred_element_type=jnp.float32)]
    scatter x4 -> x0, local copies, waits for them, and re-layouts: 44.4 us -> none  [the longest x1 13.8 us: on_device(): cot_rows = jnp.zeros((slot_rows + 1, model_width), jnp.bfloat16).at[place...]
    psum x1 -> x0, waiting for transfers between devices: 20.5 us -> none  [on_device(): d_router, d_gain = lax.psum((router_part, gain_part), ('seq', 'exp'))]
  transfers between devices with their start and end apart: 6 -> 5, of which waited for: 5 -> 4; matrix products, arithmetic and copies ran while one was open for 21% -> 1% of each run, Pallas kernels for 0% -> 17%
where the time goes in v1:
time: 333 us; the launch traced here: 329 us
  waiting for transfers between devices  186 us (56%)
  Pallas kernels  91.6 us (28%)
  starting transfers between devices  44.8 us (13%)
  local copies, waits for them, and re-layouts  5.97 us (2%)
    all_to_all x5, waiting for transfers between devices, exchange(): return lax.all_to_all(x, AXES, split_axis=0, concat_axis=0, tiled=True)  186 us
    all_to_all x5, starting transfers between devices, exchange(): return lax.all_to_all(x, AXES, split_axis=0, concat_axis=0, tiled=True)  44.8 us
    pallas_call x1, Pallas kernels, rows(): pl.pallas_call(rows_kernel, grid=(total // block,), in_specs=[pl.BlockSpe...  26 us
    pallas_call x1, Pallas kernels, weight_grads(): pl.pallas_call(weights_kernel, grid=(steps,), in_specs=[pl.BlockSpec((mai...  19.7 us
    pallas_call x1, Pallas kernels, final(): pl.pallas_call(final_kernel, grid=(steps,), in_specs=[pl.BlockSpec((chunk...  9.32 us
    pallas_call x1, Pallas kernels, tail(): pl.pallas_call(functools.partial(tail_kernel, float(limit)), out_shape=[j...  9.04 us
    pallas_call x1, Pallas kernels, front(): pl.pallas_call(front_kernel, grid=(steps,), in_specs=[whole((tokens, widt...  8.32 us
  transfers between devices with their start and end apart: 5, of which 4 were waited for; matrix products, arithmetic and copies ran while one was open for 1% of the time, Pallas kernels for 17%

profile of v1, /device:TPU:1, one launch (start us, length us, event | category | flops | bytes accessed | tf_op | source)
XLA Modules:
  0.0 329.5 jit_solution(11418870589057569165)
XLA Ops:
  0.6 1.4 copy.21.ids_ref
  2.0 8.3 %shard_map.127 = (bf16[1024,4096]{1,0:T(8,128)(2,1)}, bf16[128,2048]{1,0:T(8,128)(2,1)}, f32[128,128]{1,0:T(8,128)}, f32[128,128]{1,0:T(8,128)}) custom-call(bf16[128,2048]{1,0:T(8,128)(2,1)} %hid_ref.3, bf16[128,2048]{1,0:T(8,128)(2,1)} %cot_ref.5, f32[1,2048]{1,0:T(1,128)} %bitcast.46, s32[128,8]{1,0:T(8,128)} %copy.21.ids_ref), custom_call_target="tpu_custom_call" | custom-call | flops 1073741824 | bytes 10000000 | tf_op jit(solution)/shard_map/pallas_call | solution.py:84
  10.4 12.0 %all-to-all-start.1 = ((bf16[128,8,4096]{2,1,0:T(8,128)(2,1)}), bf16[128,8,4096]{2,1,0:T(8,128)(2,1)}, u32[]{:S(2)}, u32[]{:S(2)}) async-start(bf16[128,8,4096]{2,1,0:T(8,128)(2,1)} %bitcast.35), calls=%async_computation.1 | async-start | bytes 16777216 | tf_op jit(solution)/shard_map/all_to_all | solution.py:44
  22.3 5.3 %shard_map.128 = (f32[128,128]{1,0:T(8,128)}, bf16[1024,1152]{1,0:T(8,128)(2,1)}) custom-call(bf16[128,2048]{1,0:T(8,128)(2,1)} %get-tuple-element.33.normed_ref, bf16[128,2048]{1,0:T(8,128)(2,1)} %cot_ref.5, f32[128,128]{1,0:T(8,128)} %get-tuple-element.34.slot_ref, f32[128,128]{1,0:T(8,128)} %get-tuple-element.35.slot_t_ref, bf16[2048,128]{1,0:T(8,128)(2,1)} %router_ref.1), custom_call_target="tpu_custom_call" | custom-call | flops 1073741824 | bytes 4000000 | tf_op jit(solution)/shard_map/pallas_call | solution.py:139
  27.6 99.9 %all-to-all-done.1 = bf16[128,8,4096]{2,1,0:T(8,128)(2,1)} async-done(((bf16[128,8,4096]{2,1,0:T(8,128)(2,1)}), bf16[128,8,4096]{2,1,0:T(8,128)(2,1)}, u32[]{:S(2)}, u32[]{:S(2)}) %all-to-all-start.1) | async-done | bytes 8388640 | tf_op jit(solution)/shard_map/all_to_all | solution.py:44
  127.5 11.5 %all-to-all-start = ((bf16[128,8,1152]{2,1,0:T(8,128)(2,1)}), bf16[128,8,1152]{2,1,0:T(8,128)(2,1)S(1)}, u32[]{:S(2)}, u32[]{:S(2)}) async-start(bf16[128,8,1152]{2,1,0:T(8,128)(2,1)} %bitcast.38), calls=%async_computation | async-start | bytes 4718592 | tf_op jit(solution)/shard_map/all_to_all | solution.py:44
  139.0 26.0 %shard_map.129 = (bf16[1024,768]{1,0:T(8,128)(2,1)}, bf16[1024,768]{1,0:T(8,128)(2,1)}, bf16[1024,768]{1,0:T(8,128)(2,1)}, f32[128,128]{1,0:T(8,128)}, bf16[1024,3072]{1,0:T(8,128)(2,1)}) custom-call(bf16[1024,4096]{1,0:T(8,128)(2,1)} %bitcast.4.x_ref.c_ref, bf16[1024,4096]{1,0:T(8,128)(2,1)} %bitcast.4.x_ref.c_ref, bf16[2048,768]{1,0:T(8,128)(2,1)} %bitcast.26, ...), custom_call_target="tpu_custom_call" | custom-call | flops 16106127360 | bytes 30000000 | tf_op jit(solution)/shard_map/pallas_call | solution.py:178
  165.0 6.2 %all-to-all-done = bf16[128,8,1152]{2,1,0:T(8,128)(2,1)S(1)} async-done(((bf16[128,8,1152]{2,1,0:T(8,128)(2,1)}), bf16[128,8,1152]{2,1,0:T(8,128)(2,1)S(1)}, u32[]{:S(2)}, u32[]{:S(2)}) %all-to-all-start) | async-done | bytes 2359328 | tf_op jit(solution)/shard_map/all_to_all | solution.py:44
  171.1 0.0 copy-start
  171.1 1.4 copy-done
  172.5 9.0 %shard_map.130 = (bf16[256,4096]{1,0:T(8,128)(2,1)}, bf16[256,768]{1,0:T(8,128)(2,1)}, bf16[256,768]{1,0:T(8,128)(2,1)}, bf16[256,768]{1,0:T(8,128)(2,1)}, f32[128,128]{1,0:T(8,128)}, /*index=5*/bf16[128,128]{1,0:T(8,128)(2,1)}) custom-call(bf16[1024,1152]{1,0:T(8,128)(2,1)} %bitcast.34, f32[128,128]{1,0:T(8,128)} %get-tuple-element.38.q8_ref, ...), custom_call_target="tpu_custom_call" | custom-call | flops 2415919104 | bytes 16000000 | tf_op jit(solution)/shard_map/pallas_call | solution.py:236
  181.6 5.1 %all-to-all-start.2 = ((f32[128,1,128]{2,1,0:T(1,128)}), f32[128,1,128]{2,1,0:T(1,128)S(1)}, u32[]{:S(2)}, u32[]{:S(2)}) async-start(f32[128,1,128]{2,1,0:T(1,128)} %bitcast.44), calls=%async_computation.2 | async-start | bytes 131072 | tf_op jit(solution)/shard_map/all_to_all | solution.py:44
  186.7 19.7 %shard_map.133 = (bf16[2048,768]{1,0:T(8,128)(2,1)}, bf16[2048,768]{1,0:T(8,128)(2,1)}, bf16[768,2048]{1,0:T(8,128)(2,1)}, f32[8,2048]{1,0:T(8,128)}) custom-call(bf16[1024,4096]{1,0:T(8,128)(2,1)} %bitcast.4.x_ref.c_ref, bf16[1024,4096]{1,0:T(8,128)(2,1)} %bitcast.4.x_ref.c_ref, bf16[256,4096]{1,0:T(8,128)(2,1)} %get-tuple-element.42.x2_ref.c2_ref, ...), custom_call_target="tpu_custom_call" | custom-call | flops 12079595520 | bytes 36000000 | tf_op jit(solution)/shard_map/pallas_call | solution.py:305
  206.3 0.0 all-to-all-done.2
  206.4 0.0 copy-start.3
  206.4 0.6 copy-done.3
  207.0 1.9 shard_map.131
  208.9 9.8 %all-to-all-start.3 = ((f32[128,1,128]{2,1,0:T(1,128)}), f32[128,1,128]{2,1,0:T(1,128)S(1)}, u32[]{:S(2)}, u32[]{:S(2)}) async-start(f32[128,1,128]{2,1,0:T(1,128)} %bitcast.45), calls=%async_computation.3 | async-start | bytes 131072 | tf_op jit(solution)/shard_map/all_to_all | solution.py:44
  218.7 5.9 %shard_map.132.dx2_ref = bf16[256,2048]{1,0:T(8,128)(2,1)} custom-call(bf16[256,768]{1,0:T(8,128)(2,1)} %get-tuple-element.43.da_ref.da2_ref, bf16[256,768]{1,0:T(8,128)(2,1)} %get-tuple-element.44.db_ref.db2_ref, bf16[2048,768]{1,0:T(8,128)(2,1)} %bitcast.29, bf16[2048,768]{1,0:T(8,128)(2,1)} %bitcast.33), custom_call_target="tpu_custom_call" | custom-call | flops 1610612736 | bytes 8000000 | tf_op jit(solution)/shard_map/pallas_call | solution.py:251
  224.6 3.7 %all-to-all-done.3 = f32[128,1,128]{2,1,0:T(1,128)S(1)} async-done(((f32[128,1,128]{2,1,0:T(1,128)}), f32[128,1,128]{2,1,0:T(1,128)S(1)}, u32[]{:S(2)}, u32[]{:S(2)}) %all-to-all-start.3) | async-done | bytes 65568 | tf_op jit(solution)/shard_map/all_to_all | solution.py:44
  228.2 0.0 copy-start.2
  228.2 0.6 copy-done.2
  228.9 6.2 %shard_map.134 = bf16[1024,3072]{1,0:T(8,128)(2,1)} custom-call(f32[128,128]{1,0:T(8,128)} %bitcast.41, bf16[1024,4096]{1,0:T(8,128)(2,1)} %bitcast.4.x_ref.c_ref, bf16[256,4096]{1,0:T(8,128)(2,1)} %get-tuple-element.42.x2_ref.c2_ref, bf16[256,2048]{1,0:T(8,128)(2,1)} %shard_map.132.dx2_ref, ...), custom_call_target="tpu_custom_call", output_to_operand_aliasing={{}: (5, {})} | custom-call | flops 805306368 | bytes 9000000 | tf_op jit(solution)/shard_map/pallas_call | solution.py:402
  235.1 0.0 copy-start.1
  235.1 6.5 %all-to-all-start.4 = ((bf16[128,8,3072]{2,1,0:T(8,128)(2,1)}), bf16[128,8,3072]{2,1,0:T(8,128)(2,1)}, u32[]{:S(2)}, u32[]{:S(2)}) async-start(bf16[128,8,3072]{2,1,0:T(8,128)(2,1)} %bitcast.25), calls=%async_computation.4 | async-start | bytes 12582912 | tf_op jit(solution)/shard_map/all_to_all | solution.py:44
  241.6 0.0 copy-done.1
  241.6 1.0 copy.26
  242.6 0.0 copy-done.4
  242.6 0.1 copy.24
  242.7 0.8 copy.25
  243.5 76.7 %all-to-all-done.4 = bf16[128,8,3072]{2,1,0:T(8,128)(2,1)} async-done(((bf16[128,8,3072]{2,1,0:T(8,128)(2,1)}), bf16[128,8,3072]{2,1,0:T(8,128)(2,1)}, u32[]{:S(2)}, u32[]{:S(2)}) %all-to-all-start.4) | async-done | bytes 6291488 | tf_op jit(solution)/shard_map/all_to_all | solution.py:44
  320.1 9.3 %shard_map.135 = (bf16[128,2048]{1,0:T(8,128)(2,1)}, f32[1,2048]{1,0:T(1,128)}, f32[2048,128]{1,0:T(8,128)}) custom-call(bf16[1024,3072]{1,0:T(8,128)(2,1)} %bitcast.15.dx_ref.ext_ref, bf16[1024,3072]{1,0:T(8,128)(2,1)} %bitcast.15.dx_ref.ext_ref, f32[128,128]{1,0:T(8,128)} %get-tuple-element.35.slot_t_ref, f32[128,128]{1,0:T(8,128)} %get-tuple-element.52.gk_t_ref, ...), custom_call_target="tpu_custom_call" | custom-call | flops 1073741824 | bytes 9000000 | tf_op jit(solution)/shard_map/pallas_call | solution.py:481
  (1 shorter events, 0.0 us)
Async XLA Ops:
  10.4 117.2 %all-to-all-start.1 = ((bf16[128,8,4096]{2,1,0:T(8,128)(2,1)}), bf16[128,8,4096]{2,1,0:T(8,128)(2,1)}, u32[]{:S(2)}, u32[]{:S(2)}) async-start(bf16[128,8,4096]{2,1,0:T(8,128)(2,1)} %bitcast.35), calls=%async_computation.1 | async-start | bytes 16777216 | tf_op jit(solution)/shard_map/all_to_all | solution.py:44
  127.5 43.6 %all-to-all-start = ((bf16[128,8,1152]{2,1,0:T(8,128)(2,1)}), bf16[128,8,1152]{2,1,0:T(8,128)(2,1)S(1)}, u32[]{:S(2)}, u32[]{:S(2)}) async-start(bf16[128,8,1152]{2,1,0:T(8,128)(2,1)} %bitcast.38), calls=%async_computation | async-start | bytes 4718592 | tf_op jit(solution)/shard_map/all_to_all | solution.py:44
  171.1 1.4 copy-start
  181.6 24.8 %all-to-all-start.2 = ((f32[128,1,128]{2,1,0:T(1,128)}), f32[128,1,128]{2,1,0:T(1,128)S(1)}, u32[]{:S(2)}, u32[]{:S(2)}) async-start(f32[128,1,128]{2,1,0:T(1,128)} %bitcast.44), calls=%async_computation.2 | async-start | bytes 131072 | tf_op jit(solution)/shard_map/all_to_all | solution.py:44
  206.4 0.6 copy-start.3
  208.9 19.3 %all-to-all-start.3 = ((f32[128,1,128]{2,1,0:T(1,128)}), f32[128,1,128]{2,1,0:T(1,128)S(1)}, u32[]{:S(2)}, u32[]{:S(2)}) async-start(f32[128,1,128]{2,1,0:T(1,128)} %bitcast.45), calls=%async_computation.3 | async-start | bytes 131072 | tf_op jit(solution)/shard_map/all_to_all | solution.py:44
  228.2 0.6 copy-start.2
  235.1 6.5 %copy-start.1 = (bf16[2048,128]{1,0:T(8,128)(2,1)S(1)}, bf16[2048,128]{1,0:T(8,128)(2,1)}, u32[]{:S(2)}) copy-start(bf16[2048,128]{1,0:T(8,128)(2,1)} %router_ref.1) | copy-start | bytes 1572868
  235.1 7.5 %copy-start.4 = (bf16[128,128]{1,0:T(8,128)(2,1)S(1)}, bf16[128,128]{1,0:T(8,128)(2,1)}, u32[]{:S(2)}) copy-start(bf16[128,128]{1,0:T(8,128)(2,1)} %get-tuple-element.53) | copy-start | bytes 98308
  235.1 85.1 %all-to-all-start.4 = ((bf16[128,8,3072]{2,1,0:T(8,128)(2,1)}), bf16[128,8,3072]{2,1,0:T(8,128)(2,1)}, u32[]{:S(2)}, u32[]{:S(2)}) async-start(bf16[128,8,3072]{2,1,0:T(8,128)(2,1)} %bitcast.25), calls=%async_computation.4 | async-start | bytes 12582912 | tf_op jit(solution)/shard_map/all_to_all | solution.py:44

commit v2 on v1

v2 whole, which is shorter than its diff:
```python
import functools

import jax
import jax.numpy as jnp
from jax import lax
from jax.experimental import pallas as pl
from jax.experimental.pallas import tpu as pltpu
from jax.sharding import PartitionSpec as P

norm_eps = 1e-06
HI = 8
SUB = 8
MSG = 128
AXES = ("seq", "exp")
bf16, f32 = jnp.bfloat16, jnp.float32


def params():
    return pltpu.CompilerParams(vmem_limit_bytes=60 * 1024 * 1024)


def whole(shape, **kw):
    return pl.BlockSpec(shape, lambda *_: (0,) * len(shape), **kw)


def iota(shape, dim):
    return lax.broadcasted_iota(jnp.int32, shape, dim)


def mm(a, b):
    return jnp.dot(a, b, preferred_element_type=f32)


def mm_nt(a, b):
    return lax.dot_general(a, b, (((1,), (1,)), ((), ())), preferred_element_type=f32)


def mm_tn(a, b):
    return lax.dot_general(a, b, (((0,), (0,)), ((), ())), preferred_element_type=f32)


def exchange(x):
    return lax.all_to_all(x, AXES, split_axis=0, concat_axis=0, tiled=True)


def front_kernel(hid_ref, cot_ref, gain_ref, ids_ref, s1_ref, normed_ref, slot_ref, slot_t_ref, nc, p8):
    step = pl.program_id(0)
    tokens, width = hid_ref.shape
    experts = slot_ref.shape[1]
    tile = nc.shape[2]

    @pl.when(step == 0)
    def _():
        h = hid_ref[...].astype(f32)
        scale = lax.rsqrt(jnp.mean(h * h, axis=1, keepdims=True) + norm_eps)
        normed = (h * scale * gain_ref[...]).astype(bf16)
        normed_ref[...] = normed
        for j in range(width // tile):
            nc[j] = normed[:, j * tile : (j + 1) * tile]
            nc[width // tile + j] = cot_ref[:, j * tile : (j + 1) * tile]
        ids = ids_ref[...]
        expert = iota((experts, tokens), 0)
        member = jnp.zeros((experts, tokens), f32)
        for k in range(ids.shape[0]):
            member += jnp.where(ids[k : k + 1, :] == expert, 1.0, 0.0)
        earlier = jnp.where(iota((tokens, tokens), 0) < iota((tokens, tokens), 1), 1.0, 0.0)
        position = mm(member.astype(bf16), earlier.astype(bf16))
        slot_t = jnp.where(member > 0.0, position, 99.0)
        slot_ref[...] = slot_t.T
        slot_t_ref[...] = slot_t
        which = iota((experts, HI, tokens), 1).astype(f32)
        chosen = jnp.where(slot_t[:, None, :] == which, 1.0, 0.0)
        p8[...] = chosen.reshape(experts * HI, tokens).astype(bf16)

    s1_ref[...] = mm(p8[...], nc[step]).astype(bf16)


def front(hidden, cotangent, gain, ids, experts):
    tokens, width = hidden.shape
    tile = min(512, width)
    steps = 2 * width // tile
    return pl.pallas_call(
        front_kernel,
        grid=(steps,),
        in_specs=[whole((tokens, width)), whole((tokens, width)), whole((1, width)), whole(ids.shape)],
        out_specs=[
            pl.BlockSpec((experts * HI, tile), lambda i: (0, i)),
            whole((tokens, width)),
            whole((tokens, experts)),
            whole((experts, tokens)),
        ],
        out_shape=[
            jax.ShapeDtypeStruct((experts * HI, 2 * width), bf16),
            jax.ShapeDtypeStruct((tokens, width), bf16),
            jax.ShapeDtypeStruct((tokens, experts), f32),
            jax.ShapeDtypeStruct((experts, tokens), f32),
        ],
        scratch_shapes=[pltpu.VMEM((steps, tokens, tile), bf16), pltpu.VMEM((experts * HI, tokens), bf16)],
        compiler_params=params(),
        cost_estimate=pl.CostEstimate(flops=4 * experts * HI * tokens * width, bytes_accessed=10_000_000, transcendentals=tokens),
    )(hidden, cotangent, gain, ids)


def second_kernel(normed_ref, cot_ref, slot_ref, slot_t_ref, router_ref, gates_ref, s2_ref):
    tokens, width = normed_ref.shape
    experts = slot_ref.shape[1]
    half = width // 2
    logits = mm(normed_ref[...], router_ref[...])
    weights = jnp.where(slot_ref[...] < 50.0, jnp.exp(logits), 0.0)
    gates = weights / jnp.sum(weights, axis=1, keepdims=True)
    gates_ref[...] = gates
    slot_t = slot_t_ref[...]
    gates_t = gates.T
    lane = iota((experts, MSG), 1)
    message = jnp.where(lane == 10, jnp.sum(jnp.where(slot_t < 50.0, 1.0, 0.0), axis=1, keepdims=True), 0.0)
    for s in range(10):
        message = message + jnp.where(
            lane == s, jnp.sum(jnp.where(slot_t == s, gates_t, 0.0), axis=1, keepdims=True), 0.0
        )
    sub = iota((experts, SUB, MSG), 1)
    spread = jnp.where(sub == 0, message[:, None, :], 0.0).reshape(experts * SUB, MSG)
    s2_ref[:, half:] = spread.astype(bf16)
    row = iota((experts, SUB, tokens), 1)
    chosen = jnp.where(slot_t[:, None, :] == (HI + row // 4).astype(f32), 1.0, 0.0)
    total = None
    for j in range(4):
        pick = jnp.where(row % 4 == j, chosen, 0.0).reshape(experts * SUB, tokens).astype(bf16)
        source = normed_ref if j < 2 else cot_ref
        term = mm(pick, source[:, (j % 2) * half : (j % 2 + 1) * half])
        total = term if total is None else total + term
    s2_ref[:, :half] = total.astype(bf16)


def second(normed, cotangent, slot, slot_t, router):
    tokens, width = normed.shape
    experts = slot.shape[1]
    return pl.pallas_call(
        second_kernel,
        out_shape=[
            jax.ShapeDtypeStruct((tokens, experts), f32),
            jax.ShapeDtypeStruct((experts * SUB, width // 2 + MSG), bf16),
        ],
        compiler_params=params(),
        cost_estimate=pl.CostEstimate(flops=4 * experts * SUB * tokens * width, bytes_accessed=4_000_000, transcendentals=tokens * experts),
    )(normed, cotangent, slot, slot_t, router)


def expert_rows(x, c, wg_ref, wu_ref, wd_ref):
    a = mm(x, wg_ref[...])
    b = mm(x, wu_ref[...])
    u = mm_nt(c, wd_ref[...])
    s = jax.nn.sigmoid(a)
    act = (a * s * b).astype(bf16)
    q = jnp.sum(act.astype(f32) * u, axis=1, keepdims=True)
    da = (u * b * s * (1.0 + a * (1.0 - s))).astype(bf16)
    db = (u * a * s).astype(bf16)
    return act, q, da, db


def rows_kernel(x_ref, c_ref, wg_ref, wu_ref, wd_ref, act_ref, da_ref, db_ref, q_ref, dx_ref):
    act, q, da, db = expert_rows(x_ref[...], c_ref[...], wg_ref, wu_ref, wd_ref)
    act_ref[...] = act
    da_ref[...] = da
    db_ref[...] = db
    sources = q_ref.shape[0]
    lane, which = iota((sources, HI, MSG), 2), iota((sources, HI, MSG), 1)
    q_ref[...] = jnp.sum(jnp.where(lane == which, q.reshape(sources, HI, 1), 0.0), axis=1)
    dx_ref[...] = (mm_nt(da, wg_ref[...]) + mm_nt(db, wu_ref[...])).astype(bf16)


def rows(r1, wg, wu, wd, extra):
    total, both = r1.shape
    width, hid = wg.shape
    block = min(256, total)
    one = pl.BlockSpec((block, hid), lambda i: (i, 0))
    return pl.pallas_call(
        rows_kernel,
        grid=(total // block,),
        in_specs=[
            pl.BlockSpec((block, width), lambda i: (i, 0)),
            pl.BlockSpec((block, width), lambda i: (i, 1)),
            whole(wg.shape, pipeline_mode=pl.Buffered(1)),
            whole(wu.shape, pipeline_mode=pl.Buffered(1)),
            whole(wd.shape, pipeline_mode=pl.Buffered(1)),
        ],
        out_specs=[one, one, one, pl.BlockSpec((block // HI, MSG), lambda i: (i, 0)), pl.BlockSpec((block, width), lambda i: (i, 0))],
        out_shape=[jax.ShapeDtypeStruct((total, hid), bf16)] * 3
        + [
            jax.ShapeDtypeStruct((total // HI, MSG), f32),
            jax.ShapeDtypeStruct((total, width + extra), bf16),
        ],
        compiler_params=params(),
        cost_estimate=pl.CostEstimate(flops=10 * total * width * hid, bytes_accessed=30_000_000, transcendentals=total * hid),
    )(r1, r1, wg, wu, wd)


def tail_kernel(limit, r2_ref, q8_ref, wg_ref, wu_ref, wd_ref, xc_ref, act_ref, da_ref, db_ref, msg_ref, scale_ref, q_sum):
    step, last = pl.program_id(0), pl.num_programs(0) - 1
    sources = q8_ref.shape[0]
    width = wg_ref.shape[0]
    half = width // 2
    total = 2 * sources

    @pl.when(step == 0)
    def _():
        chunk = min(32, sources)
        out_rows, in_rows = 2 * chunk, SUB * chunk
        index, column = iota((4 * out_rows, in_rows), 0), iota((4 * out_rows, in_rows), 1)
        pick = jnp.where(column == 4 * (index % out_rows) + index // out_rows, 1.0, 0.0).astype(bf16)
        for j in range(sources // chunk):
            part = mm(pick, r2_ref[j * in_rows : (j + 1) * in_rows, :half]).astype(bf16)
            for quarter in range(4):
                xc_ref[j * out_rows : (j + 1) * out_rows, quarter * half : (quarter + 1) * half] = part[
                    quarter * out_rows : (quarter + 1) * out_rows
                ]
        q_sum[...] = jnp.zeros_like(q_sum)

    act, q, da, db = expert_rows(xc_ref[:, :width], xc_ref[:, width:], wg_ref, wu_ref, wd_ref)
    act_ref[...] = act
    da_ref[...] = da
    db_ref[...] = db
    q_sum[...] += jnp.broadcast_to(q, q_sum.shape)

    @pl.when(step == last)
    def _():
        parity = iota((total, MSG), 0) % 2
        spread = jnp.where(iota((total, MSG), 1) == HI + parity, q_sum[...], 0.0).astype(bf16)
        gather = jnp.where(iota((sources, total), 1) // 2 == iota((sources, total), 0), 1.0, 0.0).astype(bf16)
        q_all = q8_ref[...].astype(bf16).astype(f32) + mm(gather, spread)
        meta = jnp.sum(r2_ref[:, half:].astype(f32).reshape(sources, SUB, MSG), axis=1)
        lane = iota((sources, MSG), 1)
        count = jnp.sum(jnp.where(lane == 10, meta, 0.0), axis=1, keepdims=True)
        lower = jnp.where(iota((sources, sources), 1) < iota((sources, sources), 0), 1.0, 0.0).astype(bf16)
        offset = mm(lower, jnp.broadcast_to(count, (sources, MSG)).astype(bf16))
        slot = jnp.where(lane < 10, lane, lane - 10).astype(f32)
        kept = (slot < count) & (offset + slot < limit) & (lane < 20)
        msg_ref[...] = jnp.where(kept, jnp.where(lane < 10, q_all, 1.0), 0.0)
        scale_ref[...] = jnp.where(kept & (lane < 10), meta, 0.0).astype(bf16)


def tail(r2, q8, wg, wu, wd, limit):
    sources = q8.shape[0]
    width, hid = wg.shape
    tile = min(256, hid)
    total = 2 * sources
    return pl.pallas_call(
        functools.partial(tail_kernel, float(limit)),
        grid=(hid // tile,),
        in_specs=[
            whole(r2.shape, pipeline_mode=pl.Buffered(1)),
            whole(q8.shape),
            pl.BlockSpec((width, tile), lambda i: (0, i)),
            pl.BlockSpec((width, tile), lambda i: (0, i)),
            pl.BlockSpec((tile, width), lambda i: (i, 0)),
        ],
        out_specs=[whole((total, 2 * width))]
        + [pl.BlockSpec((total, tile), lambda i: (0, i))] * 3
        + [whole((sources, MSG)), whole((sources, MSG))],
        out_shape=[jax.ShapeDtypeStruct((total, 2 * width), bf16)]
        + [jax.ShapeDtypeStruct((total, hid), bf16)] * 3
        + [jax.ShapeDtypeStruct((sources, MSG), f32), jax.ShapeDtypeStruct((sources, MSG), bf16)],
        scratch_shapes=[pltpu.VMEM((total, MSG), f32)],
        compiler_params=params(),
        cost_estimate=pl.CostEstimate(flops=12 * sources * width * hid, bytes_accessed=16_000_000, transcendentals=2 * sources * hid),
    )(r2, q8, wg, wu, wd)


def column_of(table):
    sources = table.shape[0]
    lane, which = iota((sources, HI, MSG), 2), iota((sources, HI, MSG), 1)
    spread = jnp.where(lane == which, table[:, None, :], 0.0)
    return jnp.sum(spread.reshape(sources * HI, MSG), axis=1, keepdims=True)


def tail_column_of(table):
    sources = table.shape[0]
    total = 2 * sources
    scatter = jnp.where(iota((total, sources), 0) // 2 == iota((total, sources), 1), 1.0, 0.0).astype(bf16)
    lane = HI + iota((total, MSG), 0) % 2
    return jnp.sum(jnp.where(iota((total, MSG), 1) == lane, mm(scatter, table), 0.0), axis=1, keepdims=True)


def tail_dx_kernel(da_ref, db_ref, wg_ref, wu_ref, x_ref, x2_ref, scale_ref, back_ref, out_ref, part_ref, s8, s2):
    step = pl.program_id(0)
    sources = scale_ref.shape[0]
    quarter = out_ref.shape[1]

    @pl.when(step == 0)
    def _():
        table = scale_ref[...]
        s8[...] = jnp.broadcast_to(column_of(table.astype(f32)), s8.shape)
        s2[...] = jnp.broadcast_to(tail_column_of(table), s2.shape)
        out_ref[...] = jnp.zeros_like(out_ref)

    dx2 = mm_nt(da_ref[...], wg_ref[...]) + mm_nt(db_ref[...], wu_ref[...])
    rounded = dx2.astype(bf16)
    chunk = min(32, sources)
    n_rows = SUB * chunk
    pick = jnp.where(iota((n_rows, 2 * chunk), 0) == 4 * iota((n_rows, 2 * chunk), 1) + step, 1.0, 0.0).astype(bf16)
    for j in range(sources // chunk):
        out_ref[j * n_rows : (j + 1) * n_rows, :] += mm(pick, rounded[j * 2 * chunk : (j + 1) * 2 * chunk]).astype(bf16)
    part = jnp.sum(x_ref[...].astype(f32) * back_ref[...].astype(f32) * s8[:, 0:1], axis=0, keepdims=True)
    part = part + jnp.sum(x2_ref[...].astype(f32) * dx2 * s2[:, 0:1], axis=0, keepdims=True)
    column = jnp.concatenate(
        [jnp.broadcast_to(part[:, j : j + MSG], (MSG, MSG)).T for j in range(0, quarter, MSG)], axis=0
    )
    dests = part_ref.shape[0] // SUB
    groups = quarter // dests // SUB
    column = column.reshape(dests, groups, SUB, MSG)
    lane = iota((dests, SUB, MSG), 2)
    spread = jnp.zeros((dests, SUB, MSG), f32)
    for g in range(groups):
        spread = jnp.where(lane == g, column[:, g], spread)
    part_ref[...] = spread.reshape(dests * SUB, MSG).astype(bf16)


def tail_dx(da, db, wg, wu, r1, xc2, scale, back):
    sources = scale.shape[0]
    width, hid = wg.shape
    quarter = width // 4
    main, total = sources * HI, 2 * sources
    columns = pl.BlockSpec((main, quarter), lambda i: (0, i))
    return pl.pallas_call(
        tail_dx_kernel,
        grid=(4,),
        in_specs=[
            whole(da.shape),
            whole(db.shape),
            pl.BlockSpec((quarter, hid), lambda i: (i, 0)),
            pl.BlockSpec((quarter, hid), lambda i: (i, 0)),
            columns,
            pl.BlockSpec((total, quarter), lambda i: (0, i)),
            whole(scale.shape),
            columns,
        ],
        out_specs=[
            pl.BlockSpec((sources * SUB, quarter), lambda i: (0, 4)),
            pl.BlockSpec((sources * SUB // 4, MSG), lambda i: (i, 0)),
        ],
        out_shape=[jax.ShapeDtypeStruct(back.shape, bf16), jax.ShapeDtypeStruct((sources * SUB, MSG), bf16)],
        scratch_shapes=[pltpu.VMEM((main, MSG), f32), pltpu.VMEM((total, MSG), f32)],
        input_output_aliases={7: 0},
        compiler_params=params(),
        cost_estimate=pl.CostEstimate(flops=4 * total * wg.size, bytes_accessed=18_000_000, transcendentals=0),
    )(da, db, wg, wu, r1, xc2, scale, back)


def weights_kernel(x_ref, c_ref, x2_ref, c2_ref, act_ref, da_ref, db_ref, act2_ref, da2_ref, db2_ref, scale_ref, dwg_ref, dwu_ref, dwd_ref, act_s, da_s, db_s):
    main = act_ref.shape[0]

    @pl.when(pl.program_id(0) == 0)
    def _():
        table = scale_ref[...]
        column, tail_column = column_of(table.astype(f32)), tail_column_of(table)
        for source, source2, target in ((act_ref, act2_ref, act_s), (da_ref, da2_ref, da_s), (db_ref, db2_ref, db_s)):
            target[:main] = (source[...].astype(f32) * column).astype(bf16)
            target[main:] = (source2[...].astype(f32) * tail_column).astype(bf16)

    def both(first, second, scaled):
        return mm_tn(first, scaled[:main]) + mm_tn(second, scaled[main:])

    dwg_ref[...] = both(x_ref[...], x2_ref[...], da_s).astype(bf16)
    dwu_ref[...] = both(x_ref[...], x2_ref[...], db_s).astype(bf16)
    dwd_ref[...] = (mm_tn(act_s[:main], c_ref[...]) + mm_tn(act_s[main:], c2_ref[...])).astype(bf16)


def weight_grads(r1, xc2, acts, acts2, scale, width, hid):
    main, tail_rows = r1.shape[0], xc2.shape[0]
    tile = min(256, width)
    steps = width // tile
    return pl.pallas_call(
        weights_kernel,
        grid=(steps,),
        in_specs=[
            pl.BlockSpec((main, tile), lambda i: (0, i)),
            pl.BlockSpec((main, tile), lambda i: (0, i + steps)),
            pl.BlockSpec((tail_rows, tile), lambda i: (0, i)),
            pl.BlockSpec((tail_rows, tile), lambda i: (0, i + steps)),
        ]
        + [whole((main, hid))] * 3
        + [whole((tail_rows, hid))] * 3
        + [whole(scale.shape)],
        out_specs=[
            pl.BlockSpec((tile, hid), lambda i: (i, 0)),
            pl.BlockSpec((tile, hid), lambda i: (i, 0)),
            pl.BlockSpec((hid, tile), lambda i: (0, i)),
        ],
        out_shape=[
            jax.ShapeDtypeStruct((width, hid), bf16),
            jax.ShapeDtypeStruct((width, hid), bf16),
            jax.ShapeDtypeStruct((hid, width), bf16),
        ],
        scratch_shapes=[pltpu.VMEM((main + tail_rows, hid), bf16)] * 3,
        compiler_params=params(),
        cost_estimate=pl.CostEstimate(flops=6 * (main + tail_rows) * width * hid, bytes_accessed=36_000_000, transcendentals=0),
    )(r1, r1, xc2, xc2, *acts, *acts2, scale)


def home_kernel(q_ref, slot_ref, gates_ref, normed_ref, part_ref, _, back_ref, dl_ref, gk_t_ref, router_part):
    step, last = pl.program_id(0), pl.num_programs(0) - 1
    experts = q_ref.shape[0]

    @pl.when(step == 0)
    def _():
        q_t = q_ref[...].T
        slot, gates = slot_ref[...], gates_ref[...]
        dgate = jnp.zeros_like(gates)
        kept = jnp.zeros_like(gates)
        for s in range(10):
            here = slot == s
            dgate = dgate + jnp.where(here, q_t[s : s + 1, :], 0.0)
            kept = kept + jnp.where(here, q_t[10 + s : 11 + s, :], 0.0)
        dsel = gates * (dgate - jnp.sum(gates * dgate, axis=1, keepdims=True))
        dl = dsel.astype(bf16)
        dl_ref[...] = dl
        gk_t_ref[...] = (gates.astype(bf16).astype(f32) * kept).T
        if experts < MSG:
            dl = jnp.concatenate([dl, jnp.zeros((dl.shape[0], MSG - experts), bf16)], axis=1)
        groups = router_part.shape[0]
        partial = mm_tn(normed_ref[...], dl).reshape(experts, groups, SUB, MSG)
        for g in range(groups):
            router_part[g] = partial[:, g].reshape(experts * SUB, MSG).astype(bf16)

    @pl.when(step < last)
    def _():
        back_ref[...] = router_part[jnp.minimum(step, router_part.shape[0] - 1)]

    @pl.when(step == last)
    def _():
        back_ref[...] = part_ref[...]


def home(q, slot, gates, normed, part, back):
    tokens, experts = slot.shape
    width = normed.shape[1]
    groups = width // experts // SUB
    first = (width + width // 4) // MSG
    return pl.pallas_call(
        home_kernel,
        grid=(groups + 1,),
        in_specs=[whole(q.shape), whole(slot.shape), whole(gates.shape), whole(normed.shape), whole(part.shape), pl.BlockSpec(memory_space=pl.ANY)],
        out_specs=[pl.BlockSpec((experts * SUB, MSG), lambda i: (0, first + i)), whole((tokens, experts)), whole((experts, tokens))],
        out_shape=[
            jax.ShapeDtypeStruct(back.shape, bf16),
            jax.ShapeDtypeStruct((tokens, experts), bf16),
            jax.ShapeDtypeStruct((experts, tokens), f32),
        ],
        scratch_shapes=[pltpu.VMEM((groups, experts * SUB, MSG), bf16)],
        input_output_aliases={5: 0},
        compiler_params=params(),
        cost_estimate=pl.CostEstimate(flops=2 * tokens * MSG * width, bytes_accessed=2_500_000, transcendentals=0),
    )(q, slot, gates, normed, part, back)


def sums_kernel(*refs):
    *parts, gain_ref, router_ref, gain_rows_ref, target_ref, out_ref = refs
    copies, n_rows, _ = out_ref.shape
    target = target_ref[...]
    row = iota(target.shape, 0)
    gain_parts = jnp.sum(gain_ref[...].astype(f32).reshape(copies, SUB, MSG), axis=0)
    pieces = []
    placed = jnp.zeros(target.shape, f32)
    for g, ref in enumerate(parts):
        piece = jnp.sum(ref[...].astype(f32).reshape(copies, SUB, MSG), axis=0)
        pieces.append(piece)
        own = slice(g * SUB, (g + 1) * SUB)
        value = gain_parts[:, g : g + 1] + jnp.sum(router_ref[own] * piece, axis=1, keepdims=True)
        placed = jnp.where(target == g * SUB + row, value / gain_rows_ref[own], placed)
    message = jnp.concatenate(pieces + [placed], axis=0)
    out_ref[...] = jnp.broadcast_to(message[None], out_ref.shape).astype(bf16)


def sums(rd, router_rows, gain_rows, target, experts, width):
    groups = width // experts // SUB
    first = (width + width // 4) // MSG
    block = (experts * SUB, MSG)
    specs = [pl.BlockSpec(block, functools.partial(lambda g, i: (0, first + g), g)) for g in range(groups + 1)]
    return pl.pallas_call(
        sums_kernel,
        grid=(1,),
        in_specs=specs + [whole(router_rows.shape), whole(gain_rows.shape), whole(target.shape)],
        out_specs=whole((experts, (groups + 1) * SUB, MSG)),
        out_shape=jax.ShapeDtypeStruct((experts, (groups + 1) * SUB, MSG), bf16),
        compiler_params=params(),
        cost_estimate=pl.CostEstimate(flops=experts * SUB * MSG * 8, bytes_accessed=2_000_000, transcendentals=0),
    )(*[rd] * (groups + 1), router_rows, gain_rows, target)


def final_kernel(dx_ref, ext_ref, slot_t_ref, gk_t_ref, dl_ref, router_ref, gain_ref, hid_ref, cot_ref, dh_ref, total):
    step, last = pl.program_id(0), pl.num_programs(0) - 1
    chunk, tokens = slot_t_ref.shape
    n_rows = chunk * SUB
    quarter = ext_ref.shape[1]
    slot, gk = slot_t_ref[...][:, None, :], gk_t_ref[...][:, None, :]
    which = iota((chunk, SUB, tokens), 1)

    def weights(mask):
        return jnp.where(mask, gk, 0.0).reshape(n_rows, tokens).astype(bf16)

    @pl.when(step == 0)
    def _():
        total[...] = mm_nt(dl_ref[...], router_ref[...])

    total[...] += mm_tn(weights(slot == which.astype(f32)), dx_ref[...])
    in_tail = slot == (HI + which // 4).astype(f32)
    for j in range(4):
        total[:, j * quarter : (j + 1) * quarter] += mm_tn(weights(in_tail & (which % 4 == j)), ext_ref[...])

    @pl.when(step == last)
    def _():
        h = hid_ref[...].astype(f32)
        scale = lax.rsqrt(jnp.mean(h * h, axis=1, keepdims=True) + norm_eps)
        gained = gain_ref[...] * total[...]
        mean = jnp.mean(gained * h, axis=1, keepdims=True)
        dh_ref[...] = (cot_ref[...].astype(f32) + scale * gained - h * (scale * scale * scale) * mean).astype(bf16)


def final(rd, slot_t, gk_t, dl, router, gain, hidden, cotangent):
    experts, tokens = slot_t.shape
    width = hidden.shape[1]
    chunk = min(32, experts)
    steps = experts // chunk
    return pl.pallas_call(
        final_kernel,
        grid=(steps,),
        in_specs=[
            pl.BlockSpec((chunk * SUB, width), lambda i: (i, 0)),
            pl.BlockSpec((chunk * SUB, width // 4), lambda i: (i, 4)),
            pl.BlockSpec((chunk, tokens), lambda i: (i, 0)),
            pl.BlockSpec((chunk, tokens), lambda i: (i, 0)),
            whole(dl.shape),
            whole(router.shape),
            whole((1, width)),
            whole((tokens, width)),
            whole((tokens, width)),
        ],
        out_specs=whole((tokens, width)),
        out_shape=jax.ShapeDtypeStruct((tokens, width), bf16),
        scratch_shapes=[pltpu.VMEM((tokens, width), f32)],
        compiler_params=params(),
        cost_estimate=pl.CostEstimate(flops=4 * experts * SUB * tokens * width, bytes_accessed=9_000_000, transcendentals=tokens),
    )(rd, rd, slot_t, gk_t, dl, router, gain, hidden, cotangent)


def place_kernel(sums_ref, router_ref, gain_ref):
    experts, n_rows, _ = sums_ref.shape
    rows_each = n_rows - SUB
    received = sums_ref[...].astype(f32)
    router_ref[...] = received[:, :rows_each].reshape(experts * rows_each, MSG)[:, : router_ref.shape[1]]
    gain_ref[...] = jnp.sum(received[:, rows_each:].reshape(gain_ref.shape[0], -1, MSG), axis=1)


def place(received, width, experts):
    return pl.pallas_call(
        place_kernel,
        out_shape=[jax.ShapeDtypeStruct((width, experts), f32), jax.ShapeDtypeStruct((width // MSG, MSG), f32)],
        compiler_params=params(),
        cost_estimate=pl.CostEstimate(flops=received.size, bytes_accessed=2_000_000, transcendentals=0),
    )(received)


def on_device(hidden, cotangent, norm_gain, router, w_gate, w_up, w_down, expert_ids):
    tokens, width = hidden.shape
    top = expert_ids.shape[1]
    experts = router.shape[1]
    half, quarter = width // 2, width // 4
    limit = tokens * top
    gain = norm_gain.reshape(1, width)
    wg, wu, wd = w_gate[0], w_up[0], w_down[0]
    own = width // experts
    extra = quarter + (own // SUB + 1) * MSG

    me = lax.axis_index(AXES)
    router_rows = lax.dynamic_slice_in_dim(router, me * own, own, 0).astype(f32)
    router_rows = jnp.pad(router_rows, ((0, 0), (0, MSG - experts)))
    gain_rows = jnp.broadcast_to(lax.dynamic_slice_in_dim(norm_gain, me * own, own, 0)[:, None], (own, MSG))
    target = lax.broadcasted_iota(jnp.int32, (SUB, MSG), 1) - (me % (MSG // own)) * own

    s1, normed, slot, slot_t = front(hidden, cotangent, gain, expert_ids.T, experts)
    r1 = exchange(s1.reshape(experts, HI, 2 * width)).reshape(experts * HI, 2 * width)
    gates, s2 = second(normed, cotangent, slot, slot_t, router)
    r2 = exchange(s2.reshape(experts, SUB, half + MSG)).reshape(experts * SUB, half + MSG)
    act, da, db, q8, back = rows(r1, wg, wu, wd, extra)
    xc2, act2, da2, db2, q_msg, scale = tail(r2, q8, wg, wu, wd, limit)
    q_home = exchange(q_msg.reshape(experts, 1, MSG)).reshape(experts, MSG)
    back, part = tail_dx(da2, db2, wg, wu, r1, xc2, scale, back)
    back, dl, gk_t = home(q_home, slot, gates, normed, part, back)
    scale, dl = lax.optimization_barrier((scale, dl))
    d_wgate, d_wup, d_wdown = weight_grads(r1, xc2, (act, da, db), (act2, da2, db2), scale, width, wg.shape[1])
    rd = exchange(back.reshape(experts, HI, width + extra)).reshape(experts * HI, width + extra)
    d_wgate, gain_rows = lax.optimization_barrier((d_wgate, gain_rows))
    message = sums(rd, router_rows, gain_rows, target, experts, width)
    received = exchange(message)
    d_hidden = final(rd, slot_t, gk_t, dl, router, gain, hidden, cotangent)
    d_router, d_gain = place(received, width, experts)
    return (d_hidden, d_gain.reshape(width), d_router, d_wgate[None], d_wup[None], d_wdown[None])


def solution(mesh):
    rows_spec, stack_spec = P(AXES, None), P(AXES, None, None)
    in_specs = (rows_spec, rows_spec, P(), P(), stack_spec, stack_spec, stack_spec, rows_spec)
    out_specs = (rows_spec, P(), P(), stack_spec, stack_spec, stack_spec)
    return jax.shard_map(on_device, mesh=mesh, in_specs=in_specs, out_specs=out_specs, check_vma=False)
```

time: 333 us -> 315 us (0.946)
  waiting for transfers between devices: 186 us -> 169 us
    all_to_all x5, waiting for transfers between devices: 186 us -> 169 us  [exchange(): return lax.all_to_all(x, AXES, split_axis=0, concat_axis=0, tiled=True)]
    pallas_call x4 -> x5, Pallas kernels: 23 us -> 27.1 us  [the longest x1 9.83 us: tail(): pl.pallas_call(functools.partial(tail_kernel, float(limit)), grid=(hid //...]
  transfers between devices with their start and end apart: 5 -> 5, of which waited for: 4 -> 5; matrix products, arithmetic and copies ran while one was open for 1% -> 1% of each run, Pallas kernels for 17% -> 21%
where the time goes in v2:
time: 315 us; the launch traced here: 314 us
  waiting for transfers between devices  169 us (54%)
  Pallas kernels  92 us (29%)
  starting transfers between devices  46.8 us (15%)
  local copies, waits for them, and re-layouts  4.93 us (2%)
    all_to_all x5, waiting for transfers between devices, exchange(): return lax.all_to_all(x, AXES, split_axis=0, concat_axis=0, tiled=True)  169 us
    all_to_all x5, starting transfers between devices, exchange(): return lax.all_to_all(x, AXES, split_axis=0, concat_axis=0, tiled=True)  46.8 us
    pallas_call x1, Pallas kernels, rows(): pl.pallas_call(rows_kernel, grid=(total // block,), in_specs=[pl.BlockSpe...  26 us
    pallas_call x1, Pallas kernels, weight_grads(): pl.pallas_call(weights_kernel, grid=(steps,), in_specs=[pl.BlockSpec((mai...  19.3 us
    pallas_call x1, Pallas kernels, tail(): pl.pallas_call(functools.partial(tail_kernel, float(limit)), grid=(hid //...  9.83 us
    pallas_call x1, Pallas kernels, tail_dx(): pl.pallas_call(tail_dx_kernel, grid=(4,), in_specs=[whole(da.shape), whol...  9.48 us
    pallas_call x1, Pallas kernels, front(): pl.pallas_call(front_kernel, grid=(steps,), in_specs=[whole((tokens, widt...  7.94 us
    pallas_call x1, Pallas kernels, final(): pl.pallas_call(final_kernel, grid=(steps,), in_specs=[pl.BlockSpec((chunk...  6.45 us
  transfers between devices with their start and end apart: 5, of which 5 were waited for; matrix products, arithmetic and copies ran while one was open for 1% of the time, Pallas kernels for 21%

profile of v2, /device:TPU:1, one launch (start us, length us, event | category | flops | bytes accessed | tf_op | source)
XLA Modules:
  0.0 314.4 jit_solution(4614596104136925922)
XLA Ops:
  0.6 7.9 %shard_map.127 = (bf16[1024,4096]{1,0:T(8,128)(2,1)}, bf16[128,2048]{1,0:T(8,128)(2,1)}, f32[128,128]{1,0:T(8,128)}, f32[128,128]{1,0:T(8,128)}) custom-call(bf16[128,2048]{1,0:T(8,128)(2,1)} %hid_ref.3, bf16[128,2048]{1,0:T(8,128)(2,1)} %cot_ref.5, f32[1,2048]{1,0:T(1,128)} %bitcast.33, s32[8,128]{1,0:T(8,128)} %bitcast.36), custom_call_target="tpu_custom_call" | custom-call | flops 1073741824 | bytes 10000000 | tf_op jit(solution)/shard_map/pallas_call | solution.py:82
  8.6 12.0 %all-to-all-start.1 = ((bf16[128,8,4096]{2,1,0:T(8,128)(2,1)}), bf16[128,8,4096]{2,1,0:T(8,128)(2,1)}, u32[]{:S(2)}, u32[]{:S(2)}) async-start(bf16[128,8,4096]{2,1,0:T(8,128)(2,1)} %bitcast.27), calls=%async_computation.1 | async-start | bytes 16777216 | tf_op jit(solution)/shard_map/all_to_all | solution.py:43
  20.5 5.3 %shard_map.128 = (f32[128,128]{1,0:T(8,128)}, bf16[1024,1152]{1,0:T(8,128)(2,1)}) custom-call(bf16[128,2048]{1,0:T(8,128)(2,1)} %get-tuple-element.37.normed_ref, bf16[128,2048]{1,0:T(8,128)(2,1)} %cot_ref.5, f32[128,128]{1,0:T(8,128)} %get-tuple-element.38.slot_ref, f32[128,128]{1,0:T(8,128)} %get-tuple-element.39.slot_t_ref, bf16[2048,128]{1,0:T(8,128)(2,1)} %router_ref.3), custom_call_target="tpu_custom_call" | custom-call | flops 1073741824 | bytes 4000000 | tf_op jit(solution)/shard_map/pallas_call | solution.py:137
  25.8 99.9 %all-to-all-done.1 = bf16[128,8,4096]{2,1,0:T(8,128)(2,1)} async-done(((bf16[128,8,4096]{2,1,0:T(8,128)(2,1)}), bf16[128,8,4096]{2,1,0:T(8,128)(2,1)}, u32[]{:S(2)}, u32[]{:S(2)}) %all-to-all-start.1) | async-done | bytes 8388640 | tf_op jit(solution)/shard_map/all_to_all | solution.py:43
  125.7 11.5 %all-to-all-start = ((bf16[128,8,1152]{2,1,0:T(8,128)(2,1)}), bf16[128,8,1152]{2,1,0:T(8,128)(2,1)S(1)}, u32[]{:S(2)}, u32[]{:S(2)}) async-start(bf16[128,8,1152]{2,1,0:T(8,128)(2,1)} %bitcast.30), calls=%async_computation | async-start | bytes 4718592 | tf_op jit(solution)/shard_map/all_to_all | solution.py:43
  137.2 26.0 %shard_map.129 = (bf16[1024,768]{1,0:T(8,128)(2,1)}, bf16[1024,768]{1,0:T(8,128)(2,1)}, bf16[1024,768]{1,0:T(8,128)(2,1)}, f32[128,128]{1,0:T(8,128)}, bf16[1024,2944]{1,0:T(8,128)(2,1)}) custom-call(bf16[1024,4096]{1,0:T(8,128)(2,1)} %bitcast.5.x_ref.c_ref, bf16[1024,4096]{1,0:T(8,128)(2,1)} %bitcast.5.x_ref.c_ref, bf16[2048,768]{1,0:T(8,128)(2,1)} %bitcast.20, ...), custom_call_target="tpu_custom_call" | custom-call | flops 16106127360 | bytes 30000000 | tf_op jit(solution)/shard_map/pallas_call | solution.py:176
  163.2 6.2 %all-to-all-done = bf16[128,8,1152]{2,1,0:T(8,128)(2,1)S(1)} async-done(((bf16[128,8,1152]{2,1,0:T(8,128)(2,1)}), bf16[128,8,1152]{2,1,0:T(8,128)(2,1)S(1)}, u32[]{:S(2)}, u32[]{:S(2)}) %all-to-all-start) | async-done | bytes 2359328 | tf_op jit(solution)/shard_map/all_to_all | solution.py:43
  169.3 0.0 copy-start
  169.3 1.4 copy-done
  170.8 9.8 %shard_map.130 = (bf16[256,4096]{1,0:T(8,128)(2,1)}, bf16[256,768]{1,0:T(8,128)(2,1)}, bf16[256,768]{1,0:T(8,128)(2,1)}, bf16[256,768]{1,0:T(8,128)(2,1)}, f32[128,128]{1,0:T(8,128)}, /*index=5*/bf16[128,128]{1,0:T(8,128)(2,1)}) custom-call(bf16[1024,1152]{1,0:T(8,128)(2,1)} %bitcast.26, f32[128,128]{1,0:T(8,128)} %get-tuple-element.42.q8_ref, ...), custom_call_target="tpu_custom_call" | custom-call | flops 2415919104 | bytes 16000000 | tf_op jit(solution)/shard_map/pallas_call | solution.py:246
  180.6 5.1 %all-to-all-start.2 = ((f32[128,1,128]{2,1,0:T(1,128)}), f32[128,1,128]{2,1,0:T(1,128)S(1)}, u32[]{:S(2)}, u32[]{:S(2)}) async-start(f32[128,1,128]{2,1,0:T(1,128)} %bitcast.32), calls=%async_computation.2 | async-start | bytes 131072 | tf_op jit(solution)/shard_map/all_to_all | solution.py:43
  185.7 9.5 %shard_map.131 = (bf16[1024,2944]{1,0:T(8,128)(2,1)}, bf16[1024,128]{1,0:T(8,128)(2,1)}) custom-call(bf16[256,768]{1,0:T(8,128)(2,1)} %get-tuple-element.45.da_ref.da2_ref, bf16[256,768]{1,0:T(8,128)(2,1)} %get-tuple-element.46.db_ref.db2_ref, bf16[2048,768]{1,0:T(8,128)(2,1)} %bitcast.22, ...), custom_call_target="tpu_custom_call", output_to_operand_aliasing={{0}: (7, {})} | custom-call | flops 1610612736 | bytes 18000000 | tf_op jit(solution)/shard_map/pallas_call | solution.py:323
  195.1 0.1 all-to-all-done.2
  195.2 0.0 copy-start.2
  195.2 0.6 copy-done.2
  195.9 3.2 %shard_map.132 = (bf16[1024,2944]{1,0:T(8,128)(2,1)}, bf16[128,128]{1,0:T(8,128)(2,1)}, f32[128,128]{1,0:T(8,128)}) custom-call(f32[128,128]{1,0:T(8,128)} %bitcast.31, f32[128,128]{1,0:T(8,128)} %get-tuple-element.38.slot_ref, f32[128,128]{1,0:T(8,128)} %get-tuple-element.44.gates_ref, ...), custom_call_target="tpu_custom_call", output_to_operand_aliasing={{0}: (5, {})} | custom-call | flops 67108864 | bytes 2500000 | tf_op jit(solution)/shard_map/pallas_call | solution.py:438
  199.1 10.1 %all-to-all-start.3 = ((bf16[128,8,2944]{2,1,0:T(8,128)(2,1)}), bf16[128,8,2944]{2,1,0:T(8,128)(2,1)}, u32[]{:S(2)}, u32[]{:S(2)}) async-start(bf16[128,8,2944]{2,1,0:T(8,128)(2,1)} %bitcast.19), calls=%async_computation.3 | async-start | bytes 12058624 | tf_op jit(solution)/shard_map/all_to_all | solution.py:43
  209.2 0.8 dynamic_slice.7
  210.0 1.3 dynamic-slice_convert_fusion.refs_3_
  211.2 19.3 %shard_map.134 = (bf16[2048,768]{1,0:T(8,128)(2,1)}, bf16[2048,768]{1,0:T(8,128)(2,1)}, bf16[768,2048]{1,0:T(8,128)(2,1)}) custom-call(bf16[1024,4096]{1,0:T(8,128)(2,1)} %bitcast.5.x_ref.c_ref, bf16[1024,4096]{1,0:T(8,128)(2,1)} %bitcast.5.x_ref.c_ref, bf16[256,4096]{1,0:T(8,128)(2,1)} %get-tuple-element.47.x2_ref.c2_ref, ...), custom_call_target="tpu_custom_call" | custom-call | flops 12079595520 | bytes 36000000 | tf_op jit(solution)/shard_map/pallas_call | solution.py:371
  230.5 0.7 broadcast_in_dim.15.refs_4_
  231.2 52.5 %all-to-all-done.3 = bf16[128,8,2944]{2,1,0:T(8,128)(2,1)} async-done(((bf16[128,8,2944]{2,1,0:T(8,128)(2,1)}), bf16[128,8,2944]{2,1,0:T(8,128)(2,1)}, u32[]{:S(2)}, u32[]{:S(2)}) %all-to-all-start.3) | async-done | bytes 6029344 | tf_op jit(solution)/shard_map/all_to_all | solution.py:43
  283.7 0.6 iota.7.refs_5_
  284.3 2.4 shard_map.135
  286.7 8.2 %all-to-all-start.4 = ((bf16[128,24,128]{2,1,0:T(8,128)(2,1)}), bf16[128,24,128]{2,1,0:T(8,128)(2,1)S(1)}, u32[]{:S(2)}, u32[]{:S(2)}) async-start(bf16[128,24,128]{2,1,0:T(8,128)(2,1)} %shard_map.135), calls=%async_computation.4 | async-start | bytes 1572864 | tf_op jit(solution)/shard_map/all_to_all | solution.py:43
  294.9 6.5 %shard_map.133 = bf16[128,2048]{1,0:T(8,128)(2,1)} custom-call(bf16[1024,2944]{1,0:T(8,128)(2,1)} %bitcast.13.dx_ref.ext_ref.refs_0_.refs_1_.refs_2_, bf16[1024,2944]{1,0:T(8,128)(2,1)} %bitcast.13.dx_ref.ext_ref.refs_0_.refs_1_.refs_2_, f32[128,128]{1,0:T(8,128)} %get-tuple-element.39.slot_t_ref, f32[128,128]{1,0:T(8,128)} %get-tuple-element.53.gk_t_ref, ...), custom_call_target="tpu_custom_call" | custom-call | flops 1073741824 | bytes 9000000 | tf_op jit(solution)/shard_map/pallas_call | solution.py:523
  301.3 10.0 %all-to-all-done.4.sums_ref = bf16[128,24,128]{2,1,0:T(8,128)(2,1)S(1)} async-done(((bf16[128,24,128]{2,1,0:T(8,128)(2,1)}), bf16[128,24,128]{2,1,0:T(8,128)(2,1)S(1)}, u32[]{:S(2)}, u32[]{:S(2)}) %all-to-all-start.4) | async-done | bytes 786464 | tf_op jit(solution)/shard_map/all_to_all | solution.py:43
  311.3 0.0 copy-start.1
  311.3 0.9 copy-done.1
  312.2 2.2 shard_map.136
  (1 shorter events, 0.0 us)
Async XLA Ops:
  8.6 117.2 %all-to-all-start.1 = ((bf16[128,8,4096]{2,1,0:T(8,128)(2,1)}), bf16[128,8,4096]{2,1,0:T(8,128)(2,1)}, u32[]{:S(2)}, u32[]{:S(2)}) async-start(bf16[128,8,4096]{2,1,0:T(8,128)(2,1)} %bitcast.27), calls=%async_computation.1 | async-start | bytes 16777216 | tf_op jit(solution)/shard_map/all_to_all | solution.py:43
  125.7 43.6 %all-to-all-start = ((bf16[128,8,1152]{2,1,0:T(8,128)(2,1)}), bf16[128,8,1152]{2,1,0:T(8,128)(2,1)S(1)}, u32[]{:S(2)}, u32[]{:S(2)}) async-start(bf16[128,8,1152]{2,1,0:T(8,128)(2,1)} %bitcast.30), calls=%async_computation | async-start | bytes 4718592 | tf_op jit(solution)/shard_map/all_to_all | solution.py:43
  169.3 1.4 copy-start
  180.6 14.7 %all-to-all-start.2 = ((f32[128,1,128]{2,1,0:T(1,128)}), f32[128,1,128]{2,1,0:T(1,128)S(1)}, u32[]{:S(2)}, u32[]{:S(2)}) async-start(f32[128,1,128]{2,1,0:T(1,128)} %bitcast.32), calls=%async_computation.2 | async-start | bytes 131072 | tf_op jit(solution)/shard_map/all_to_all | solution.py:43
  195.2 0.6 copy-start.2
  199.1 84.6 %all-to-all-start.3 = ((bf16[128,8,2944]{2,1,0:T(8,128)(2,1)}), bf16[128,8,2944]{2,1,0:T(8,128)(2,1)}, u32[]{:S(2)}, u32[]{:S(2)}) async-start(bf16[128,8,2944]{2,1,0:T(8,128)(2,1)} %bitcast.19), calls=%async_computation.3 | async-start | bytes 12058624 | tf_op jit(solution)/shard_map/all_to_all | solution.py:43
  286.7 24.6 %all-to-all-start.4 = ((bf16[128,24,128]{2,1,0:T(8,128)(2,1)}), bf16[128,24,128]{2,1,0:T(8,128)(2,1)S(1)}, u32[]{:S(2)}, u32[]{:S(2)}) async-start(bf16[128,24,128]{2,1,0:T(8,128)(2,1)} %shard_map.135), calls=%async_computation.4 | async-start | bytes 1572864 | tf_op jit(solution)/shard_map/all_to_all | solution.py:43
  311.3 0.9 copy-start.1

commit v3 on v2

v3 whole, which is shorter than its diff:
```python
import functools

import jax
import jax.numpy as jnp
from jax import lax
from jax.experimental import pallas as pl
from jax.experimental.pallas import tpu as pltpu
from jax.sharding import PartitionSpec as P

norm_eps = 1e-06
HI = 8
SUB = 8
MSG = 128
TILE = 256
AXES = ("seq", "exp")
bf16, f32 = jnp.bfloat16, jnp.float32


def params(mib=60):
    return pltpu.CompilerParams(vmem_limit_bytes=mib * 1024 * 1024)


def whole(shape, **kw):
    return pl.BlockSpec(shape, lambda *_: (0,) * len(shape), **kw)


def iota(shape, dim):
    return lax.broadcasted_iota(jnp.int32, shape, dim)


def mm(a, b):
    return jnp.dot(a, b, preferred_element_type=f32)


def mm_nt(a, b):
    return lax.dot_general(a, b, (((1,), (1,)), ((), ())), preferred_element_type=f32)


def mm_tn(a, b):
    return lax.dot_general(a, b, (((0,), (0,)), ((), ())), preferred_element_type=f32)


def exchange(x):
    return lax.all_to_all(x, AXES, split_axis=0, concat_axis=0, tiled=True)


def slots_chosen(slot_t):
    experts, tokens = slot_t.shape
    which = iota((experts, HI, tokens), 1).astype(f32)
    chosen = jnp.where(slot_t[:, None, :] == which, 1.0, 0.0)
    return chosen.reshape(experts * HI, tokens).astype(bf16)


def quarter_chosen(slot_t, j):
    experts, tokens = slot_t.shape
    row = iota((experts, SUB, tokens), 1)
    chosen = (slot_t[:, None, :] == (HI + row // 4).astype(f32)) & (row % 4 == j)
    return jnp.where(chosen, 1.0, 0.0).reshape(experts * SUB, tokens).astype(bf16)


def front_kernel(hid_ref, gain_ref, ids_ref, out_ref, normed_ref, slot_ref, slot_t_ref, tiles, p8):
    step = pl.program_id(0)
    tokens = hid_ref.shape[0]
    experts = slot_ref.shape[1]
    tile = tiles.shape[2]

    @pl.when(step == 0)
    def _():
        h = hid_ref[...].astype(f32)
        scale = lax.rsqrt(jnp.mean(h * h, axis=1, keepdims=True) + norm_eps)
        normed = (h * scale * gain_ref[...]).astype(bf16)
        normed_ref[...] = normed
        for j in range(4):
            tiles[j] = normed[:, j * tile : (j + 1) * tile]
        ids = ids_ref[...]
        expert = iota((experts, tokens), 0)
        member = jnp.zeros((experts, tokens), f32)
        for k in range(ids.shape[0]):
            member += jnp.where(ids[k : k + 1, :] == expert, 1.0, 0.0)
        earlier = jnp.where(iota((tokens, tokens), 0) < iota((tokens, tokens), 1), 1.0, 0.0)
        position = mm(member.astype(bf16), earlier.astype(bf16))
        slot_t = jnp.where(member > 0.0, position, 99.0)
        slot_ref[...] = slot_t.T
        slot_t_ref[...] = slot_t
        p8[...] = slots_chosen(slot_t)

    @pl.when(step < 4)
    def _():
        out_ref[...] = mm(p8[...], tiles[jnp.minimum(step, 3)]).astype(bf16)

    @pl.when(step == 4)
    def _():
        slot_t = slot_t_ref[...]
        total = mm(quarter_chosen(slot_t, 0), tiles[0])
        for j in range(1, 4):
            total = total + mm(quarter_chosen(slot_t, j), tiles[j])
        out_ref[...] = total.astype(bf16)


def front(hidden, gain, ids, experts):
    tokens, width = hidden.shape
    tile = width // 4
    return pl.pallas_call(
        front_kernel,
        grid=(5,),
        in_specs=[whole((tokens, width)), whole((1, width)), whole(ids.shape)],
        out_specs=[
            pl.BlockSpec((experts * HI, tile), lambda i: (0, i)),
            whole((tokens, width)),
            whole((tokens, experts)),
            whole((experts, tokens)),
        ],
        out_shape=[
            jax.ShapeDtypeStruct((experts * HI, width + tile), bf16),
            jax.ShapeDtypeStruct((tokens, width), bf16),
            jax.ShapeDtypeStruct((tokens, experts), f32),
            jax.ShapeDtypeStruct((experts, tokens), f32),
        ],
        scratch_shapes=[pltpu.VMEM((4, tokens, tile), bf16), pltpu.VMEM((experts * HI, tokens), bf16)],
        compiler_params=params(),
        cost_estimate=pl.CostEstimate(flops=4 * experts * HI * tokens * width, bytes_accessed=7_000_000, transcendentals=tokens),
    )(hidden, gain, ids)


def second_kernel(normed_ref, cot_ref, slot_ref, slot_t_ref, router_ref, gates_ref, out_ref, tiles, p8, p2, meta):
    step, last = pl.program_id(0), pl.num_programs(0) - 1
    experts = slot_ref.shape[1]
    count = tiles.shape[0]
    per = count // 4

    @pl.when(step == 0)
    def _():
        logits = mm(normed_ref[...], router_ref[...])
        weights = jnp.where(slot_ref[...] < 50.0, jnp.exp(logits), 0.0)
        gates = weights / jnp.sum(weights, axis=1, keepdims=True)
        gates_ref[...] = gates
        slot_t = slot_t_ref[...]
        gates_t = gates.T
        lane = iota((experts, MSG), 1)
        message = jnp.where(lane == 10, jnp.sum(jnp.where(slot_t < 50.0, 1.0, 0.0), axis=1, keepdims=True), 0.0)
        for s in range(10):
            message = message + jnp.where(
                lane == s, jnp.sum(jnp.where(slot_t == s, gates_t, 0.0), axis=1, keepdims=True), 0.0
            )
        sub = iota((experts, SUB, MSG), 1)
        meta[...] = jnp.where(sub == 0, message[:, None, :], 0.0).reshape(experts * SUB, MSG).astype(bf16)
        for j in range(count):
            tiles[j] = cot_ref[:, j * MSG : (j + 1) * MSG]
        p8[...] = slots_chosen(slot_t)
        for j in range(4):
            p2[j] = quarter_chosen(slot_t, j)

    @pl.when(step < count)
    def _():
        out_ref[...] = mm(p8[...], tiles[jnp.minimum(step, count - 1)]).astype(bf16)

    @pl.when((step >= count) & (step < last))
    def _():
        at = jnp.clip(step - count, 0, per - 1)
        total = mm(p2[0], tiles[at])
        for j in range(1, 4):
            total = total + mm(p2[j], tiles[j * per + at])
        out_ref[...] = total.astype(bf16)

    @pl.when(step == last)
    def _():
        out_ref[...] = meta[...]


def second(normed, cotangent, slot, slot_t, router):
    tokens, width = normed.shape
    experts = slot.shape[1]
    count = width // MSG
    steps = count + count // 4 + 1
    n_rows = experts * HI
    return pl.pallas_call(
        second_kernel,
        grid=(steps,),
        in_specs=[whole(normed.shape), whole(cotangent.shape), whole(slot.shape), whole(slot_t.shape), whole(router.shape)],
        out_specs=[whole((tokens, experts)), pl.BlockSpec((n_rows, MSG), lambda i: (0, i))],
        out_shape=[
            jax.ShapeDtypeStruct((tokens, experts), f32),
            jax.ShapeDtypeStruct((n_rows, steps * MSG), bf16),
        ],
        scratch_shapes=[
            pltpu.VMEM((count, tokens, MSG), bf16),
            pltpu.VMEM((n_rows, tokens), bf16),
            pltpu.VMEM((4, n_rows, tokens), bf16),
            pltpu.VMEM((n_rows, MSG), bf16),
        ],
        compiler_params=params(),
        cost_estimate=pl.CostEstimate(flops=4 * n_rows * tokens * width, bytes_accessed=8_000_000, transcendentals=tokens * experts),
    )(normed, cotangent, slot, slot_t, router)


def turn_kernel(wg_ref, wu_ref, wd_ref, both_ref, wd_t_ref):
    both_ref[: wg_ref.shape[1]] = wg_ref[...].T
    both_ref[wg_ref.shape[1] :] = wu_ref[...].T
    wd_t_ref[...] = wd_ref[...].T


def turn(wg, wu, wd):
    width, hid = wg.shape
    tile = min(TILE, hid)
    tall, wide = pl.BlockSpec((width, tile), lambda i: (0, i)), pl.BlockSpec((tile, width), lambda i: (i, 0))
    return pl.pallas_call(
        turn_kernel,
        grid=(hid // tile,),
        in_specs=[tall, tall, wide],
        out_specs=[pl.BlockSpec((2 * tile, width), lambda i: (i, 0)), tall],
        out_shape=[jax.ShapeDtypeStruct((2 * hid, width), bf16), jax.ShapeDtypeStruct((width, hid), bf16)],
        compiler_params=params(),
        cost_estimate=pl.CostEstimate(flops=3 * wg.size, bytes_accessed=19_000_000, transcendentals=0),
    )(wg, wu, wd)


def gather_quarters(ext_ref, target):
    n_rows, quarter = ext_ref.shape
    sources = n_rows // SUB
    chunk = min(32, sources)
    out_rows, in_rows = 2 * chunk, SUB * chunk
    index, column = iota((4 * out_rows, in_rows), 0), iota((4 * out_rows, in_rows), 1)
    pick = jnp.where(column == 4 * (index % out_rows) + index // out_rows, 1.0, 0.0).astype(bf16)
    for j in range(sources // chunk):
        part = mm(pick, ext_ref[j * in_rows : (j + 1) * in_rows, :]).astype(bf16)
        for q in range(4):
            target[j * out_rows : (j + 1) * out_rows, q * quarter : (q + 1) * quarter] = part[q * out_rows : (q + 1) * out_rows]


def x_kernel(x_ref, ext_ref, wg_ref, wu_ref, act_ref, fa_ref, fb_ref, x2_ref, held):
    step = pl.program_id(0)

    @pl.when(step < 4)
    def _():
        held[...] = x_ref[...]

    @pl.when(step == 4)
    def _():
        gather_quarters(ext_ref, held)
        x2_ref[...] = held[...]

    a = mm(held[...], wg_ref[...])
    b = mm(held[...], wu_ref[...])
    s = jax.nn.sigmoid(a)
    act_ref[...] = (a * s * b).astype(bf16)
    fa_ref[...] = (b * s * (1.0 + a * (1.0 - s))).astype(bf16)
    fb_ref[...] = (a * s).astype(bf16)


def x_side(r1, wg, wu):
    width, hid = wg.shape
    main = r1.shape[0]
    block = main // 4
    total = 5 * block
    out = pl.BlockSpec((block, hid), lambda i: (i, 0))
    return pl.pallas_call(
        x_kernel,
        grid=(5,),
        in_specs=[
            pl.BlockSpec((block, width), lambda i: (jnp.minimum(i, 3), 0)),
            pl.BlockSpec((main, width // 4), lambda i: (0, 4)),
            whole(wg.shape),
            whole(wu.shape),
        ],
        out_specs=[out, out, out, whole((block, width))],
        out_shape=[
            jax.ShapeDtypeStruct((total, hid), bf16),
            jax.ShapeDtypeStruct((total, hid), bf16),
            jax.ShapeDtypeStruct((total, hid), bf16),
            jax.ShapeDtypeStruct((block, width), bf16),
        ],
        scratch_shapes=[pltpu.VMEM((block, width), bf16)],
        compiler_params=params(),
        cost_estimate=pl.CostEstimate(flops=4 * total * wg.size, bytes_accessed=24_000_000, transcendentals=total * hid),
    )(r1, r1, wg, wu)


def folded(product):
    total = product[:, :MSG]
    for j in range(1, product.shape[1] // MSG):
        total = total + product[:, j * MSG : (j + 1) * MSG]
    return total


def c_kernel(limit, c_ref, ext_ref, meta_ref, wd_t_ref, act_ref, fa_ref, fb_ref, dab_ref, c2_ref, msg_ref, scale_ref, q8, q2):
    step, last = pl.program_id(0), pl.num_programs(0) - 1
    sources = msg_ref.shape[0]
    main, tail = c_ref.shape[0], c2_ref.shape[0]
    tile = act_ref.shape[1]

    @pl.when(step == 0)
    def _():
        gather_quarters(ext_ref, c2_ref)
        q8[...] = jnp.zeros_like(q8)
        q2[...] = jnp.zeros_like(q2)

    for rows, c, total in ((slice(0, main), c_ref, q8), (slice(main, main + tail), c2_ref, q2)):
        u = mm(c[...], wd_t_ref[...])
        total[...] += folded(act_ref[rows].astype(f32) * u)
        dab_ref[rows, :tile] = (u * fa_ref[rows].astype(f32)).astype(bf16)
        dab_ref[rows, tile:] = (u * fb_ref[rows].astype(f32)).astype(bf16)

    @pl.when(step == last)
    def _():
        lane, which = iota((sources, HI, MSG), 2), iota((sources, HI, MSG), 1)
        q = jnp.sum(q8[...], axis=1, keepdims=True)
        q_rows = jnp.sum(jnp.where(lane == which, q.reshape(sources, HI, 1), 0.0), axis=1).astype(bf16).astype(f32)
        q = jnp.sum(q2[...], axis=1, keepdims=True)
        parity = iota((tail, MSG), 0) % 2
        spread = jnp.where(iota((tail, MSG), 1) == HI + parity, q, 0.0).astype(bf16)
        gather = jnp.where(iota((sources, tail), 1) // 2 == iota((sources, tail), 0), 1.0, 0.0).astype(bf16)
        q_rows = q_rows + mm(gather, spread)
        meta = jnp.sum(meta_ref[...].astype(f32).reshape(sources, SUB, MSG), axis=1)
        lane = iota((sources, MSG), 1)
        count = jnp.sum(jnp.where(lane == 10, meta, 0.0), axis=1, keepdims=True)
        lower = jnp.where(iota((sources, sources), 1) < iota((sources, sources), 0), 1.0, 0.0).astype(bf16)
        offset = mm(lower, jnp.broadcast_to(count, (sources, MSG)).astype(bf16))
        slot = jnp.where(lane < 10, lane, lane - 10).astype(f32)
        kept = (slot < count) & (offset + slot < limit) & (lane < 20)
        msg_ref[...] = jnp.where(kept, jnp.where(lane < 10, q_rows, 1.0), 0.0)
        scale_ref[...] = jnp.where(kept & (lane < 10), meta, 0.0).astype(bf16)


def c_side(r2, wd_t, act, fa, fb, limit):
    width, hid = wd_t.shape
    main = r2.shape[0]
    sources, tail = main // SUB, main // 4
    total = main + tail
    tile = min(TILE, hid)

    def columns(n_rows, n_columns):
        return pl.BlockSpec((n_rows, n_columns), lambda i: (0, i))

    return pl.pallas_call(
        functools.partial(c_kernel, float(limit)),
        grid=(hid // tile,),
        in_specs=[
            whole((main, width)),
            pl.BlockSpec((main, width // 4), lambda i: (0, 4)),
            pl.BlockSpec((main, MSG), lambda i: (0, (width + width // 4) // MSG)),
            columns(width, tile),
            columns(total, tile),
            columns(total, tile),
            columns(total, tile),
        ],
        out_specs=[columns(total, 2 * tile), whole((tail, width)), whole((sources, MSG)), whole((sources, MSG))],
        out_shape=[
            jax.ShapeDtypeStruct((total, 2 * hid), bf16),
            jax.ShapeDtypeStruct((tail, width), bf16),
            jax.ShapeDtypeStruct((sources, MSG), f32),
            jax.ShapeDtypeStruct((sources, MSG), bf16),
        ],
        scratch_shapes=[pltpu.VMEM((main, MSG), f32), pltpu.VMEM((tail, MSG), f32)],
        compiler_params=params(),
        cost_estimate=pl.CostEstimate(flops=2 * total * wd_t.size, bytes_accessed=20_000_000, transcendentals=0),
    )(r2, r2, r2, wd_t, act, fa, fb)


def column_of(table):
    sources = table.shape[0]
    lane, which = iota((sources, HI, MSG), 2), iota((sources, HI, MSG), 1)
    spread = jnp.where(lane == which, table[:, None, :], 0.0)
    return jnp.sum(spread.reshape(sources * HI, MSG), axis=1, keepdims=True)


def tail_column_of(table):
    sources = table.shape[0]
    total = 2 * sources
    scatter = jnp.where(iota((total, sources), 0) // 2 == iota((total, sources), 1), 1.0, 0.0).astype(bf16)
    lane = HI + iota((total, MSG), 0) % 2
    return jnp.sum(jnp.where(iota((total, MSG), 1) == lane, mm(scatter, table), 0.0), axis=1, keepdims=True)


def dx_kernel(dab_ref, both_ref, x_ref, x2_ref, scale_ref, out_ref, part_ref, ext, s8, s2):
    step = pl.program_id(0)
    sources = scale_ref.shape[0]
    main, quarter = out_ref.shape

    @pl.when(step == 0)
    def _():
        table = scale_ref[...]
        s8[...] = jnp.broadcast_to(column_of(table.astype(f32)), s8.shape)
        s2[...] = jnp.broadcast_to(tail_column_of(table), s2.shape)
        ext[...] = jnp.zeros_like(ext)

    @pl.when(step < 4)
    def _():
        dx = mm(dab_ref[...], both_ref[...])
        rounded = dx.astype(bf16)
        out_ref[...] = rounded[:main]
        chunk = min(32, sources)
        n_rows = SUB * chunk
        pick = jnp.where(iota((n_rows, 2 * chunk), 0) == 4 * iota((n_rows, 2 * chunk), 1) + step, 1.0, 0.0).astype(bf16)
        for j in range(sources // chunk):
            tail = rounded[main + j * 2 * chunk : main + (j + 1) * 2 * chunk]
            ext[j * n_rows : (j + 1) * n_rows, :] += mm(pick, tail).astype(bf16)
        part = jnp.sum(x_ref[...].astype(f32) * dx[:main] * s8[:, 0:1], axis=0, keepdims=True)
        part = part + jnp.sum(x2_ref[...].astype(f32) * dx[main:] * s2[:, 0:1], axis=0, keepdims=True)
        column = jnp.concatenate(
            [jnp.broadcast_to(part[:, j : j + MSG], (MSG, MSG)).T for j in range(0, quarter, MSG)], axis=0
        )
        dests = part_ref.shape[0] // SUB
        groups = quarter // dests // SUB
        column = column.reshape(dests, groups, SUB, MSG)
        lane = iota((dests, SUB, MSG), 2)
        spread = jnp.zeros((dests, SUB, MSG), f32)
        for g in range(groups):
            spread = jnp.where(lane == g, column[:, g], spread)
        part_ref[...] = spread.reshape(dests * SUB, MSG).astype(bf16)

    @pl.when(step == 4)
    def _():
        out_ref[...] = ext[...]


def dx_side(dab, both, r1, x2, scale, extra):
    sources = scale.shape[0]
    twice, width = both.shape
    quarter = width // 4
    main, total = sources * HI, 2 * sources

    def columns(n_rows):
        return pl.BlockSpec((n_rows, quarter), lambda i: (0, jnp.minimum(i, 3)))

    return pl.pallas_call(
        dx_kernel,
        grid=(5,),
        in_specs=[whole(dab.shape), columns(twice), columns(main), columns(total), whole(scale.shape)],
        out_specs=[
            pl.BlockSpec((main, quarter), lambda i: (0, i)),
            pl.BlockSpec((main // 4, MSG), lambda i: (jnp.minimum(i, 3), 0)),
        ],
        out_shape=[jax.ShapeDtypeStruct((main, width + extra), bf16), jax.ShapeDtypeStruct((main, MSG), bf16)],
        scratch_shapes=[pltpu.VMEM((main, quarter), bf16), pltpu.VMEM((main, MSG), f32), pltpu.VMEM((total, MSG), f32)],
        compiler_params=params(),
        cost_estimate=pl.CostEstimate(flops=2 * (main + total) * both.size, bytes_accessed=20_000_000, transcendentals=0),
    )(dab, both, r1, x2, scale)


def weights_kernel(x_ref, c_ref, x2_ref, c2_ref, act_ref, dab_ref, scale_ref, dwg_ref, dwu_ref, dwd_ref, act_s, dab_s):
    main = x_ref.shape[0]
    hid = act_ref.shape[1]
    tile = min(TILE, hid)

    @pl.when(pl.program_id(0) == 0)
    def _():
        table = scale_ref[...]
        column, tail_column = column_of(table.astype(f32)), tail_column_of(table)
        for source, target in ((act_ref, act_s), (dab_ref, dab_s)):
            target[:main] = (source[:main].astype(f32) * column).astype(bf16)
            target[main:] = (source[main:].astype(f32) * tail_column).astype(bf16)

    both = (mm_tn(x_ref[...], dab_s[:main]) + mm_tn(x2_ref[...], dab_s[main:])).astype(bf16)
    for j in range(hid // tile):
        dwg_ref[:, j * tile : (j + 1) * tile] = both[:, 2 * j * tile : (2 * j + 1) * tile]
        dwu_ref[:, j * tile : (j + 1) * tile] = both[:, (2 * j + 1) * tile : (2 * j + 2) * tile]
    dwd_ref[...] = (mm_tn(act_s[:main], c_ref[...]) + mm_tn(act_s[main:], c2_ref[...])).astype(bf16)


def weight_grads(r1, r2, x2, c2, act, dab, scale):
    total, hid = act.shape
    main, width = r1.shape[0], x2.shape[1]
    tile = min(256, width)
    steps = width // tile

    def columns(n_rows):
        return pl.BlockSpec((n_rows, tile), lambda i: (0, i))

    return pl.pallas_call(
        weights_kernel,
        grid=(steps,),
        in_specs=[columns(main), columns(main), columns(total - main), columns(total - main)]
        + [whole(act.shape), whole(dab.shape), whole(scale.shape)],
        out_specs=[pl.BlockSpec((tile, hid), lambda i: (i, 0)), pl.BlockSpec((tile, hid), lambda i: (i, 0)), columns(hid)],
        out_shape=[
            jax.ShapeDtypeStruct((width, hid), bf16),
            jax.ShapeDtypeStruct((width, hid), bf16),
            jax.ShapeDtypeStruct((hid, width), bf16),
        ],
        scratch_shapes=[pltpu.VMEM(act.shape, bf16), pltpu.VMEM(dab.shape, bf16)],
        compiler_params=params(),
        cost_estimate=pl.CostEstimate(flops=6 * total * width * hid, bytes_accessed=36_000_000, transcendentals=0),
    )(r1, r2, x2, c2, act, dab, scale)


def home_kernel(q_ref, slot_ref, gates_ref, normed_ref, part_ref, _, back_ref, dl_ref, gk_t_ref, router_part):
    step, last = pl.program_id(0), pl.num_programs(0) - 1
    experts = q_ref.shape[0]

    @pl.when(step == 0)
    def _():
        q_t = q_ref[...].T
        slot, gates = slot_ref[...], gates_ref[...]
        dgate = jnp.zeros_like(gates)
        kept = jnp.zeros_like(gates)
        for s in range(10):
            here = slot == s
            dgate = dgate + jnp.where(here, q_t[s : s + 1, :], 0.0)
            kept = kept + jnp.where(here, q_t[10 + s : 11 + s, :], 0.0)
        dsel = gates * (dgate - jnp.sum(gates * dgate, axis=1, keepdims=True))
        dl = dsel.astype(bf16)
        dl_ref[...] = dl
        gk_t_ref[...] = (gates.astype(bf16).astype(f32) * kept).T
        if experts < MSG:
            dl = jnp.concatenate([dl, jnp.zeros((dl.shape[0], MSG - experts), bf16)], axis=1)
        groups = router_part.shape[0]
        partial = mm_tn(normed_ref[...], dl).reshape(experts, groups, SUB, MSG)
        for g in range(groups):
            router_part[g] = partial[:, g].reshape(experts * SUB, MSG).astype(bf16)

    @pl.when(step < last)
    def _():
        back_ref[...] = router_part[jnp.minimum(step, router_part.shape[0] - 1)]

    @pl.when(step == last)
    def _():
        back_ref[...] = part_ref[...]


def home(q, slot, gates, normed, part, back):
    tokens, experts = slot.shape
    width = normed.shape[1]
    groups = width // experts // SUB
    first = (width + width // 4) // MSG
    return pl.pallas_call(
        home_kernel,
        grid=(groups + 1,),
        in_specs=[whole(q.shape), whole(slot.shape), whole(gates.shape), whole(normed.shape), whole(part.shape), pl.BlockSpec(memory_space=pl.ANY)],
        out_specs=[pl.BlockSpec((experts * SUB, MSG), lambda i: (0, first + i)), whole((tokens, experts)), whole((experts, tokens))],
        out_shape=[
            jax.ShapeDtypeStruct(back.shape, bf16),
            jax.ShapeDtypeStruct((tokens, experts), bf16),
            jax.ShapeDtypeStruct((experts, tokens), f32),
        ],
        scratch_shapes=[pltpu.VMEM((groups, experts * SUB, MSG), bf16)],
        input_output_aliases={5: 0},
        compiler_params=params(),
        cost_estimate=pl.CostEstimate(flops=2 * tokens * MSG * width, bytes_accessed=2_500_000, transcendentals=0),
    )(q, slot, gates, normed, part, back)


def sums_kernel(*refs):
    *parts, gain_ref, router_ref, gain_rows_ref, target_ref, out_ref = refs
    copies, n_rows, _ = out_ref.shape
    target = target_ref[...]
    row = iota(target.shape, 0)
    gain_parts = jnp.sum(gain_ref[...].astype(f32).reshape(copies, SUB, MSG), axis=0)
    pieces = []
    placed = jnp.zeros(target.shape, f32)
    for g, ref in enumerate(parts):
        piece = jnp.sum(ref[...].astype(f32).reshape(copies, SUB, MSG), axis=0)
        pieces.append(piece)
        own = slice(g * SUB, (g + 1) * SUB)
        value = gain_parts[:, g : g + 1] + jnp.sum(router_ref[own] * piece, axis=1, keepdims=True)
        placed = jnp.where(target == g * SUB + row, value / gain_rows_ref[own], placed)
    message = jnp.concatenate(pieces + [placed], axis=0)
    out_ref[...] = jnp.broadcast_to(message[None], out_ref.shape).astype(bf16)


def sums(rd, router_rows, gain_rows, target, experts, width):
    groups = width // experts // SUB
    first = (width + width // 4) // MSG
    block = (experts * SUB, MSG)
    specs = [pl.BlockSpec(block, functools.partial(lambda g, i: (0, first + g), g)) for g in range(groups + 1)]
    return pl.pallas_call(
        sums_kernel,
        grid=(1,),
        in_specs=specs + [whole(router_rows.shape), whole(gain_rows.shape), whole(target.shape)],
        out_specs=whole((experts, (groups + 1) * SUB, MSG)),
        out_shape=jax.ShapeDtypeStruct((experts, (groups + 1) * SUB, MSG), bf16),
        compiler_params=params(),
        cost_estimate=pl.CostEstimate(flops=experts * SUB * MSG * 8, bytes_accessed=2_000_000, transcendentals=0),
    )(*[rd] * (groups + 1), router_rows, gain_rows, target)


def final_kernel(dx_ref, ext_ref, slot_t_ref, gk_t_ref, dl_ref, router_ref, gain_ref, hid_ref, cot_ref, dh_ref, total):
    step, last = pl.program_id(0), pl.num_programs(0) - 1
    chunk, tokens = slot_t_ref.shape
    n_rows = chunk * SUB
    quarter = ext_ref.shape[1]
    slot, gk = slot_t_ref[...][:, None, :], gk_t_ref[...][:, None, :]
    which = iota((chunk, SUB, tokens), 1)

    def weights(mask):
        return jnp.where(mask, gk, 0.0).reshape(n_rows, tokens).astype(bf16)

    @pl.when(step == 0)
    def _():
        total[...] = mm_nt(dl_ref[...], router_ref[...])

    total[...] += mm_tn(weights(slot == which.astype(f32)), dx_ref[...])
    in_tail = slot == (HI + which // 4).astype(f32)
    for j in range(4):
        total[:, j * quarter : (j + 1) * quarter] += mm_tn(weights(in_tail & (which % 4 == j)), ext_ref[...])

    @pl.when(step == last)
    def _():
        h = hid_ref[...].astype(f32)
        scale = lax.rsqrt(jnp.mean(h * h, axis=1, keepdims=True) + norm_eps)
        gained = gain_ref[...] * total[...]
        mean = jnp.mean(gained * h, axis=1, keepdims=True)
        dh_ref[...] = (cot_ref[...].astype(f32) + scale * gained - h * (scale * scale * scale) * mean).astype(bf16)


def final(rd, slot_t, gk_t, dl, router, gain, hidden, cotangent):
    experts, tokens = slot_t.shape
    width = hidden.shape[1]
    chunk = min(32, experts)
    steps = experts // chunk
    return pl.pallas_call(
        final_kernel,
        grid=(steps,),
        in_specs=[
            pl.BlockSpec((chunk * SUB, width), lambda i: (i, 0)),
            pl.BlockSpec((chunk * SUB, width // 4), lambda i: (i, 4)),
            pl.BlockSpec((chunk, tokens), lambda i: (i, 0)),
            pl.BlockSpec((chunk, tokens), lambda i: (i, 0)),
            whole(dl.shape),
            whole(router.shape),
            whole((1, width)),
            whole((tokens, width)),
            whole((tokens, width)),
        ],
        out_specs=whole((tokens, width)),
        out_shape=jax.ShapeDtypeStruct((tokens, width), bf16),
        scratch_shapes=[pltpu.VMEM((tokens, width), f32)],
        compiler_params=params(),
        cost_estimate=pl.CostEstimate(flops=4 * experts * SUB * tokens * width, bytes_accessed=9_000_000, transcendentals=tokens),
    )(rd, rd, slot_t, gk_t, dl, router, gain, hidden, cotangent)


def place_kernel(sums_ref, router_ref, gain_ref):
    experts, n_rows, _ = sums_ref.shape
    rows_each = n_rows - SUB
    received = sums_ref[...].astype(f32)
    router_ref[...] = received[:, :rows_each].reshape(experts * rows_each, MSG)[:, : router_ref.shape[1]]
    gain_ref[...] = jnp.sum(received[:, rows_each:].reshape(gain_ref.shape[0], -1, MSG), axis=1)


def place(received, width, experts):
    return pl.pallas_call(
        place_kernel,
        out_shape=[jax.ShapeDtypeStruct((width, experts), f32), jax.ShapeDtypeStruct((width // MSG, MSG), f32)],
        compiler_params=params(16),
        cost_estimate=pl.CostEstimate(flops=received.size, bytes_accessed=2_000_000, transcendentals=0),
    )(received)


def on_device(hidden, cotangent, norm_gain, router, w_gate, w_up, w_down, expert_ids):
    tokens, width = hidden.shape
    top = expert_ids.shape[1]
    experts = router.shape[1]
    quarter = width // 4
    limit = tokens * top
    gain = norm_gain.reshape(1, width)
    wg, wu, wd = w_gate[0], w_up[0], w_down[0]
    own = width // experts
    extra = quarter + (own // SUB + 1) * MSG

    me = lax.axis_index(AXES)
    router_rows = lax.dynamic_slice_in_dim(router, me * own, own, 0).astype(f32)
    router_rows = jnp.pad(router_rows, ((0, 0), (0, MSG - experts)))
    gain_rows = jnp.broadcast_to(lax.dynamic_slice_in_dim(norm_gain, me * own, own, 0)[:, None], (own, MSG))
    target = lax.broadcasted_iota(jnp.int32, (SUB, MSG), 1) - (me % (MSG // own)) * own

    s1, normed, slot, slot_t = front(hidden, gain, expert_ids.T, experts)
    r1 = exchange(s1.reshape(experts, HI, width + quarter)).reshape(experts * HI, width + quarter)
    gates, s2 = second(normed, cotangent, slot, slot_t, router)
    both, wd_t = turn(wg, wu, wd)
    r2 = exchange(s2.reshape(experts, SUB, width + quarter + MSG)).reshape(experts * SUB, width + quarter + MSG)
    act, fa, fb, x2 = x_side(r1, wg, wu)
    dab, c2, q_msg, scale = c_side(r2, wd_t, act, fa, fb, limit)
    q_home = exchange(q_msg.reshape(experts, 1, MSG)).reshape(experts, MSG)
    back, part = dx_side(dab, both, r1, x2, scale, extra)
    back, dl, gk_t = home(q_home, slot, gates, normed, part, back)
    scale, dl = lax.optimization_barrier((scale, dl))
    d_wgate, d_wup, d_wdown = weight_grads(r1, r2, x2, c2, act, dab, scale)
    rd = exchange(back.reshape(experts, HI, width + extra)).reshape(experts * HI, width + extra)
    d_wgate, gain_rows, router_rows, target = lax.optimization_barrier((d_wgate, gain_rows, router_rows, target))
    message = sums(rd, router_rows, gain_rows, target, experts, width)
    received = exchange(message)
    d_hidden = final(rd, slot_t, gk_t, dl, router, gain, hidden, cotangent)
    d_router, d_gain = place(received, width, experts)
    return (d_hidden, d_gain.reshape(width), d_router, d_wgate[None], d_wup[None], d_wdown[None])


def solution(mesh):
    rows_spec, stack_spec = P(AXES, None), P(AXES, None, None)
    in_specs = (rows_spec, rows_spec, P(), P(), stack_spec, stack_spec, stack_spec, rows_spec)
    out_specs = (rows_spec, P(), P(), stack_spec, stack_spec, stack_spec)
    return jax.shard_map(on_device, mesh=mesh, in_specs=in_specs, out_specs=out_specs, check_vma=False)
```

time: 315 us -> 309 us (0.981)
  Pallas kernels: 92 us -> 104 us
  waiting for transfers between devices: 169 us -> 157 us
  starting transfers between devices: 46.8 us -> 42.2 us
    pallas_call x6 -> x7, Pallas kernels: 77.8 us -> 90.6 us  [the longest x1 19.1 us: weight_grads(): pl.pallas_call(weights_kernel, grid=(steps,), in_specs=[columns(main), co...]
    all_to_all x5, waiting for transfers between devices: 169 us -> 157 us  [exchange(): return lax.all_to_all(x, AXES, split_axis=0, concat_axis=0, tiled=True)]
    all_to_all x5, starting transfers between devices: 46.8 us -> 42.2 us  [exchange(): return lax.all_to_all(x, AXES, split_axis=0, concat_axis=0, tiled=True)]
  transfers between devices with their start and end apart: 5 -> 5, of which waited for: 5 -> 4; matrix products, arithmetic and copies ran while one was open for 1% -> 1% of each run, Pallas kernels for 21% -> 25%
where the time goes in v3:
time: 309 us; the launch traced here: 308 us
  waiting for transfers between devices  157 us (51%)
  Pallas kernels  104 us (34%)
  starting transfers between devices  42.2 us (14%)
    all_to_all x5, waiting for transfers between devices, exchange(): return lax.all_to_all(x, AXES, split_axis=0, concat_axis=0, tiled=True)  157 us
    all_to_all x5, starting transfers between devices, exchange(): return lax.all_to_all(x, AXES, split_axis=0, concat_axis=0, tiled=True)  42.2 us
    pallas_call x1, Pallas kernels, weight_grads(): pl.pallas_call(weights_kernel, grid=(steps,), in_specs=[columns(main), co...  19.1 us
    pallas_call x1, Pallas kernels, dx_side(): pl.pallas_call(dx_kernel, grid=(5,), in_specs=[whole(dab.shape), columns(...  16 us
    pallas_call x1, Pallas kernels, x_side(): pl.pallas_call(x_kernel, grid=(5,), in_specs=[pl.BlockSpec((block, width)...  14.7 us
    pallas_call x1, Pallas kernels, second(): pl.pallas_call(second_kernel, grid=(steps,), in_specs=[whole(normed.shape...  13.3 us
    pallas_call x1, Pallas kernels, c_side(): pl.pallas_call(functools.partial(c_kernel, float(limit)), grid=(hid // ti...  11.8 us
    pallas_call x1, Pallas kernels, turn(): pl.pallas_call(turn_kernel, grid=(hid // tile,), in_specs=[tall, tall, wi...  8.98 us
  transfers between devices with their start and end apart: 5, of which 4 were waited for; matrix products, arithmetic and copies ran while one was open for 1% of the time, Pallas kernels for 25%

profile of v3, /device:TPU:1, one launch (start us, length us, event | category | flops | bytes accessed | tf_op | source)
XLA Modules:
  0.0 308.0 jit_solution(14524972110600120553)
XLA Ops:
  0.6 6.8 %shard_map.127 = (bf16[1024,2560]{1,0:T(8,128)(2,1)}, bf16[128,2048]{1,0:T(8,128)(2,1)}, f32[128,128]{1,0:T(8,128)}, f32[128,128]{1,0:T(8,128)}) custom-call(bf16[128,2048]{1,0:T(8,128)(2,1)} %hid_ref.3, f32[1,2048]{1,0:T(1,128)} %bitcast.29, s32[8,128]{1,0:T(8,128)} %bitcast.32), custom_call_target="tpu_custom_call" | custom-call | flops 1073741824 | bytes 7000000 | tf_op jit(solution)/shard_map/pallas_call | solution.py:103
  7.4 11.9 %all-to-all-start.1 = ((bf16[128,8,2560]{2,1,0:T(8,128)(2,1)}), bf16[128,8,2560]{2,1,0:T(8,128)(2,1)}, u32[]{:S(2)}, u32[]{:S(2)}) async-start(bf16[128,8,2560]{2,1,0:T(8,128)(2,1)} %bitcast.21), calls=%async_computation.1 | async-start | bytes 10485760 | tf_op jit(solution)/shard_map/all_to_all | solution.py:44
  19.3 13.3 %shard_map.128 = (f32[128,128]{1,0:T(8,128)}, bf16[1024,2688]{1,0:T(8,128)(2,1)}) custom-call(bf16[128,2048]{1,0:T(8,128)(2,1)} %get-tuple-element.38.normed_ref, bf16[128,2048]{1,0:T(8,128)(2,1)} %cot_ref.3, f32[128,128]{1,0:T(8,128)} %get-tuple-element.39.slot_ref, f32[128,128]{1,0:T(8,128)} %get-tuple-element.40.slot_t_ref, bf16[2048,128]{1,0:T(8,128)(2,1)} %router_ref.3), custom_call_target="tpu_custom_call" | custom-call | flops 1073741824 | bytes 8000000 | tf_op jit(solution)/shard_map/pallas_call | solution.py:176
  32.6 50.6 %all-to-all-done.1 = bf16[128,8,2560]{2,1,0:T(8,128)(2,1)} async-done(((bf16[128,8,2560]{2,1,0:T(8,128)(2,1)}), bf16[128,8,2560]{2,1,0:T(8,128)(2,1)}, u32[]{:S(2)}, u32[]{:S(2)}) %all-to-all-start.1) | async-done | bytes 5242912 | tf_op jit(solution)/shard_map/all_to_all | solution.py:44
  83.2 6.8 %all-to-all-start = ((bf16[128,8,2688]{2,1,0:T(8,128)(2,1)}), bf16[128,8,2688]{2,1,0:T(8,128)(2,1)}, u32[]{:S(2)}, u32[]{:S(2)}) async-start(bf16[128,8,2688]{2,1,0:T(8,128)(2,1)} %bitcast.20), calls=%async_computation | async-start | bytes 11010048 | tf_op jit(solution)/shard_map/all_to_all | solution.py:44
  90.0 9.0 %shard_map.129 = (bf16[1536,2048]{1,0:T(8,128)(2,1)}, bf16[2048,768]{1,0:T(8,128)(2,1)}) custom-call(bf16[2048,768]{1,0:T(8,128)(2,1)} %bitcast.23, bf16[2048,768]{1,0:T(8,128)(2,1)} %bitcast.25, bf16[768,2048]{1,0:T(8,128)(2,1)} %bitcast.22), custom_call_target="tpu_custom_call" | custom-call | flops 4718592 | bytes 19000000 | tf_op jit(solution)/shard_map/pallas_call | solution.py:206
  99.0 14.7 %shard_map.130 = (bf16[1280,768]{1,0:T(8,128)(2,1)}, bf16[1280,768]{1,0:T(8,128)(2,1)}, bf16[1280,768]{1,0:T(8,128)(2,1)}, bf16[256,2048]{1,0:T(8,128)(2,1)}) custom-call(bf16[1024,2560]{1,0:T(8,128)(2,1)} %bitcast.8.x_ref.ext_ref, bf16[1024,2560]{1,0:T(8,128)(2,1)} %bitcast.8.x_ref.ext_ref, bf16[2048,768]{1,0:T(8,128)(2,1)} %bitcast.24, ...), custom_call_target="tpu_custom_call" | custom-call | flops 8053063680 | bytes 24000000 | tf_op jit(solution)/shard_map/pallas_call | solution.py:256
  113.7 44.7 %all-to-all-done = bf16[128,8,2688]{2,1,0:T(8,128)(2,1)} async-done(((bf16[128,8,2688]{2,1,0:T(8,128)(2,1)}), bf16[128,8,2688]{2,1,0:T(8,128)(2,1)}, u32[]{:S(2)}, u32[]{:S(2)}) %all-to-all-start) | async-done | bytes 5505056 | tf_op jit(solution)/shard_map/all_to_all | solution.py:44
  158.4 11.8 %shard_map.131 = (bf16[1280,1536]{1,0:T(8,128)(2,1)}, bf16[256,2048]{1,0:T(8,128)(2,1)}, f32[128,128]{1,0:T(8,128)}, bf16[128,128]{1,0:T(8,128)(2,1)}) custom-call(bf16[1024,2688]{1,0:T(8,128)(2,1)} %bitcast.3.c_ref.ext_ref.meta_ref, bf16[1024,2688]{1,0:T(8,128)(2,1)} %bitcast.3.c_ref.ext_ref.meta_ref, bf16[1024,2688]{1,0:T(8,128)(2,1)} %bitcast.3.c_ref.ext_ref.meta_ref, ...), custom_call_target="tpu_custom_call" | custom-call | flops 4026531840 | bytes 20000000 | tf_op jit(solution)/shard_map/pallas_call | solution.py:334
  170.2 5.0 %all-to-all-start.2 = ((f32[128,1,128]{2,1,0:T(1,128)}), f32[128,1,128]{2,1,0:T(1,128)S(1)}, u32[]{:S(2)}, u32[]{:S(2)}) async-start(f32[128,1,128]{2,1,0:T(1,128)} %bitcast.28), calls=%async_computation.2 | async-start | bytes 131072 | tf_op jit(solution)/shard_map/all_to_all | solution.py:44
  175.2 16.0 %shard_map.132 = (bf16[1024,2944]{1,0:T(8,128)(2,1)}, bf16[1024,128]{1,0:T(8,128)(2,1)}) custom-call(bf16[1280,1536]{1,0:T(8,128)(2,1)} %get-tuple-element.49.dab_ref, bf16[1536,2048]{1,0:T(8,128)(2,1)} %get-tuple-element.50.both_ref, bf16[1024,2560]{1,0:T(8,128)(2,1)} %bitcast.8.x_ref.ext_ref, bf16[256,2048]{1,0:T(8,128)(2,1)} %get-tuple-element.51.x2_ref, ...), custom_call_target="tpu_custom_call" | custom-call | flops 8053063680 | bytes 20000000 | tf_op jit(solution)/shard_map/pallas_call | solution.py:425
  191.2 0.0 all-to-all-done.2
  191.2 0.0 copy-start
  191.2 0.6 copy-done
  191.8 3.3 %shard_map.133 = (bf16[1024,2944]{1,0:T(8,128)(2,1)}, bf16[128,128]{1,0:T(8,128)(2,1)}, f32[128,128]{1,0:T(8,128)}) custom-call(f32[128,128]{1,0:T(8,128)} %bitcast.27, f32[128,128]{1,0:T(8,128)} %get-tuple-element.39.slot_ref, f32[128,128]{1,0:T(8,128)} %get-tuple-element.48.gates_ref, ...), custom_call_target="tpu_custom_call", output_to_operand_aliasing={{0}: (5, {})} | custom-call | flops 67108864 | bytes 2500000 | tf_op jit(solution)/shard_map/pallas_call | solution.py:525
  195.1 10.3 %all-to-all-start.3 = ((bf16[128,8,2944]{2,1,0:T(8,128)(2,1)}), bf16[128,8,2944]{2,1,0:T(8,128)(2,1)}, u32[]{:S(2)}, u32[]{:S(2)}) async-start(bf16[128,8,2944]{2,1,0:T(8,128)(2,1)} %bitcast.19), calls=%async_computation.3 | async-start | bytes 12058624 | tf_op jit(solution)/shard_map/all_to_all | solution.py:44
  205.4 0.8 dynamic_slice.6
  206.2 1.3 dynamic-slice_convert_fusion.refs_3_
  207.4 19.1 %shard_map.135 = (bf16[2048,768]{1,0:T(8,128)(2,1)}, bf16[2048,768]{1,0:T(8,128)(2,1)}, bf16[768,2048]{1,0:T(8,128)(2,1)}) custom-call(bf16[1024,2560]{1,0:T(8,128)(2,1)} %bitcast.8.x_ref.ext_ref, bf16[1024,2688]{1,0:T(8,128)(2,1)} %bitcast.3.c_ref.ext_ref.meta_ref, bf16[256,2048]{1,0:T(8,128)(2,1)} %get-tuple-element.51.x2_ref, ...), custom_call_target="tpu_custom_call" | custom-call | flops 12079595520 | bytes 36000000 | tf_op jit(solution)/shard_map/pallas_call | solution.py:469
  226.5 0.6 iota.7.refs_5_
  227.1 0.7 broadcast_in_dim.15.refs_4_
  227.8 52.2 %all-to-all-done.3 = bf16[128,8,2944]{2,1,0:T(8,128)(2,1)} async-done(((bf16[128,8,2944]{2,1,0:T(8,128)(2,1)}), bf16[128,8,2944]{2,1,0:T(8,128)(2,1)}, u32[]{:S(2)}, u32[]{:S(2)}) %all-to-all-start.3) | async-done | bytes 6029344 | tf_op jit(solution)/shard_map/all_to_all | solution.py:44
  279.9 2.4 shard_map.136
  282.3 8.2 %all-to-all-start.4 = ((bf16[128,24,128]{2,1,0:T(8,128)(2,1)}), bf16[128,24,128]{2,1,0:T(8,128)(2,1)S(1)}, u32[]{:S(2)}, u32[]{:S(2)}) async-start(bf16[128,24,128]{2,1,0:T(8,128)(2,1)} %shard_map.136), calls=%async_computation.4 | async-start | bytes 1572864 | tf_op jit(solution)/shard_map/all_to_all | solution.py:44
  290.5 6.5 %shard_map.134 = bf16[128,2048]{1,0:T(8,128)(2,1)} custom-call(bf16[1024,2944]{1,0:T(8,128)(2,1)} %bitcast.13.dx_ref.ext_ref.refs_0_.refs_1_.refs_2_, bf16[1024,2944]{1,0:T(8,128)(2,1)} %bitcast.13.dx_ref.ext_ref.refs_0_.refs_1_.refs_2_, f32[128,128]{1,0:T(8,128)} %get-tuple-element.40.slot_t_ref, f32[128,128]{1,0:T(8,128)} %get-tuple-element.56.gk_t_ref, ...), custom_call_target="tpu_custom_call" | custom-call | flops 1073741824 | bytes 9000000 | tf_op jit(solution)/shard_map/pallas_call | solution.py:610
  296.9 10.0 %all-to-all-done.4.sums_ref = bf16[128,24,128]{2,1,0:T(8,128)(2,1)S(1)} async-done(((bf16[128,24,128]{2,1,0:T(8,128)(2,1)}), bf16[128,24,128]{2,1,0:T(8,128)(2,1)S(1)}, u32[]{:S(2)}, u32[]{:S(2)}) %all-to-all-start.4) | async-done | bytes 786464 | tf_op jit(solution)/shard_map/all_to_all | solution.py:44
  306.9 1.0 shard_map.137
  (1 shorter events, 0.0 us)
Async XLA Ops:
  7.4 75.8 %all-to-all-start.1 = ((bf16[128,8,2560]{2,1,0:T(8,128)(2,1)}), bf16[128,8,2560]{2,1,0:T(8,128)(2,1)}, u32[]{:S(2)}, u32[]{:S(2)}) async-start(bf16[128,8,2560]{2,1,0:T(8,128)(2,1)} %bitcast.21), calls=%async_computation.1 | async-start | bytes 10485760 | tf_op jit(solution)/shard_map/all_to_all | solution.py:44
  83.2 75.2 %all-to-all-start = ((bf16[128,8,2688]{2,1,0:T(8,128)(2,1)}), bf16[128,8,2688]{2,1,0:T(8,128)(2,1)}, u32[]{:S(2)}, u32[]{:S(2)}) async-start(bf16[128,8,2688]{2,1,0:T(8,128)(2,1)} %bitcast.20), calls=%async_computation | async-start | bytes 11010048 | tf_op jit(solution)/shard_map/all_to_all | solution.py:44
  170.2 21.0 %all-to-all-start.2 = ((f32[128,1,128]{2,1,0:T(1,128)}), f32[128,1,128]{2,1,0:T(1,128)S(1)}, u32[]{:S(2)}, u32[]{:S(2)}) async-start(f32[128,1,128]{2,1,0:T(1,128)} %bitcast.28), calls=%async_computation.2 | async-start | bytes 131072 | tf_op jit(solution)/shard_map/all_to_all | solution.py:44
  191.2 0.6 copy-start
  195.1 84.9 %all-to-all-start.3 = ((bf16[128,8,2944]{2,1,0:T(8,128)(2,1)}), bf16[128,8,2944]{2,1,0:T(8,128)(2,1)}, u32[]{:S(2)}, u32[]{:S(2)}) async-start(bf16[128,8,2944]{2,1,0:T(8,128)(2,1)} %bitcast.19), calls=%async_computation.3 | async-start | bytes 12058624 | tf_op jit(solution)/shard_map/all_to_all | solution.py:44
  282.3 24.6 %all-to-all-start.4 = ((bf16[128,24,128]{2,1,0:T(8,128)(2,1)}), bf16[128,24,128]{2,1,0:T(8,128)(2,1)S(1)}, u32[]{:S(2)}, u32[]{:S(2)}) async-start(bf16[128,24,128]{2,1,0:T(8,128)(2,1)} %shard_map.136), calls=%async_computation.4 | async-start | bytes 1572864 | tf_op jit(solution)/shard_map/all_to_all | solution.py:44

commit v4 on v3

--- a/solution.py
+++ b/solution.py
@@ -11,6 +11,7 @@
 HI = 8
 SUB = 8
 MSG = 128
+MARK = 128.0
 TILE = 256
 AXES = ("seq", "exp")
 bf16, f32 = jnp.bfloat16, jnp.float32
@@ -44,34 +45,33 @@
     return lax.all_to_all(x, AXES, split_axis=0, concat_axis=0, tiled=True)
 
 
-def slots_chosen(slot_t):
+def slots_chosen(slot_t, weight_t=None):
     experts, tokens = slot_t.shape
     which = iota((experts, HI, tokens), 1).astype(f32)
-    chosen = jnp.where(slot_t[:, None, :] == which, 1.0, 0.0)
+    chosen = jnp.where(slot_t[:, None, :] == which, 1.0 if weight_t is None else weight_t[:, None, :], 0.0)
     return chosen.reshape(experts * HI, tokens).astype(bf16)
 
 
-def quarter_chosen(slot_t, j):
+def quarter_chosen(slot_t, j, weight_t=None):
     experts, tokens = slot_t.shape
     row = iota((experts, SUB, tokens), 1)
     chosen = (slot_t[:, None, :] == (HI + row // 4).astype(f32)) & (row % 4 == j)
-    return jnp.where(chosen, 1.0, 0.0).reshape(experts * SUB, tokens).astype(bf16)
-
-
-def front_kernel(hid_ref, gain_ref, ids_ref, out_ref, normed_ref, slot_ref, slot_t_ref, tiles, p8):
+    weight = 1.0 if weight_t is None else weight_t[:, None, :]
+    return jnp.where(chosen, weight, 0.0).reshape(experts * SUB, tokens).astype(bf16)
+
+
+def front_kernel(hid_ref, gain_ref, ids_ref, out_ref, normed_ref, slot_ref, slot_t_ref):
     step = pl.program_id(0)
-    tokens = hid_ref.shape[0]
+    tokens, width = hid_ref.shape
     experts = slot_ref.shape[1]
-    tile = tiles.shape[2]
+    quarter = width // 4
+    chunk = out_ref.shape[0] // HI
 
     @pl.when(step == 0)
     def _():
         h = hid_ref[...].astype(f32)
         scale = lax.rsqrt(jnp.mean(h * h, axis=1, keepdims=True) + norm_eps)
-        normed = (h * scale * gain_ref[...]).astype(bf16)
-        normed_ref[...] = normed
-        for j in range(4):
-            tiles[j] = normed[:, j * tile : (j + 1) * tile]
+        normed_ref[...] = (h * scale * gain_ref[...]).astype(bf16)
         ids = ids_ref[...]
         expert = iota((experts, tokens), 0)
         member = jnp.zeros((experts, tokens), f32)
@@ -82,49 +82,42 @@
         slot_t = jnp.where(member > 0.0, position, 99.0)
         slot_ref[...] = slot_t.T
         slot_t_ref[...] = slot_t
-        p8[...] = slots_chosen(slot_t)
-
-    @pl.when(step < 4)
-    def _():
-        out_ref[...] = mm(p8[...], tiles[jnp.minimum(step, 3)]).astype(bf16)
-
-    @pl.when(step == 4)
-    def _():
-        slot_t = slot_t_ref[...]
-        total = mm(quarter_chosen(slot_t, 0), tiles[0])
-        for j in range(1, 4):
-            total = total + mm(quarter_chosen(slot_t, j), tiles[j])
-        out_ref[...] = total.astype(bf16)
+
+    slot_t = slot_t_ref[pl.ds(pl.multiple_of(step * chunk, chunk), chunk), :]
+    out_ref[:, :width] = mm(slots_chosen(slot_t), normed_ref[...]).astype(bf16)
+    total = mm(quarter_chosen(slot_t, 0), normed_ref[:, :quarter])
+    for j in range(1, 4):
+        total = total + mm(quarter_chosen(slot_t, j), normed_ref[:, j * quarter : (j + 1) * quarter])
+    out_ref[:, width:] = total.astype(bf16)
 
 
 def front(hidden, gain, ids, experts):
     tokens, width = hidden.shape
-    tile = width // 4
+    columns = width + width // 4
+    chunk = experts // 4
     return pl.pallas_call(
         front_kernel,
-        grid=(5,),
+        grid=(4,),
         in_specs=[whole((tokens, width)), whole((1, width)), whole(ids.shape)],
         out_specs=[
-            pl.BlockSpec((experts * HI, tile), lambda i: (0, i)),
+            pl.BlockSpec((chunk * HI, columns), lambda i: (i, 0)),
             whole((tokens, width)),
             whole((tokens, experts)),
             whole((experts, tokens)),
         ],
         out_shape=[
-            jax.ShapeDtypeStruct((experts * HI, width + tile), bf16),
+            jax.ShapeDtypeStruct((experts * HI, columns), bf16),
             jax.ShapeDtypeStruct((tokens, width), bf16),
             jax.ShapeDtypeStruct((tokens, experts), f32),
             jax.ShapeDtypeStruct((experts, tokens), f32),
         ],
-        scratch_shapes=[pltpu.VMEM((4, tokens, tile), bf16), pltpu.VMEM((experts * HI, tokens), bf16)],
         compiler_params=params(),
         cost_estimate=pl.CostEstimate(flops=4 * experts * HI * tokens * width, bytes_accessed=7_000_000, transcendentals=tokens),
     )(hidden, gain, ids)
 
 
-def second_kernel(normed_ref, cot_ref, slot_ref, slot_t_ref, router_ref, gates_ref, out_ref, tiles, p8, p2, meta):
-    step, last = pl.program_id(0), pl.num_programs(0) - 1
-    experts = slot_ref.shape[1]
+def second_kernel(normed_ref, cot_ref, slot_ref, slot_t_ref, router_ref, gates_ref, out_ref, tiles, p8, p2, empty):
+    step = pl.program_id(0)
     count = tiles.shape[0]
     per = count // 4
 
@@ -135,43 +128,37 @@
         gates = weights / jnp.sum(weights, axis=1, keepdims=True)
         gates_ref[...] = gates
         slot_t = slot_t_ref[...]
-        gates_t = gates.T
-        lane = iota((experts, MSG), 1)
-        message = jnp.where(lane == 10, jnp.sum(jnp.where(slot_t < 50.0, 1.0, 0.0), axis=1, keepdims=True), 0.0)
-        for s in range(10):
-            message = message + jnp.where(
-                lane == s, jnp.sum(jnp.where(slot_t == s, gates_t, 0.0), axis=1, keepdims=True), 0.0
-            )
-        sub = iota((experts, SUB, MSG), 1)
-        meta[...] = jnp.where(sub == 0, message[:, None, :], 0.0).reshape(experts * SUB, MSG).astype(bf16)
+        gates_t = gates.astype(bf16).astype(f32).T
         for j in range(count):
             tiles[j] = cot_ref[:, j * MSG : (j + 1) * MSG]
-        p8[...] = slots_chosen(slot_t)
+        p8[...] = slots_chosen(slot_t, gates_t)
+        first = iota(empty.shape[1:], 1) == 0
+        used = jnp.sum(slots_chosen(slot_t).astype(f32), axis=1, keepdims=True)
+        empty[0] = jnp.where(first & (used < 0.5), MARK, 0.0)
         for j in range(4):
-            p2[j] = quarter_chosen(slot_t, j)
+            p2[j] = quarter_chosen(slot_t, j, gates_t)
+        used = sum(jnp.sum(quarter_chosen(slot_t, j).astype(f32), axis=1, keepdims=True) for j in range(4))
+        empty[1] = jnp.where(first & (used < 0.5), MARK, 0.0)
 
     @pl.when(step < count)
     def _():
-        out_ref[...] = mm(p8[...], tiles[jnp.minimum(step, count - 1)]).astype(bf16)
-
-    @pl.when((step >= count) & (step < last))
+        mark = jnp.where(step == 0, empty[0], 0.0)
+        out_ref[...] = (mm(p8[...], tiles[jnp.minimum(step, count - 1)]) + mark).astype(bf16)
+
+    @pl.when(step >= count)
     def _():
         at = jnp.clip(step - count, 0, per - 1)
         total = mm(p2[0], tiles[at])
         for j in range(1, 4):
             total = total + mm(p2[j], tiles[j * per + at])
-        out_ref[...] = total.astype(bf16)
-
-    @pl.when(step == last)
-    def _():
-        out_ref[...] = meta[...]
+        out_ref[...] = (total + jnp.where(step == count, empty[1], 0.0)).astype(bf16)
 
 
 def second(normed, cotangent, slot, slot_t, router):
     tokens, width = normed.shape
     experts = slot.shape[1]
     count = width // MSG
-    steps = count + count // 4 + 1
+    steps = count + count // 4
     n_rows = experts * HI
     return pl.pallas_call(
         second_kernel,
@@ -186,7 +173,7 @@
             pltpu.VMEM((count, tokens, MSG), bf16),
             pltpu.VMEM((n_rows, tokens), bf16),
             pltpu.VMEM((4, n_rows, tokens), bf16),
-            pltpu.VMEM((n_rows, MSG), bf16),
+            pltpu.VMEM((2, n_rows, MSG), f32),
         ],
         compiler_params=params(),
         cost_estimate=pl.CostEstimate(flops=4 * n_rows * tokens * width, bytes_accessed=8_000_000, transcendentals=tokens * experts),
@@ -282,7 +269,7 @@
     return total
 
 
-def c_kernel(limit, c_ref, ext_ref, meta_ref, wd_t_ref, act_ref, fa_ref, fb_ref, dab_ref, c2_ref, msg_ref, scale_ref, q8, q2):
+def c_kernel(limit, c_ref, ext_ref, wd_t_ref, act_ref, fa_ref, fb_ref, dab_ref, c2_ref, msg_ref, scale_ref, q8, q2):
     step, last = pl.program_id(0), pl.num_programs(0) - 1
     sources = msg_ref.shape[0]
     main, tail = c_ref.shape[0], c2_ref.shape[0]
@@ -303,22 +290,25 @@
     @pl.when(step == last)
     def _():
         lane, which = iota((sources, HI, MSG), 2), iota((sources, HI, MSG), 1)
-        q = jnp.sum(q8[...], axis=1, keepdims=True)
-        q_rows = jnp.sum(jnp.where(lane == which, q.reshape(sources, HI, 1), 0.0), axis=1).astype(bf16).astype(f32)
-        q = jnp.sum(q2[...], axis=1, keepdims=True)
-        parity = iota((tail, MSG), 0) % 2
-        spread = jnp.where(iota((tail, MSG), 1) == HI + parity, q, 0.0).astype(bf16)
         gather = jnp.where(iota((sources, tail), 1) // 2 == iota((sources, tail), 0), 1.0, 0.0).astype(bf16)
-        q_rows = q_rows + mm(gather, spread)
-        meta = jnp.sum(meta_ref[...].astype(f32).reshape(sources, SUB, MSG), axis=1)
-        lane = iota((sources, MSG), 1)
-        count = jnp.sum(jnp.where(lane == 10, meta, 0.0), axis=1, keepdims=True)
+        own_lane = iota((tail, MSG), 1) == HI + iota((tail, MSG), 0) % 2
+
+        def table(column, tail_column):
+            table = jnp.sum(jnp.where(lane == which, column.reshape(sources, HI, 1), 0.0), axis=1)
+            return table + mm(gather, jnp.where(own_lane, tail_column, 0.0).astype(bf16))
+
+        def live(ref):
+            return jnp.where(ref[:, :MSG].astype(f32)[:, 0:1] < MARK / 2, 1.0, 0.0)
+
+        q_rows = table(jnp.sum(q8[...], axis=1, keepdims=True), jnp.sum(q2[...], axis=1, keepdims=True))
+        count = jnp.sum(table(live(c_ref), live(c2_ref)), axis=1, keepdims=True)
         lower = jnp.where(iota((sources, sources), 1) < iota((sources, sources), 0), 1.0, 0.0).astype(bf16)
         offset = mm(lower, jnp.broadcast_to(count, (sources, MSG)).astype(bf16))
+        lane = iota((sources, MSG), 1)
         slot = jnp.where(lane < 10, lane, lane - 10).astype(f32)
         kept = (slot < count) & (offset + slot < limit) & (lane < 20)
         msg_ref[...] = jnp.where(kept, jnp.where(lane < 10, q_rows, 1.0), 0.0)
-        scale_ref[...] = jnp.where(kept & (lane < 10), meta, 0.0).astype(bf16)
+        scale_ref[...] = jnp.where(kept & (lane < 10), 1.0, 0.0).astype(bf16)
 
 
 def c_side(r2, wd_t, act, fa, fb, limit):
@@ -337,7 +327,6 @@
         in_specs=[
             whole((main, width)),
             pl.BlockSpec((main, width // 4), lambda i: (0, 4)),
-            pl.BlockSpec((main, MSG), lambda i: (0, (width + width // 4) // MSG)),
             columns(width, tile),
             columns(total, tile),
             columns(total, tile),
@@ -353,7 +342,7 @@
         scratch_shapes=[pltpu.VMEM((main, MSG), f32), pltpu.VMEM((tail, MSG), f32)],
         compiler_params=params(),
         cost_estimate=pl.CostEstimate(flops=2 * total * wd_t.size, bytes_accessed=20_000_000, transcendentals=0),
-    )(r2, r2, r2, wd_t, act, fa, fb)
+    )(r2, r2, wd_t, act, fa, fb)
 
 
 def column_of(table):
@@ -491,16 +480,18 @@
     def _():
         q_t = q_ref[...].T
         slot, gates = slot_ref[...], gates_ref[...]
-        dgate = jnp.zeros_like(gates)
+        gated = jnp.zeros_like(gates)
         kept = jnp.zeros_like(gates)
         for s in range(10):
             here = slot == s
-            dgate = dgate + jnp.where(here, q_t[s : s + 1, :], 0.0)
+            gated = gated + jnp.where(here, q_t[s : s + 1, :], 0.0)
             kept = kept + jnp.where(here, q_t[10 + s : 11 + s, :], 0.0)
-        dsel = gates * (dgate - jnp.sum(gates * dgate, axis=1, keepdims=True))
+        rounded = gates.astype(bf16).astype(f32)
+        gated = gated * jnp.where(rounded > 0.0, gates / jnp.where(rounded > 0.0, rounded, 1.0), 0.0)
+        dsel = gated - gates * jnp.sum(gated, axis=1, keepdims=True)
         dl = dsel.astype(bf16)
         dl_ref[...] = dl
-        gk_t_ref[...] = (gates.astype(bf16).astype(f32) * kept).T
+        gk_t_ref[...] = kept.T
         if experts < MSG:
             dl = jnp.concatenate([dl, jnp.zeros((dl.shape[0], MSG - experts), bf16)], axis=1)
         groups = router_part.shape[0]
@@ -667,7 +658,7 @@
     r1 = exchange(s1.reshape(experts, HI, width + quarter)).reshape(experts * HI, width + quarter)
     gates, s2 = second(normed, cotangent, slot, slot_t, router)
     both, wd_t = turn(wg, wu, wd)
-    r2 = exchange(s2.reshape(experts, SUB, width + quarter + MSG)).reshape(experts * SUB, width + quarter + MSG)
+    r2 = exchange(s2.reshape(experts, SUB, width + quarter)).reshape(experts * SUB, width + quarter)
     act, fa, fb, x2 = x_side(r1, wg, wu)
     dab, c2, q_msg, scale = c_side(r2, wd_t, act, fa, fb, limit)
     q_home = exchange(q_msg.reshape(experts, 1, MSG)).reshape(experts, MSG)

time: 309 us -> 304 us (0.984)
  waiting for transfers between devices: 157 us -> 153 us
    all_to_all x5, waiting for transfers between devices: 157 us -> 153 us  [exchange(): return lax.all_to_all(x, AXES, split_axis=0, concat_axis=0, tiled=True)]
  transfers between devices with their start and end apart: 5 -> 5, of which waited for: 4 -> 4; matrix products, arithmetic and copies ran while one was open for 1% -> 1% of each run, Pallas kernels for 25% -> 26%
where the time goes in v4:
time: 304 us
  waiting for transfers between devices  153 us (50%)
  Pallas kernels  103 us (34%)
  starting transfers between devices  43.5 us (14%)
    all_to_all x5, waiting for transfers between devices, exchange(): return lax.all_to_all(x, AXES, split_axis=0, concat_axis=0, tiled=True)  153 us
    all_to_all x5, starting transfers between devices, exchange(): return lax.all_to_all(x, AXES, split_axis=0, concat_axis=0, tiled=True)  43.5 us
    pallas_call x1, Pallas kernels, weight_grads(): pl.pallas_call(weights_kernel, grid=(steps,), in_specs=[columns(main), co...  19.2 us
    pallas_call x1, Pallas kernels, dx_side(): pl.pallas_call(dx_kernel, grid=(5,), in_specs=[whole(dab.shape), columns(...  16 us
    pallas_call x1, Pallas kernels, x_side(): pl.pallas_call(x_kernel, grid=(5,), in_specs=[pl.BlockSpec((block, width)...  14.7 us
    pallas_call x1, Pallas kernels, second(): pl.pallas_call(second_kernel, grid=(steps,), in_specs=[whole(normed.shape...  13.3 us
    pallas_call x1, Pallas kernels, c_side(): pl.pallas_call(functools.partial(c_kernel, float(limit)), grid=(hid // ti...  11.9 us
    pallas_call x1, Pallas kernels, turn(): pl.pallas_call(turn_kernel, grid=(hid // tile,), in_specs=[tall, tall, wi...  8.98 us
  transfers between devices with their start and end apart: 5, of which 4 were waited for; matrix products, arithmetic and copies ran while one was open for 1% of the time, Pallas kernels for 26%

profile of v4, /device:TPU:1, one launch (start us, length us, event | category | flops | bytes accessed | tf_op | source)
XLA Modules:
  0.0 303.8 jit_solution(18048600623167664607)
XLA Ops:
  0.6 5.6 %shard_map.127 = (bf16[1024,2560]{1,0:T(8,128)(2,1)}, bf16[128,2048]{1,0:T(8,128)(2,1)}, f32[128,128]{1,0:T(8,128)}, f32[128,128]{1,0:T(8,128)}) custom-call(bf16[128,2048]{1,0:T(8,128)(2,1)} %hid_ref.3, f32[1,2048]{1,0:T(1,128)} %bitcast.29, s32[8,128]{1,0:T(8,128)} %bitcast.32), custom_call_target="tpu_custom_call" | custom-call | flops 1073741824 | bytes 7000000 | tf_op jit(solution)/shard_map/pallas_call | solution.py:98
  6.2 11.9 %all-to-all-start.1 = ((bf16[128,8,2560]{2,1,0:T(8,128)(2,1)}), bf16[128,8,2560]{2,1,0:T(8,128)(2,1)}, u32[]{:S(2)}, u32[]{:S(2)}) async-start(bf16[128,8,2560]{2,1,0:T(8,128)(2,1)} %bitcast.21), calls=%async_computation.1 | async-start | bytes 10485760 | tf_op jit(solution)/shard_map/all_to_all | solution.py:45
  18.1 13.3 %shard_map.128 = (f32[128,128]{1,0:T(8,128)}, bf16[1024,2560]{1,0:T(8,128)(2,1)}) custom-call(bf16[128,2048]{1,0:T(8,128)(2,1)} %get-tuple-element.38.normed_ref, bf16[128,2048]{1,0:T(8,128)(2,1)} %cot_ref.3, f32[128,128]{1,0:T(8,128)} %get-tuple-element.39.slot_ref, f32[128,128]{1,0:T(8,128)} %get-tuple-element.40.slot_t_ref, bf16[2048,128]{1,0:T(8,128)(2,1)} %router_ref.3), custom_call_target="tpu_custom_call" | custom-call | flops 1073741824 | bytes 8000000 | tf_op jit(solution)/shard_map/pallas_call | solution.py:163
  31.5 50.6 %all-to-all-done.1 = bf16[128,8,2560]{2,1,0:T(8,128)(2,1)} async-done(((bf16[128,8,2560]{2,1,0:T(8,128)(2,1)}), bf16[128,8,2560]{2,1,0:T(8,128)(2,1)}, u32[]{:S(2)}, u32[]{:S(2)}) %all-to-all-start.1) | async-done | bytes 5242912 | tf_op jit(solution)/shard_map/all_to_all | solution.py:45
  82.0 6.8 %all-to-all-start = ((bf16[128,8,2560]{2,1,0:T(8,128)(2,1)}), bf16[128,8,2560]{2,1,0:T(8,128)(2,1)}, u32[]{:S(2)}, u32[]{:S(2)}) async-start(bf16[128,8,2560]{2,1,0:T(8,128)(2,1)} %bitcast.20), calls=%async_computation | async-start | bytes 10485760 | tf_op jit(solution)/shard_map/all_to_all | solution.py:45
  88.9 9.0 %shard_map.129 = (bf16[1536,2048]{1,0:T(8,128)(2,1)}, bf16[2048,768]{1,0:T(8,128)(2,1)}) custom-call(bf16[2048,768]{1,0:T(8,128)(2,1)} %bitcast.23, bf16[2048,768]{1,0:T(8,128)(2,1)} %bitcast.25, bf16[768,2048]{1,0:T(8,128)(2,1)} %bitcast.22), custom_call_target="tpu_custom_call" | custom-call | flops 4718592 | bytes 19000000 | tf_op jit(solution)/shard_map/pallas_call | solution.py:193
  97.9 14.7 %shard_map.130 = (bf16[1280,768]{1,0:T(8,128)(2,1)}, bf16[1280,768]{1,0:T(8,128)(2,1)}, bf16[1280,768]{1,0:T(8,128)(2,1)}, bf16[256,2048]{1,0:T(8,128)(2,1)}) custom-call(bf16[1024,2560]{1,0:T(8,128)(2,1)} %bitcast.8.x_ref.ext_ref, bf16[1024,2560]{1,0:T(8,128)(2,1)} %bitcast.8.x_ref.ext_ref, bf16[2048,768]{1,0:T(8,128)(2,1)} %bitcast.24, ...), custom_call_target="tpu_custom_call" | custom-call | flops 8053063680 | bytes 24000000 | tf_op jit(solution)/shard_map/pallas_call | solution.py:243
  112.6 40.2 %all-to-all-done = bf16[128,8,2560]{2,1,0:T(8,128)(2,1)} async-done(((bf16[128,8,2560]{2,1,0:T(8,128)(2,1)}), bf16[128,8,2560]{2,1,0:T(8,128)(2,1)}, u32[]{:S(2)}, u32[]{:S(2)}) %all-to-all-start) | async-done | bytes 5242912 | tf_op jit(solution)/shard_map/all_to_all | solution.py:45
  152.8 11.9 %shard_map.131 = (bf16[1280,1536]{1,0:T(8,128)(2,1)}, bf16[256,2048]{1,0:T(8,128)(2,1)}, f32[128,128]{1,0:T(8,128)}, bf16[128,128]{1,0:T(8,128)(2,1)}) custom-call(bf16[1024,2560]{1,0:T(8,128)(2,1)} %bitcast.3.c_ref.ext_ref, bf16[1024,2560]{1,0:T(8,128)(2,1)} %bitcast.3.c_ref.ext_ref, bf16[2048,768]{1,0:T(8,128)(2,1)} %get-tuple-element.42.wd_t_ref, ...), custom_call_target="tpu_custom_call" | custom-call | flops 4026531840 | bytes 20000000 | tf_op jit(solution)/shard_map/pallas_call | solution.py:324
  164.7 6.5 %all-to-all-start.2 = ((f32[128,1,128]{2,1,0:T(1,128)}), f32[128,1,128]{2,1,0:T(1,128)S(1)}, u32[]{:S(2)}, u32[]{:S(2)}) async-start(f32[128,1,128]{2,1,0:T(1,128)} %bitcast.28), calls=%async_computation.2 | async-start | bytes 131072 | tf_op jit(solution)/shard_map/all_to_all | solution.py:45
  171.1 16.0 %shard_map.132 = (bf16[1024,2944]{1,0:T(8,128)(2,1)}, bf16[1024,128]{1,0:T(8,128)(2,1)}) custom-call(bf16[1280,1536]{1,0:T(8,128)(2,1)} %get-tuple-element.49.dab_ref, bf16[1536,2048]{1,0:T(8,128)(2,1)} %get-tuple-element.50.both_ref, bf16[1024,2560]{1,0:T(8,128)(2,1)} %bitcast.8.x_ref.ext_ref, bf16[256,2048]{1,0:T(8,128)(2,1)} %get-tuple-element.51.x2_ref, ...), custom_call_target="tpu_custom_call" | custom-call | flops 8053063680 | bytes 20000000 | tf_op jit(solution)/shard_map/pallas_call | solution.py:414
  187.2 0.0 all-to-all-done.2
  187.2 0.0 copy-start
  187.2 0.6 copy-done
  187.8 3.2 %shard_map.133 = (bf16[1024,2944]{1,0:T(8,128)(2,1)}, bf16[128,128]{1,0:T(8,128)(2,1)}, f32[128,128]{1,0:T(8,128)}) custom-call(f32[128,128]{1,0:T(8,128)} %bitcast.27, f32[128,128]{1,0:T(8,128)} %get-tuple-element.39.slot_ref, f32[128,128]{1,0:T(8,128)} %get-tuple-element.48.gates_ref, ...), custom_call_target="tpu_custom_call", output_to_operand_aliasing={{0}: (5, {})} | custom-call | flops 67108864 | bytes 2500000 | tf_op jit(solution)/shard_map/pallas_call | solution.py:516
  191.0 10.1 %all-to-all-start.3 = ((bf16[128,8,2944]{2,1,0:T(8,128)(2,1)}), bf16[128,8,2944]{2,1,0:T(8,128)(2,1)}, u32[]{:S(2)}, u32[]{:S(2)}) async-start(bf16[128,8,2944]{2,1,0:T(8,128)(2,1)} %bitcast.19), calls=%async_computation.3 | async-start | bytes 12058624 | tf_op jit(solution)/shard_map/all_to_all | solution.py:45
  201.2 0.8 dynamic_slice.6
  201.9 1.3 dynamic-slice_convert_fusion.refs_3_
  203.2 19.2 %shard_map.135 = (bf16[2048,768]{1,0:T(8,128)(2,1)}, bf16[2048,768]{1,0:T(8,128)(2,1)}, bf16[768,2048]{1,0:T(8,128)(2,1)}) custom-call(bf16[1024,2560]{1,0:T(8,128)(2,1)} %bitcast.8.x_ref.ext_ref, bf16[1024,2560]{1,0:T(8,128)(2,1)} %bitcast.3.c_ref.ext_ref, bf16[256,2048]{1,0:T(8,128)(2,1)} %get-tuple-element.51.x2_ref, ...), custom_call_target="tpu_custom_call" | custom-call | flops 12079595520 | bytes 36000000 | tf_op jit(solution)/shard_map/pallas_call | solution.py:458
  222.4 0.6 iota.7.refs_5_
  223.0 0.7 broadcast_in_dim.15.refs_4_
  223.7 52.0 %all-to-all-done.3 = bf16[128,8,2944]{2,1,0:T(8,128)(2,1)} async-done(((bf16[128,8,2944]{2,1,0:T(8,128)(2,1)}), bf16[128,8,2944]{2,1,0:T(8,128)(2,1)}, u32[]{:S(2)}, u32[]{:S(2)}) %all-to-all-start.3) | async-done | bytes 6029344 | tf_op jit(solution)/shard_map/all_to_all | solution.py:45
  275.7 2.4 shard_map.136
  278.1 8.2 %all-to-all-start.4 = ((bf16[128,24,128]{2,1,0:T(8,128)(2,1)}), bf16[128,24,128]{2,1,0:T(8,128)(2,1)S(1)}, u32[]{:S(2)}, u32[]{:S(2)}) async-start(bf16[128,24,128]{2,1,0:T(8,128)(2,1)} %shard_map.136), calls=%async_computation.4 | async-start | bytes 1572864 | tf_op jit(solution)/shard_map/all_to_all | solution.py:45
  286.3 6.5 %shard_map.134 = bf16[128,2048]{1,0:T(8,128)(2,1)} custom-call(bf16[1024,2944]{1,0:T(8,128)(2,1)} %bitcast.13.dx_ref.ext_ref.refs_0_.refs_1_.refs_2_, bf16[1024,2944]{1,0:T(8,128)(2,1)} %bitcast.13.dx_ref.ext_ref.refs_0_.refs_1_.refs_2_, f32[128,128]{1,0:T(8,128)} %get-tuple-element.40.slot_t_ref, f32[128,128]{1,0:T(8,128)} %get-tuple-element.56.gk_t_ref, ...), custom_call_target="tpu_custom_call" | custom-call | flops 1073741824 | bytes 9000000 | tf_op jit(solution)/shard_map/pallas_call | solution.py:601
  292.7 10.0 %all-to-all-done.4.sums_ref = bf16[128,24,128]{2,1,0:T(8,128)(2,1)S(1)} async-done(((bf16[128,24,128]{2,1,0:T(8,128)(2,1)}), bf16[128,24,128]{2,1,0:T(8,128)(2,1)S(1)}, u32[]{:S(2)}, u32[]{:S(2)}) %all-to-all-start.4) | async-done | bytes 786464 | tf_op jit(solution)/shard_map/all_to_all | solution.py:45
  302.7 1.0 shard_map.137
  (1 shorter events, 0.0 us)
Async XLA Ops:
  6.2 75.8 %all-to-all-start.1 = ((bf16[128,8,2560]{2,1,0:T(8,128)(2,1)}), bf16[128,8,2560]{2,1,0:T(8,128)(2,1)}, u32[]{:S(2)}, u32[]{:S(2)}) async-start(bf16[128,8,2560]{2,1,0:T(8,128)(2,1)} %bitcast.21), calls=%async_computation.1 | async-start | bytes 10485760 | tf_op jit(solution)/shard_map/all_to_all | solution.py:45
  82.0 70.7 %all-to-all-start = ((bf16[128,8,2560]{2,1,0:T(8,128)(2,1)}), bf16[128,8,2560]{2,1,0:T(8,128)(2,1)}, u32[]{:S(2)}, u32[]{:S(2)}) async-start(bf16[128,8,2560]{2,1,0:T(8,128)(2,1)} %bitcast.20), calls=%async_computation | async-start | bytes 10485760 | tf_op jit(solution)/shard_map/all_to_all | solution.py:45
  164.7 22.5 %all-to-all-start.2 = ((f32[128,1,128]{2,1,0:T(1,128)}), f32[128,1,128]{2,1,0:T(1,128)S(1)}, u32[]{:S(2)}, u32[]{:S(2)}) async-start(f32[128,1,128]{2,1,0:T(1,128)} %bitcast.28), calls=%async_computation.2 | async-start | bytes 131072 | tf_op jit(solution)/shard_map/all_to_all | solution.py:45
  187.2 0.6 copy-start
  191.0 84.7 %all-to-all-start.3 = ((bf16[128,8,2944]{2,1,0:T(8,128)(2,1)}), bf16[128,8,2944]{2,1,0:T(8,128)(2,1)}, u32[]{:S(2)}, u32[]{:S(2)}) async-start(bf16[128,8,2944]{2,1,0:T(8,128)(2,1)} %bitcast.19), calls=%async_computation.3 | async-start | bytes 12058624 | tf_op jit(solution)/shard_map/all_to_all | solution.py:45
  278.1 24.6 %all-to-all-start.4 = ((bf16[128,24,128]{2,1,0:T(8,128)(2,1)}), bf16[128,24,128]{2,1,0:T(8,128)(2,1)S(1)}, u32[]{:S(2)}, u32[]{:S(2)}) async-start(bf16[128,24,128]{2,1,0:T(8,128)(2,1)} %shard_map.136), calls=%async_computation.4 | async-start | bytes 1572864 | tf_op jit(solution)/shard_map/all_to_all | solution.py:45

commit v5 on v4

--- a/solution.py
+++ b/solution.py
@@ -94,10 +94,10 @@
 def front(hidden, gain, ids, experts):
     tokens, width = hidden.shape
     columns = width + width // 4
-    chunk = experts // 4
+    chunk = experts // 8
     return pl.pallas_call(
         front_kernel,
-        grid=(4,),
+        grid=(8,),
         in_specs=[whole((tokens, width)), whole((1, width)), whole(ids.shape)],
         out_specs=[
             pl.BlockSpec((chunk * HI, columns), lambda i: (i, 0)),
@@ -370,19 +370,13 @@
         table = scale_ref[...]
         s8[...] = jnp.broadcast_to(column_of(table.astype(f32)), s8.shape)
         s2[...] = jnp.broadcast_to(tail_column_of(table), s2.shape)
-        ext[...] = jnp.zeros_like(ext)
 
     @pl.when(step < 4)
     def _():
         dx = mm(dab_ref[...], both_ref[...])
         rounded = dx.astype(bf16)
         out_ref[...] = rounded[:main]
-        chunk = min(32, sources)
-        n_rows = SUB * chunk
-        pick = jnp.where(iota((n_rows, 2 * chunk), 0) == 4 * iota((n_rows, 2 * chunk), 1) + step, 1.0, 0.0).astype(bf16)
-        for j in range(sources // chunk):
-            tail = rounded[main + j * 2 * chunk : main + (j + 1) * 2 * chunk]
-            ext[j * n_rows : (j + 1) * n_rows, :] += mm(pick, tail).astype(bf16)
+        ext[jnp.minimum(step, 3)] = rounded[main:]
         part = jnp.sum(x_ref[...].astype(f32) * dx[:main] * s8[:, 0:1], axis=0, keepdims=True)
         part = part + jnp.sum(x2_ref[...].astype(f32) * dx[main:] * s2[:, 0:1], axis=0, keepdims=True)
         column = jnp.concatenate(
@@ -399,7 +393,13 @@
 
     @pl.when(step == 4)
     def _():
-        out_ref[...] = ext[...]
+        chunk = min(32, sources)
+        n_rows, tail_rows = SUB * chunk, 2 * chunk
+        row, col = iota((n_rows, 4 * tail_rows), 0), iota((n_rows, 4 * tail_rows), 1)
+        pick = jnp.where(row == 4 * (col % tail_rows) + col // tail_rows, 1.0, 0.0).astype(bf16)
+        for j in range(sources // chunk):
+            quarters = [ext[q, j * tail_rows : (j + 1) * tail_rows, :] for q in range(4)]
+            out_ref[j * n_rows : (j + 1) * n_rows, :] = mm(pick, jnp.concatenate(quarters, axis=0)).astype(bf16)
 
 
 def dx_side(dab, both, r1, x2, scale, extra):
@@ -420,7 +420,7 @@
             pl.BlockSpec((main // 4, MSG), lambda i: (jnp.minimum(i, 3), 0)),
         ],
         out_shape=[jax.ShapeDtypeStruct((main, width + extra), bf16), jax.ShapeDtypeStruct((main, MSG), bf16)],
-        scratch_shapes=[pltpu.VMEM((main, quarter), bf16), pltpu.VMEM((main, MSG), f32), pltpu.VMEM((total, MSG), f32)],
+        scratch_shapes=[pltpu.VMEM((4, total, quarter), bf16), pltpu.VMEM((main, MSG), f32), pltpu.VMEM((total, MSG), f32)],
         compiler_params=params(),
         cost_estimate=pl.CostEstimate(flops=2 * (main + total) * both.size, bytes_accessed=20_000_000, transcendentals=0),
     )(dab, both, r1, x2, scale)

time: 304 us -> 305 us (level)
  no operation moved by 1% of the time
where the time goes in v5:
time: 305 us; the launch traced here: 304 us
  waiting for transfers between devices  153 us (50%)
  Pallas kernels  103 us (34%)
  starting transfers between devices  43.5 us (14%)
    all_to_all x5, waiting for transfers between devices, exchange(): return lax.all_to_all(x, AXES, split_axis=0, concat_axis=0, tiled=True)  153 us
    all_to_all x5, starting transfers between devices, exchange(): return lax.all_to_all(x, AXES, split_axis=0, concat_axis=0, tiled=True)  43.5 us
    pallas_call x1, Pallas kernels, weight_grads(): pl.pallas_call(weights_kernel, grid=(steps,), in_specs=[columns(main), co...  19.2 us
    pallas_call x1, Pallas kernels, dx_side(): pl.pallas_call(dx_kernel, grid=(5,), in_specs=[whole(dab.shape), columns(...  15 us
    pallas_call x1, Pallas kernels, x_side(): pl.pallas_call(x_kernel, grid=(5,), in_specs=[pl.BlockSpec((block, width)...  14.7 us
    pallas_call x1, Pallas kernels, second(): pl.pallas_call(second_kernel, grid=(steps,), in_specs=[whole(normed.shape...  13.3 us
    pallas_call x1, Pallas kernels, c_side(): pl.pallas_call(functools.partial(c_kernel, float(limit)), grid=(hid // ti...  11.9 us
    pallas_call x1, Pallas kernels, turn(): pl.pallas_call(turn_kernel, grid=(hid // tile,), in_specs=[tall, tall, wi...  8.98 us
  transfers between devices with their start and end apart: 5, of which 4 were waited for; matrix products, arithmetic and copies ran while one was open for 1% of the time, Pallas kernels for 26%

profile of v5, /device:TPU:1, one launch (start us, length us, event | category | flops | bytes accessed | tf_op | source)
XLA Modules:
  0.0 304.2 jit_solution(7029360622193486687)
XLA Ops:
  0.6 6.9 %shard_map.127 = (bf16[1024,2560]{1,0:T(8,128)(2,1)}, bf16[128,2048]{1,0:T(8,128)(2,1)}, f32[128,128]{1,0:T(8,128)}, f32[128,128]{1,0:T(8,128)}) custom-call(bf16[128,2048]{1,0:T(8,128)(2,1)} %hid_ref.3, f32[1,2048]{1,0:T(1,128)} %bitcast.29, s32[8,128]{1,0:T(8,128)} %bitcast.32), custom_call_target="tpu_custom_call" | custom-call | flops 1073741824 | bytes 7000000 | tf_op jit(solution)/shard_map/pallas_call | solution.py:98
  7.6 11.9 %all-to-all-start.1 = ((bf16[128,8,2560]{2,1,0:T(8,128)(2,1)}), bf16[128,8,2560]{2,1,0:T(8,128)(2,1)}, u32[]{:S(2)}, u32[]{:S(2)}) async-start(bf16[128,8,2560]{2,1,0:T(8,128)(2,1)} %bitcast.21), calls=%async_computation.1 | async-start | bytes 10485760 | tf_op jit(solution)/shard_map/all_to_all | solution.py:45
  19.5 13.3 %shard_map.128 = (f32[128,128]{1,0:T(8,128)}, bf16[1024,2560]{1,0:T(8,128)(2,1)}) custom-call(bf16[128,2048]{1,0:T(8,128)(2,1)} %get-tuple-element.38.normed_ref, bf16[128,2048]{1,0:T(8,128)(2,1)} %cot_ref.3, f32[128,128]{1,0:T(8,128)} %get-tuple-element.39.slot_ref, f32[128,128]{1,0:T(8,128)} %get-tuple-element.40.slot_t_ref, bf16[2048,128]{1,0:T(8,128)(2,1)} %router_ref.3), custom_call_target="tpu_custom_call" | custom-call | flops 1073741824 | bytes 8000000 | tf_op jit(solution)/shard_map/pallas_call | solution.py:163
  32.8 50.6 %all-to-all-done.1 = bf16[128,8,2560]{2,1,0:T(8,128)(2,1)} async-done(((bf16[128,8,2560]{2,1,0:T(8,128)(2,1)}), bf16[128,8,2560]{2,1,0:T(8,128)(2,1)}, u32[]{:S(2)}, u32[]{:S(2)}) %all-to-all-start.1) | async-done | bytes 5242912 | tf_op jit(solution)/shard_map/all_to_all | solution.py:45
  83.4 6.8 %all-to-all-start = ((bf16[128,8,2560]{2,1,0:T(8,128)(2,1)}), bf16[128,8,2560]{2,1,0:T(8,128)(2,1)}, u32[]{:S(2)}, u32[]{:S(2)}) async-start(bf16[128,8,2560]{2,1,0:T(8,128)(2,1)} %bitcast.20), calls=%async_computation | async-start | bytes 10485760 | tf_op jit(solution)/shard_map/all_to_all | solution.py:45
  90.2 9.0 %shard_map.129 = (bf16[1536,2048]{1,0:T(8,128)(2,1)}, bf16[2048,768]{1,0:T(8,128)(2,1)}) custom-call(bf16[2048,768]{1,0:T(8,128)(2,1)} %bitcast.23, bf16[2048,768]{1,0:T(8,128)(2,1)} %bitcast.25, bf16[768,2048]{1,0:T(8,128)(2,1)} %bitcast.22), custom_call_target="tpu_custom_call" | custom-call | flops 4718592 | bytes 19000000 | tf_op jit(solution)/shard_map/pallas_call | solution.py:193
  99.2 14.7 %shard_map.130 = (bf16[1280,768]{1,0:T(8,128)(2,1)}, bf16[1280,768]{1,0:T(8,128)(2,1)}, bf16[1280,768]{1,0:T(8,128)(2,1)}, bf16[256,2048]{1,0:T(8,128)(2,1)}) custom-call(bf16[1024,2560]{1,0:T(8,128)(2,1)} %bitcast.8.x_ref.ext_ref, bf16[1024,2560]{1,0:T(8,128)(2,1)} %bitcast.8.x_ref.ext_ref, bf16[2048,768]{1,0:T(8,128)(2,1)} %bitcast.24, ...), custom_call_target="tpu_custom_call" | custom-call | flops 8053063680 | bytes 24000000 | tf_op jit(solution)/shard_map/pallas_call | solution.py:243
  113.9 40.2 %all-to-all-done = bf16[128,8,2560]{2,1,0:T(8,128)(2,1)} async-done(((bf16[128,8,2560]{2,1,0:T(8,128)(2,1)}), bf16[128,8,2560]{2,1,0:T(8,128)(2,1)}, u32[]{:S(2)}, u32[]{:S(2)}) %all-to-all-start) | async-done | bytes 5242912 | tf_op jit(solution)/shard_map/all_to_all | solution.py:45
  154.1 11.9 %shard_map.131 = (bf16[1280,1536]{1,0:T(8,128)(2,1)}, bf16[256,2048]{1,0:T(8,128)(2,1)}, f32[128,128]{1,0:T(8,128)}, bf16[128,128]{1,0:T(8,128)(2,1)}) custom-call(bf16[1024,2560]{1,0:T(8,128)(2,1)} %bitcast.3.c_ref.ext_ref, bf16[1024,2560]{1,0:T(8,128)(2,1)} %bitcast.3.c_ref.ext_ref, bf16[2048,768]{1,0:T(8,128)(2,1)} %get-tuple-element.42.wd_t_ref, ...), custom_call_target="tpu_custom_call" | custom-call | flops 4026531840 | bytes 20000000 | tf_op jit(solution)/shard_map/pallas_call | solution.py:324
  166.0 6.5 %all-to-all-start.2 = ((f32[128,1,128]{2,1,0:T(1,128)}), f32[128,1,128]{2,1,0:T(1,128)S(1)}, u32[]{:S(2)}, u32[]{:S(2)}) async-start(f32[128,1,128]{2,1,0:T(1,128)} %bitcast.28), calls=%async_computation.2 | async-start | bytes 131072 | tf_op jit(solution)/shard_map/all_to_all | solution.py:45
  172.5 15.0 %shard_map.132 = (bf16[1024,2944]{1,0:T(8,128)(2,1)}, bf16[1024,128]{1,0:T(8,128)(2,1)}) custom-call(bf16[1280,1536]{1,0:T(8,128)(2,1)} %get-tuple-element.49.dab_ref, bf16[1536,2048]{1,0:T(8,128)(2,1)} %get-tuple-element.50.both_ref, bf16[1024,2560]{1,0:T(8,128)(2,1)} %bitcast.8.x_ref.ext_ref, bf16[256,2048]{1,0:T(8,128)(2,1)} %get-tuple-element.51.x2_ref, ...), custom_call_target="tpu_custom_call" | custom-call | flops 8053063680 | bytes 20000000 | tf_op jit(solution)/shard_map/pallas_call | solution.py:414
  187.5 0.0 all-to-all-done.2
  187.5 0.0 copy-start
  187.5 0.6 copy-done
  188.2 3.2 %shard_map.133 = (bf16[1024,2944]{1,0:T(8,128)(2,1)}, bf16[128,128]{1,0:T(8,128)(2,1)}, f32[128,128]{1,0:T(8,128)}) custom-call(f32[128,128]{1,0:T(8,128)} %bitcast.27, f32[128,128]{1,0:T(8,128)} %get-tuple-element.39.slot_ref, f32[128,128]{1,0:T(8,128)} %get-tuple-element.48.gates_ref, ...), custom_call_target="tpu_custom_call", output_to_operand_aliasing={{0}: (5, {})} | custom-call | flops 67108864 | bytes 2500000 | tf_op jit(solution)/shard_map/pallas_call | solution.py:516
  191.4 10.2 %all-to-all-start.3 = ((bf16[128,8,2944]{2,1,0:T(8,128)(2,1)}), bf16[128,8,2944]{2,1,0:T(8,128)(2,1)}, u32[]{:S(2)}, u32[]{:S(2)}) async-start(bf16[128,8,2944]{2,1,0:T(8,128)(2,1)} %bitcast.19), calls=%async_computation.3 | async-start | bytes 12058624 | tf_op jit(solution)/shard_map/all_to_all | solution.py:45
  201.6 0.8 dynamic_slice.6
  202.3 1.3 dynamic-slice_convert_fusion.refs_3_
  203.6 19.2 %shard_map.135 = (bf16[2048,768]{1,0:T(8,128)(2,1)}, bf16[2048,768]{1,0:T(8,128)(2,1)}, bf16[768,2048]{1,0:T(8,128)(2,1)}) custom-call(bf16[1024,2560]{1,0:T(8,128)(2,1)} %bitcast.8.x_ref.ext_ref, bf16[1024,2560]{1,0:T(8,128)(2,1)} %bitcast.3.c_ref.ext_ref, bf16[256,2048]{1,0:T(8,128)(2,1)} %get-tuple-element.51.x2_ref, ...), custom_call_target="tpu_custom_call" | custom-call | flops 12079595520 | bytes 36000000 | tf_op jit(solution)/shard_map/pallas_call | solution.py:458
  222.8 0.6 iota.7.refs_5_
  223.4 0.7 broadcast_in_dim.15.refs_4_
  224.1 52.0 %all-to-all-done.3 = bf16[128,8,2944]{2,1,0:T(8,128)(2,1)} async-done(((bf16[128,8,2944]{2,1,0:T(8,128)(2,1)}), bf16[128,8,2944]{2,1,0:T(8,128)(2,1)}, u32[]{:S(2)}, u32[]{:S(2)}) %all-to-all-start.3) | async-done | bytes 6029344 | tf_op jit(solution)/shard_map/all_to_all | solution.py:45
  276.1 2.4 shard_map.136
  278.5 8.2 %all-to-all-start.4 = ((bf16[128,24,128]{2,1,0:T(8,128)(2,1)}), bf16[128,24,128]{2,1,0:T(8,128)(2,1)S(1)}, u32[]{:S(2)}, u32[]{:S(2)}) async-start(bf16[128,24,128]{2,1,0:T(8,128)(2,1)} %shard_map.136), calls=%async_computation.4 | async-start | bytes 1572864 | tf_op jit(solution)/shard_map/all_to_all | solution.py:45
  286.7 6.5 %shard_map.134 = bf16[128,2048]{1,0:T(8,128)(2,1)} custom-call(bf16[1024,2944]{1,0:T(8,128)(2,1)} %bitcast.13.dx_ref.ext_ref.refs_0_.refs_1_.refs_2_, bf16[1024,2944]{1,0:T(8,128)(2,1)} %bitcast.13.dx_ref.ext_ref.refs_0_.refs_1_.refs_2_, f32[128,128]{1,0:T(8,128)} %get-tuple-element.40.slot_t_ref, f32[128,128]{1,0:T(8,128)} %get-tuple-element.56.gk_t_ref, ...), custom_call_target="tpu_custom_call" | custom-call | flops 1073741824 | bytes 9000000 | tf_op jit(solution)/shard_map/pallas_call | solution.py:601
  293.1 10.0 %all-to-all-done.4.sums_ref = bf16[128,24,128]{2,1,0:T(8,128)(2,1)S(1)} async-done(((bf16[128,24,128]{2,1,0:T(8,128)(2,1)}), bf16[128,24,128]{2,1,0:T(8,128)(2,1)S(1)}, u32[]{:S(2)}, u32[]{:S(2)}) %all-to-all-start.4) | async-done | bytes 786464 | tf_op jit(solution)/shard_map/all_to_all | solution.py:45
  303.1 1.0 shard_map.137
  (1 shorter events, 0.0 us)
Async XLA Ops:
  7.6 75.8 %all-to-all-start.1 = ((bf16[128,8,2560]{2,1,0:T(8,128)(2,1)}), bf16[128,8,2560]{2,1,0:T(8,128)(2,1)}, u32[]{:S(2)}, u32[]{:S(2)}) async-start(bf16[128,8,2560]{2,1,0:T(8,128)(2,1)} %bitcast.21), calls=%async_computation.1 | async-start | bytes 10485760 | tf_op jit(solution)/shard_map/all_to_all | solution.py:45
  83.4 70.7 %all-to-all-start = ((bf16[128,8,2560]{2,1,0:T(8,128)(2,1)}), bf16[128,8,2560]{2,1,0:T(8,128)(2,1)}, u32[]{:S(2)}, u32[]{:S(2)}) async-start(bf16[128,8,2560]{2,1,0:T(8,128)(2,1)} %bitcast.20), calls=%async_computation | async-start | bytes 10485760 | tf_op jit(solution)/shard_map/all_to_all | solution.py:45
  166.0 21.5 %all-to-all-start.2 = ((f32[128,1,128]{2,1,0:T(1,128)}), f32[128,1,128]{2,1,0:T(1,128)S(1)}, u32[]{:S(2)}, u32[]{:S(2)}) async-start(f32[128,1,128]{2,1,0:T(1,128)} %bitcast.28), calls=%async_computation.2 | async-start | bytes 131072 | tf_op jit(solution)/shard_map/all_to_all | solution.py:45
  187.5 0.6 copy-start
  191.4 84.7 %all-to-all-start.3 = ((bf16[128,8,2944]{2,1,0:T(8,128)(2,1)}), bf16[128,8,2944]{2,1,0:T(8,128)(2,1)}, u32[]{:S(2)}, u32[]{:S(2)}) async-start(bf16[128,8,2944]{2,1,0:T(8,128)(2,1)} %bitcast.19), calls=%async_computation.3 | async-start | bytes 12058624 | tf_op jit(solution)/shard_map/all_to_all | solution.py:45
  278.5 24.6 %all-to-all-start.4 = ((bf16[128,24,128]{2,1,0:T(8,128)(2,1)}), bf16[128,24,128]{2,1,0:T(8,128)(2,1)S(1)}, u32[]{:S(2)}, u32[]{:S(2)}) async-start(bf16[128,24,128]{2,1,0:T(8,128)(2,1)} %shard_map.136), calls=%async_computation.4 | async-start | bytes 1572864 | tf_op jit(solution)/shard_map/all_to_all | solution.py:45
